TPU v7x, 32 devices: a whole 2x2x4 slice. The times are simulated.
32 devices in a mesh: row: 16 (over z, x, core), col: 2 (over y).
Axes of the slice: x: 2, y: 2, z: 4, core: 2. Of those that a mesh axis runs over, the one named last changes fastest.
Arguments:
- hessian: float32 [14336, 14336], P('row', 'col'), may hold values from -1 to 6, as said below
- dense_weight: float32 [14336, 1024], P('col', 'row'), may hold values from -6 to 6
- start_iterate: float32 [14336, 1024], P('col', 'row'), may hold values from -6 to 6
- start_multiplier: float32 [14336, 1024], P('col', 'row'), may hold values from -3 to 3
- keep_mask: int32 [14336, 1024], P('col', 'row'), may hold values 0 or 1
Outputs:
- iterate: float32 [14336, 1024], P('col', 'row')
- projected: float32 [14336, 1024], P('col', 'row')
- multiplier: float32 [14336, 1024], P('col', 'row')
Inputs may be any that keep to these rules, and one draw needn't show every extreme that they name: `hessian`: a calibration Hessian: symmetric up to rounding and positive definite.
All inputs are finite; a program needn't handle non-finite values. No bound on the sum of `keep_mask` on one device may be relied on, other than what follows from the above.
Results may differ from a plain program's by a relative error of at most 0.0001.
Values sent between devices are 32-bit elements; how exact they have to be, the bound alone decides.
No kernel may reach another device: no remote copies, remote signals or barrier semaphores. Data moves between devices by JAX's collectives and lax.ppermute only.
A program may use at most 128 MiB of HBM per device.

v0:
```python
import jax
import jax.numpy as jnp
from jax import lax
from jax.sharding import PartitionSpec as P

ITERS = 2


step_size = 0.25
penalty = 1.0


def per_device(hessian, dense_weight, start_iterate, start_multiplier, keep_mask):
    keeping = keep_mask.astype(jnp.float32)
    iterate = start_iterate
    multiplier = start_multiplier
    projected = keeping * (iterate + multiplier)
    for rounds in range(ITERS):
        change = iterate - dense_weight
        gathered = lax.all_gather(change, "row", axis=1, tiled=True)
        partial_value = jnp.dot(
            hessian, gathered, precision=lax.Precision.HIGHEST, preferred_element_type=jnp.float32
        )
        moved = lax.all_to_all(partial_value, "row", split_axis=1, concat_axis=0, tiled=True)
        gradient = lax.psum_scatter(moved, "col", scatter_dimension=0, tiled=True)
        iterate = iterate - step_size * (gradient + penalty * (iterate - projected + multiplier))
        projected = keeping * (iterate + multiplier)
        multiplier = multiplier + iterate - projected
    return (iterate, projected, multiplier)


def solution(mesh):
    return jax.shard_map(
        per_device,
        mesh=mesh,
        in_specs=(
            P("row", "col"),
            P("col", "row"),
            P("col", "row"),
            P("col", "row"),
            P("col", "row"),
        ),
        out_specs=(P("col", "row"), P("col", "row"), P("col", "row")),
        check_vma=False,
    )
```

profile of v0, /device:TPU:0, one launch (start us, length us, event | category | flops | bytes accessed | tf_op | source)
XLA Modules:
  0.0 811.9 jit_solution(5341137809310281413)
XLA Ops:
  7.2 0.0 all-gather.3.cloned.1.call-start
  7.2 3.5 sub.24
  10.7 0.0 all-gather.3.cloned.1.call-update
  10.7 0.0 reduce-scatter.3.cloned.1.call-start
  10.8 151.2 %all-gather.3.cloned.1.call-done = f32[7168,1024]{0,1:T(8,128)} async-done(((f32[7168,64]{0,1:T(8,128)}), f32[7168,1024]{0,1:T(8,128)}) %all-gather.3.cloned.1.call-update) | async-done | bytes 29360144 | tf_op jit(solution)/shard_map/all_gather | solution.py:20
  161.9 104.3 %fusion.4 = f32[1024,896]{1,0:T(8,128)S(1)} fusion(f32[7168,1024]{0,1:T(8,128)} %all-gather.3.cloned.1.call-done, f32[896,7168]{1,0:T(8,128)} %param.5), kind=kOutput, calls=%fused_computation.8 | convolution fusion | flops 78920024064 | bytes 58720256 | tf_op jit(solution)/shard_map/dot_general | solution.py:21
  266.2 85.5 %all_to_all.38 = f32[896,16,64]{0,2,1:T(8,128)S(1)} all-to-all(f32[896,16,64]{0,2,1:T(8,128)S(1)} %bitcast.20), channel_id=1, replica_groups=mesh['row'=16,'col'=2] {'row'}, dimensions={1} | all-to-all | bytes 7340032 | tf_op jit(solution)/shard_map/all_to_all | solution.py:24
  351.8 2.0 copy.10
  353.8 0.0 copy-start
  353.8 0.0 reduce-scatter.3.cloned.1.call-update
  353.8 0.0 all-gather.5.cloned.1.call-start
  353.9 49.7 %reduce-scatter.3.cloned.1.call-done = f32[7168,64]{0,1:T(8,128)} async-done(((f32[14336,64]{0,1:T(8,128)}), f32[7168,64]{0,1:T(8,128)}) %reduce-scatter.3.cloned.1.call-update) | async-done | bytes 1835024 | tf_op jit(solution)/shard_map/reduce_scatter | solution.py:25
  403.6 0.0 copy-done
  403.6 5.6 fusion.3
  409.2 0.0 all-gather.5.cloned.1.call-update
  409.2 0.2 reduce-scatter.5.cloned.1.call-start
  409.4 148.3 %all-gather.5.cloned.1.call-done = f32[7168,1024]{0,1:T(8,128)} async-done(((f32[7168,64]{0,1:T(8,128)}), f32[7168,1024]{0,1:T(8,128)}) %all-gather.5.cloned.1.call-update) | async-done | bytes 29360144 | tf_op jit(solution)/shard_map/all_gather | solution.py:20
  557.7 104.3 %fusion.5 = f32[1024,896]{1,0:T(8,128)S(1)} fusion(f32[7168,1024]{0,1:T(8,128)} %all-gather.5.cloned.1.call-done, f32[896,7168]{1,0:T(8,128)} %param.5), kind=kOutput, calls=%fused_computation.9 | convolution fusion | flops 78920024064 | bytes 58720256 | tf_op jit(solution)/shard_map/dot_general | solution.py:21
  662.0 85.5 %all_to_all.39 = f32[896,16,64]{0,2,1:T(8,128)S(1)} all-to-all(f32[896,16,64]{0,2,1:T(8,128)S(1)} %bitcast.21), channel_id=1, replica_groups=mesh['row'=16,'col'=2] {'row'}, dimensions={1} | all-to-all | bytes 7340032 | tf_op jit(solution)/shard_map/all_to_all | solution.py:24
  747.6 2.0 copy.11
  749.6 0.0 reduce-scatter.5.cloned.1.call-update
  749.6 49.8 %reduce-scatter.5.cloned.1.call-done = f32[7168,64]{0,1:T(8,128)} async-done(((f32[14336,64]{0,1:T(8,128)}), f32[7168,64]{0,1:T(8,128)}) %reduce-scatter.5.cloned.1.call-update) | async-done | bytes 1835024 | tf_op jit(solution)/shard_map/reduce_scatter | solution.py:25
  799.4 6.0 fusion.2
Async XLA Ops:
  7.2 154.7 %all-gather.3.cloned.1.call-start = ((), (), s32[]{:S(2)}) async-start(), calls=%async_computation.4 | async-start | bytes 31195136 | tf_op jit(solution)/shard_map/all_gather | solution.py:20
  10.7 392.9 %reduce-scatter.3.cloned.1.call-start = ((), (), s32[]{:S(2)}) async-start(), calls=%async_computation.5 | async-start | bytes 5505024 | tf_op jit(solution)/shard_map/reduce_scatter | solution.py:25
  353.8 49.8 %copy-start = (s32[7168,64]{0,1:T(8,128)S(1)}, s32[7168,64]{0,1:T(8,128)}, u32[]{:S(2)}) copy-start(s32[7168,64]{0,1:T(8,128)} %param.9) | copy-start | bytes 5505028
  353.8 203.9 %all-gather.5.cloned.1.call-start = ((), (), s32[]{:S(2)}) async-start(), calls=%async_computation.6 | async-start | bytes 31195136 | tf_op jit(solution)/shard_map/all_gather | solution.py:20
  409.2 390.2 %reduce-scatter.5.cloned.1.call-start = ((), (), s32[]{:S(2)}) async-start(), calls=%async_computation.7 | async-start | bytes 5505024 | tf_op jit(solution)/shard_map/reduce_scatter | solution.py:25
Sparse Core Ops, SparseCore 0:
  10.8 151.0 all-gather.2
  353.9 49.6 reduce-scatter.2
  409.3 148.3 all-gather.4
  749.8 49.5 reduce-scatter.4
where the time goes:
time: 812 us
  waiting for transfers between devices  399 us (49%)
  matrix products  209 us (26%)
  blocking collectives  171 us (21%)
  other arithmetic  15 us (2%)
  between operations  13.8 us (2%)
    all_gather x2, waiting for transfers between devices, per_device(): gathered = lax.all_gather(change, 'row', axis=1, tiled=True)  299 us
    dot_general x2, matrix products, per_device(): jnp.dot(hessian, gathered, precision=lax.Precision.HIGHEST, preferred_ele...  209 us
    all_to_all x2, blocking collectives, per_device(): lax.all_to_all(partial_value, 'row', split_axis=1, concat_axis=0, tiled=T...  171 us
    reduce_scatter x2, waiting for transfers between devices, per_device(): gradient = lax.psum_scatter(moved, 'col', scatter_dimension=0, tiled=True)  99.5 us
  transfers between devices with their start and end apart: 4, of which 4 were waited for; matrix products, arithmetic and copies ran while one was open for 0% of the time, Pallas kernels for 0%

commit v1 on v0

v1 whole, which is shorter than its diff:
```python
import functools

import jax
import jax.numpy as jnp
from jax import lax
from jax.experimental import pallas as pl
from jax.experimental.pallas import tpu as pltpu
from jax.sharding import PartitionSpec as P

step_size = 0.25
penalty = 1.0

CORES = 2
PAIR = 2
VMEM_BYTES = 48 * 1024 * 1024


def split(value):
    high = value.astype(jnp.bfloat16)
    low = (value - high.astype(jnp.float32)).astype(jnp.bfloat16)
    return high, low


def dot_f32(left, right, rows, dims):
    high, low = split(right)
    both = lax.dot_general(left[...], high, dims, preferred_element_type=jnp.float32)
    cross = lax.dot_general(left[:rows], low, dims, preferred_element_type=jnp.float32)
    return both[:rows] + (both[rows:] + cross)


def first_kernel(near_ref, far_ref, own_ref, sib_ref, xnear_ref, xfar_ref, out_ref, parts):
    half = near_ref.shape[0]
    rows = 2 * half

    @pl.when(pl.program_id(0) == 0)
    def _():
        parts[:half], parts[rows : rows + half] = split(near_ref[...])
        parts[half:rows], parts[rows + half :] = split(far_ref[...])

    tile = own_ref.shape[0]
    rows_of_h = jnp.concatenate([own_ref[...], sib_ref[...]], axis=0)
    product = dot_f32(parts, rows_of_h, rows, (((1,), (1,)), ((), ())))
    for which in range(2):
        part = product[:, which * tile : (which + 1) * tile]
        out_ref[which, :half] = xnear_ref[which] - step_size * part[:half]
        out_ref[which, half:] = xfar_ref[which] - step_size * part[half:]


def first(near, far, own, sib, xnear, xfar):
    half, depth = near.shape
    rows = own.shape[0]
    tile = 128 if rows % 128 == 0 else rows
    whole = pl.BlockSpec((half, depth), lambda i: (0, 0))
    band = pl.BlockSpec((tile, depth), lambda i: (i, 0))
    piece = pl.BlockSpec((2, half, tile), lambda i: (0, 0, i))
    return pl.pallas_call(
        first_kernel,
        grid=(rows // tile,),
        in_specs=[whole, whole, band, band, piece, piece],
        out_specs=pl.BlockSpec((2, 2 * half, tile), lambda i: (0, 0, i)),
        out_shape=jax.ShapeDtypeStruct((2, 2 * half, rows), jnp.float32),
        scratch_shapes=[pltpu.VMEM((4 * half, depth), jnp.bfloat16)],
        compiler_params=pltpu.CompilerParams(vmem_limit_bytes=VMEM_BYTES),
        cost_estimate=pl.CostEstimate(
            flops=3 * 2 * 4 * half * depth * rows, bytes_accessed=8 * rows * depth, transcendentals=0
        ),
        name="first_product",
    )(near, far, own, sib, xnear, xfar)


def second_kernel(mine_ref, other_ref, own_ref, sib_ref, near_ref, far_ref, cnear_ref, cfar_ref, parts):
    _, rows, depth = mine_ref.shape
    half = rows // 2

    @pl.when(pl.program_id(0) == 0)
    def _():
        for which in range(2):
            change = mine_ref[which] + other_ref[which]
            cnear_ref[which] = change[:half]
            cfar_ref[which] = change[half:]
            places = slice(which * depth, (which + 1) * depth)
            parts[:rows, places], parts[rows:, places] = split(change)

    rows_of_h = jnp.concatenate([own_ref[...], sib_ref[...]], axis=0)
    product = dot_f32(parts, rows_of_h, rows, (((1,), (0,)), ((), ())))
    near_ref[...] = product[:half]
    far_ref[...] = product[half:]


def second(mine, other, own, sib):
    _, rows, depth = mine.shape
    half = rows // 2
    columns = own.shape[1]
    tile = next((t for t in (512, 256, 128) if columns % t == 0), columns)
    whole = pl.BlockSpec((2, rows, depth), lambda i: (0, 0, 0))
    band = pl.BlockSpec((depth, tile), lambda i: (0, i))
    out = pl.BlockSpec((half, tile), lambda i: (0, i))
    kept = pl.BlockSpec((2, half, depth), lambda i: (0, 0, 0))
    f32 = jnp.float32
    return pl.pallas_call(
        second_kernel,
        grid=(columns // tile,),
        in_specs=[whole, whole, band, band],
        out_specs=[out, out, kept, kept],
        out_shape=[jax.ShapeDtypeStruct((half, columns), f32)] * 2 + [jax.ShapeDtypeStruct((2, half, depth), f32)] * 2,
        scratch_shapes=[pltpu.VMEM((2 * rows, 2 * depth), jnp.bfloat16)],
        compiler_params=pltpu.CompilerParams(vmem_limit_bytes=VMEM_BYTES),
        cost_estimate=pl.CostEstimate(
            flops=3 * 2 * 2 * rows * depth * columns, bytes_accessed=8 * depth * columns, transcendentals=0
        ),
        name="second_product",
    )(mine, other, own, sib)


def per_device(rows_of, planes, hessian, dense_weight, start_iterate, start_multiplier, keep_mask):
    ring = rows_of // (CORES * PAIR)
    chips = ring * PAIR
    per_plane = chips // planes
    depth, columns = hessian.shape
    half = dense_weight.shape[1]
    row = lax.axis_index("row")
    plane = lax.axis_index("col")
    core = row % CORES
    pair = (row // CORES) % PAIR
    place = row // (CORES * PAIR)

    def device(z, x, c):
        return ((z % ring) * PAIR + x) * CORES + c

    everyone = [(z, x, c) for z in range(ring) for x in range(PAIR) for c in range(CORES)]
    to_sibling = [(device(z, x, c), device(z, x, 1 - c)) for z, x, c in everyone]
    to_pair = [(device(z, x, c), device(z, x ^ 1, c)) for z, x, c in everyone]
    to_next = [(device(z, x, c), device(z + 1, x, c)) for z, x, c in everyone]

    def route(shift, flip):
        pairs = []
        for z, x, c in everyone:
            for y in range(planes):
                chip = ((z + shift) % ring) * PAIR + (x ^ flip)
                if chip // per_plane == y:
                    pairs.append((device(z, x, c) * planes + y, device(z + shift, x ^ flip, c) * planes + y))
        return pairs

    both = ("row", "col")
    permute = lax.ppermute

    keeping = keep_mask.astype(jnp.float32)
    projected = keeping * (start_iterate + start_multiplier)
    change = (start_iterate - dense_weight).T
    sibling = permute(hessian, "row", to_sibling)

    rest = start_iterate - step_size * (penalty * (start_iterate - projected + start_multiplier)) - dense_weight
    rest = rest.reshape(per_plane, CORES, depth, half)
    rest = jnp.where(core == 0, rest, rest[:, ::-1])
    rest = rest.transpose(0, 1, 3, 2)

    def piece(shift, flip):
        chip = ((place + shift) % ring) * PAIR + (pair ^ flip)
        part = lax.dynamic_index_in_dim(rest, jnp.clip(chip - plane * per_plane, 0, per_plane - 1), 0, keepdims=False)
        if shift == 0 and flip == 0:
            return jnp.where(chip // per_plane == plane, part, 0.0)
        return permute(part, both, route(shift, flip))

    def sum_planes(part):
        others = [permute(part, "col", [(y, (y + turn) % planes) for y in range(planes)]) for turn in range(1, planes)]
        return functools.reduce(jnp.add, others) if others else jnp.zeros_like(part)

    near, far, added = {0: change}, {}, {(0, 0): piece(0, 0)}
    mine, other, kept, sent, changed, swapped, back = {}, {}, {}, {}, {}, {}, {}
    total = None
    start = max(ring, 4)
    for window in range(start + ring):
        fresh = []

        def put(where, key, value):
            where[key] = value
            fresh.append((where, key))

        if window == 0:
            put(added, (0, 1), piece(0, 1))
            sibling = permute(hessian, "row", to_sibling)
        if window < ring - 1:
            put(near, window + 1, permute(near[window], "row", to_next))
        if window < ring:
            put(far, window, permute(near[window], "row", to_pair))
        if window < ring - 1:
            for flip in range(PAIR):
                put(added, (window + 1, flip), piece(window + 1, flip))
        group = window - start + 1
        if group >= 1:
            if total is not None:
                total = permute(total, "row", to_next)
            put(swapped, group % ring, permute(sent[group % ring], "row", to_pair))
        group = window - 3
        if 0 <= group < ring:
            for flip in range(PAIR):
                part = changed[group][flip]
                if group or flip:
                    part = permute(part, both, [(b, a) for a, b in route(group, flip)])
                put(back, (group, flip), part)
        group = window - 1
        if 0 <= group < ring:
            put(mine, group, first(near[group], far[group], hessian, sibling, added[group, 0], added[group, 1]))
            put(other, group, sum_planes(mine[group]))
        group = window - 2
        if 0 <= group < ring:
            keep, send, cnear, cfar = second(mine[group], other[group], hessian, sibling)
            put(kept, group, keep)
            put(sent, group, send)
            changed[group] = (cnear, cfar)
        group = window - start + 1
        values = [where[key] for where, key in fresh]
        values, sibling, total = lax.optimization_barrier((values, sibling, total))
        for (where, key), value in zip(fresh, values):
            where[key] = value
        if group >= 1:
            part = kept[group % ring] + swapped[group % ring]
            total = part if total is None else total + part

    back = jnp.stack([back[shift, flip] for shift in range(ring) for flip in range(PAIR)])
    blocks = []
    for block in range(per_plane):
        chip = plane * per_plane + block
        slot = ((chip // PAIR - place) % ring) * PAIR + ((chip % PAIR) ^ pair)
        blocks.append(lax.dynamic_index_in_dim(back, slot, 0, keepdims=False))
    blocks = jnp.stack(blocks)
    blocks = jnp.where(core == 0, blocks, blocks[:, ::-1])
    iterate = blocks.transpose(0, 1, 3, 2).reshape(columns, half) + dense_weight

    projected = keeping * (iterate + start_multiplier)
    multiplier = start_multiplier + iterate - projected
    iterate = iterate - step_size * (total.T + penalty * (iterate - projected + multiplier))
    projected = keeping * (iterate + multiplier)
    multiplier = multiplier + iterate - projected
    return (iterate, projected, multiplier)


def solution(mesh):
    return jax.shard_map(
        functools.partial(per_device, mesh.shape["row"], mesh.shape["col"]),
        mesh=mesh,
        in_specs=(
            P("row", "col"),
            P("col", "row"),
            P("col", "row"),
            P("col", "row"),
            P("col", "row"),
        ),
        out_specs=(P("col", "row"), P("col", "row"), P("col", "row")),
        check_vma=False,
    )
```

time: 812 us -> 530 us (0.65)
  the two profiles are of different devices: /device:TPU:0 before, /device:TPU:4 now
where the time goes in v1:
time: 530 us; the launch traced here: 529 us
  waiting for transfers between devices  191 us (36%)
  Pallas kernels  187 us (35%)
  starting transfers between devices  110 us (21%)
  other arithmetic  21.3 us (4%)
  local copies, waits for them, and re-layouts  18.2 us (3%)
    ppermute x7, waiting for transfers between devices, per_device(): part = permute(part, both, [(b, a) for a, b in route(group, flip)])  105 us
    pallas_call x4, Pallas kernels, second(): pl.pallas_call(second_kernel, grid=(columns // tile,), in_specs=[whole, w...  99.1 us
    pallas_call x4, Pallas kernels, first(): pl.pallas_call(first_kernel, grid=(rows // tile,), in_specs=[whole, whole...  88.2 us
    ppermute x7, starting transfers between devices, piece(): return permute(part, both, route(shift, flip))  51.9 us
    ppermute x3, waiting for transfers between devices, per_device(): put(near, window + 1, permute(near[window], 'row', to_next))  29.7 us
    ppermute x3, starting transfers between devices, per_device(): put(near, window + 1, permute(near[window], 'row', to_next))  26.2 us
    ppermute x3, waiting for transfers between devices, per_device(): total = permute(total, 'row', to_next)  21.5 us
    ppermute x7, waiting for transfers between devices, piece(): return permute(part, both, route(shift, flip))  21.2 us
  transfers between devices with their start and end apart: 33, of which 8 were waited for; matrix products, arithmetic and copies ran while one was open for 5% of the time, Pallas kernels for 35%

profile of v1, /device:TPU:4, one launch (start us, length us, event | category | flops | bytes accessed | tf_op | source)
XLA Modules:
  0.0 529.2 jit_solution(7014358402682425248)
XLA Ops:
  0.7 4.9 subtract_bitcast_fusion
  8.7 3.7 reshape.15
  20.3 29.7 %collective-permute-done.1.near_ref = f32[64,7168]{1,0:T(8,128)} collective-permute-done((f32[64,7168]{1,0:T(8,128)S(1)}, f32[64,7168]{1,0:T(8,128)}, u32[]{:S(2)}, u32[]{:S(2)}) %collective-permute-start.1) | collective-permute-done | bytes 1835040 | tf_op jit(solution)/shard_map/ppermute | solution.py:183
  50.0 24.5 %collective-permute-start.6 = (f32[64,7168]{1,0:T(8,128)}, f32[64,7168]{1,0:T(8,128)S(1)}, u32[]{:S(2)}, u32[]{:S(2)}) collective-permute-start(f32[64,7168]{1,0:T(8,128)} %collective-permute-done.1.near_ref), channel_id=1, source_target_pairs={{0,8},{2,10},{4,12},{6,14},{8,16},{10,18},{12,20},{14,22},{16,24},... | collective-permute-start | bytes 5505032 | tf_op jit(solution)/shard_map/ppermute | solution.py:183
  75.1 22.3 %first_product.4.mine_ref = f32[2,128,896]{2,1,0:T(8,128)S(1)} custom-call(f32[64,7168]{1,0:T(8,128)S(1)} %get-tuple-element.142.near_ref, f32[64,7168]{1,0:T(8,128)} %collective-permute-done.2.far_ref, f32[896,7168]{1,0:T(8,128)} %own_ref.15, f32[896,7168]{1,0:T(8,128)} %collective-permute-done.5.sib_ref, f32[2,64,896]{2,1,0:T(8,128)S(1)} %get-tuple-element.146.xnear_ref, ...), custom_call_target="tpu_custom_call" | custom-call | flops 9865003008 | bytes 51380224 | tf_op jit(solution)/shard_map/first_product/pallas_call | solution.py:56
  104.0 21.1 %collective-permute-done.8.xnear_ref = f32[2,64,896]{2,1,0:T(8,128)S(1)} collective-permute-done((f32[2,64,896]{2,1,0:T(8,128)S(1)}, f32[2,64,896]{2,1,0:T(8,128)S(1)}, u32[]{:S(2)}, u32[]{:S(2)}) %collective-permute-start.8) | collective-permute-done | bytes 458784 | tf_op jit(solution)/shard_map/ppermute | solution.py:162
  125.1 26.8 %collective-permute-start.13 = (f32[2,64,896]{2,1,0:T(8,128)S(1)}, f32[2,64,896]{2,1,0:T(8,128)S(1)}, u32[]{:S(2)}, u32[]{:S(2)}) collective-permute-start(f32[2,64,896]{2,1,0:T(8,128)S(1)} %get-tuple-element.145), channel_id=1, source_target_pairs={{1,25},{3,27},{5,29},{7,31},{8,0},{10,2},{12,4},{14,6},{16,8},{18,... | collective-permute-start | bytes 1376264 | tf_op jit(solution)/shard_map/ppermute | solution.py:162
  151.9 19.2 %collective-permute-start.14 = (f32[2,64,896]{2,1,0:T(8,128)S(1)}, f32[2,64,896]{2,1,0:T(8,128)S(1)}, u32[]{:S(2)}, u32[]{:S(2)}) collective-permute-start(f32[2,64,896]{2,1,0:T(8,128)S(1)} %get-tuple-element.144), channel_id=1, source_target_pairs={{1,29},{3,31},{5,25},{7,27},{8,4},{10,6},{12,0},{14,2},{16,12},{18... | collective-permute-start | bytes 1376264 | tf_op jit(solution)/shard_map/ppermute | solution.py:162
  172.8 22.3 %first_product.5.mine_ref = f32[2,128,896]{2,1,0:T(8,128)S(1)} custom-call(f32[64,7168]{1,0:T(8,128)} %collective-permute-done.1.near_ref, f32[64,7168]{1,0:T(8,128)S(1)} %collective-permute-done.7.far_ref, f32[896,7168]{1,0:T(8,128)} %own_ref.15, f32[896,7168]{1,0:T(8,128)} %collective-permute-done.5.sib_ref, ...), custom_call_target="tpu_custom_call" | custom-call | flops 9865003008 | bytes 51380224 | tf_op jit(solution)/shard_map/first_product/pallas_call | solution.py:56
  195.2 24.9 %second_product.4 = (f32[64,7168]{1,0:T(8,128)S(1)}, f32[64,7168]{1,0:T(8,128)}, f32[2,64,896]{2,1,0:T(8,128)S(1)}, f32[2,64,896]{2,1,0:T(8,128)}) custom-call(f32[2,128,896]{2,1,0:T(8,128)S(1)} %first_product.4.mine_ref, f32[2,128,896]{2,1,0:T(8,128)S(1)} %collective-permute-done.10.other_ref, f32[896,7168]{1,0:T(8,128)} %own_ref.15, ...), custom_call_target="tpu_custom_call" | custom-call | flops 9865003008 | bytes 51380224 | tf_op jit(solution)/shard_map/second_product/pallas_call | solution.py:100
  221.6 21.8 %first_product.6.mine_ref = f32[2,128,896]{2,1,0:T(8,128)S(1)} custom-call(f32[64,7168]{1,0:T(8,128)S(1)} %collective-permute-done.6.near_ref, f32[64,7168]{1,0:T(8,128)S(1)} %collective-permute-done.12.far_ref, f32[896,7168]{1,0:T(8,128)} %own_ref.15, f32[896,7168]{1,0:T(8,128)} %collective-permute-done.5.sib_ref, ...), custom_call_target="tpu_custom_call" | custom-call | flops 9865003008 | bytes 51380224 | tf_op jit(solution)/shard_map/first_product/pallas_call | solution.py:56
  243.5 4.8 collective-permute-start.18
  248.2 24.8 %second_product.5 = (f32[64,7168]{1,0:T(8,128)S(1)}, f32[64,7168]{1,0:T(8,128)}, f32[2,64,896]{2,1,0:T(8,128)S(1)}, f32[2,64,896]{2,1,0:T(8,128)S(1)}) custom-call(f32[2,128,896]{2,1,0:T(8,128)S(1)} %first_product.5.mine_ref, f32[2,128,896]{2,1,0:T(8,128)S(1)} %collective-permute-done.15.other_ref, f32[896,7168]{1,0:T(8,128)} %own_ref.15, ...), custom_call_target="tpu_custom_call" | custom-call | flops 9865003008 | bytes 51380224 | tf_op jit(solution)/shard_map/second_product/pallas_call | solution.py:100
  275.8 21.8 %first_product.7.mine_ref = f32[2,128,896]{2,1,0:T(8,128)S(1)} custom-call(f32[64,7168]{1,0:T(8,128)S(1)} %collective-permute-done.11.near_ref, f32[64,7168]{1,0:T(8,128)S(1)} %collective-permute-done.16.far_ref, f32[896,7168]{1,0:T(8,128)} %own_ref.15, f32[896,7168]{1,0:T(8,128)} %collective-permute-done.5.sib_ref, f32[2,64,896]{2,1,0:T(8,128)S(1)} %copy-done.3, ...), custom_call_target="tpu_custom_call" | custom-call | flops 9865003008 | bytes 51380224 | tf_op jit(solution)/shard_map/first_product/pallas_call | solution.py:56
  297.6 6.6 %collective-permute-start.22 = (f32[2,128,896]{2,1,0:T(8,128)S(1)}, f32[2,128,896]{2,1,0:T(8,128)S(1)}, u32[]{:S(2)}, u32[]{:S(2)}) collective-permute-start(f32[2,128,896]{2,1,0:T(8,128)S(1)} %first_product.7.mine_ref), channel_id=1, source_target_pairs={{0,1},{1,0},{2,3},{3,2},{4,5},{5,4},{6,7},{7,6},{8,9},{9,8},{10,11... | collective-permute-start | bytes 2752520 | tf_op jit(solution)/shard_map/ppermute | solution.py:165
  304.2 24.7 %second_product.6 = (f32[64,7168]{1,0:T(8,128)S(1)}, f32[64,7168]{1,0:T(8,128)}, f32[2,64,896]{2,1,0:T(8,128)S(1)}, f32[2,64,896]{2,1,0:T(8,128)S(1)}) custom-call(f32[2,128,896]{2,1,0:T(8,128)S(1)} %first_product.6.mine_ref, f32[2,128,896]{2,1,0:T(8,128)S(1)} %collective-permute-done.18.other_ref, f32[896,7168]{1,0:T(8,128)} %own_ref.15, ...), custom_call_target="tpu_custom_call" | custom-call | flops 9865003008 | bytes 51380224 | tf_op jit(solution)/shard_map/second_product/pallas_call | solution.py:100
  335.9 24.7 %second_product.7 = (f32[64,7168]{1,0:T(8,128)S(1)}, f32[64,7168]{1,0:T(8,128)}, f32[2,64,896]{2,1,0:T(8,128)S(1)}, f32[2,64,896]{2,1,0:T(8,128)S(1)}) custom-call(f32[2,128,896]{2,1,0:T(8,128)S(1)} %first_product.7.mine_ref, f32[2,128,896]{2,1,0:T(8,128)S(1)} %collective-permute-done.22.other_ref, f32[896,7168]{1,0:T(8,128)} %own_ref.15, ...), custom_call_target="tpu_custom_call" | custom-call | flops 9865003008 | bytes 51380224 | tf_op jit(solution)/shard_map/second_product/pallas_call | solution.py:100
  360.6 37.5 %collective-permute-done.24 = f32[2,64,896]{2,1,0:T(8,128)S(1)} collective-permute-done((f32[2,64,896]{2,1,0:T(8,128)S(1)}, f32[2,64,896]{2,1,0:T(8,128)S(1)}, u32[]{:S(2)}, u32[]{:S(2)}) %collective-permute-start.24) | collective-permute-done | bytes 458784 | tf_op jit(solution)/shard_map/ppermute | solution.py:199
  398.1 10.0 %collective-permute-done.25 = f32[2,64,896]{2,1,0:T(8,128)S(1)} collective-permute-done((f32[2,64,896]{2,1,0:T(8,128)S(1)}, f32[2,64,896]{2,1,0:T(8,128)S(1)}, u32[]{:S(2)}, u32[]{:S(2)}) %collective-permute-start.25) | collective-permute-done | bytes 458784 | tf_op jit(solution)/shard_map/ppermute | solution.py:199
  416.8 48.9 %collective-permute-done.28 = f32[2,64,896]{2,1,0:T(8,128)S(1)} collective-permute-done((f32[2,64,896]{2,1,0:T(8,128)S(1)}, f32[2,64,896]{2,1,0:T(8,128)S(1)}, u32[]{:S(2)}, u32[]{:S(2)}) %collective-permute-start.28) | collective-permute-done | bytes 458784 | tf_op jit(solution)/shard_map/ppermute | solution.py:199
  465.7 8.9 %collective-permute-done.29 = f32[2,64,896]{2,1,0:T(8,128)S(1)} collective-permute-done((f32[2,64,896]{2,1,0:T(8,128)S(1)}, f32[2,64,896]{2,1,0:T(8,128)S(1)}, u32[]{:S(2)}, u32[]{:S(2)}) %collective-permute-start.29) | collective-permute-done | bytes 458784 | tf_op jit(solution)/shard_map/ppermute | solution.py:199
  486.2 13.5 %collective-permute-done.31 = f32[64,7168]{1,0:T(8,128)} collective-permute-done((f32[64,7168]{1,0:T(8,128)}, f32[64,7168]{1,0:T(8,128)}, u32[]{:S(2)}, u32[]{:S(2)}) %collective-permute-start.31) | collective-permute-done | bytes 1835040 | tf_op jit(solution)/shard_map/ppermute | solution.py:193
  499.6 21.5 %collective-permute-done.32 = f32[64,7168]{1,0:T(8,128)} collective-permute-done((f32[64,7168]{1,0:T(8,128)}, f32[64,7168]{1,0:T(8,128)}, u32[]{:S(2)}, u32[]{:S(2)}) %collective-permute-start.32) | collective-permute-done | bytes 1835040 | tf_op jit(solution)/shard_map/ppermute | solution.py:192
  521.1 8.1 %fusion.5 = (f32[7168,64]{0,1:T(8,128)}, f32[7168,64]{0,1:T(8,128)}, f32[7168,64]{0,1:T(8,128)}) fusion(s32[7168,64]{0,1:T(8,128)} %param.9, f32[7168,64]{0,1:T(8,128)} %param.8, f32[64,7168]{1,0:T(8,128)} %collective-permute-done.32, f32[64,7168]{1,0:T(8,128)S(1)} %get-tuple-element.133, f32[64,7168]{1,0:T(8,128)} %collective-permute-done.31, ...), kind=kLoop, calls=%fused_computation.35 | loop fusion | flops 6881280 | bytes 18350080 | tf_op jit(solution)/shard_map/sub | solution.py:234
  (104 shorter events, 50.8 us)
Async XLA Ops:
  0.6 49.4 %collective-permute-start.5 = (f32[896,7168]{1,0:T(8,128)}, f32[896,7168]{1,0:T(8,128)}, u32[]{:S(2)}, u32[]{:S(2)}) collective-permute-start(f32[896,7168]{1,0:T(8,128)} %own_ref.15), channel_id=1, source_target_pairs={{0,2},{2,0},{4,6},{6,4},{8,10},{10,8},{12,14},{14,12},{16,18},{18,... | collective-permute-start | bytes 77070344 | tf_op jit(solution)/shard_map/ppermute | solution.py:181
  5.6 44.4 %collective-permute-start.1 = (f32[64,7168]{1,0:T(8,128)S(1)}, f32[64,7168]{1,0:T(8,128)}, u32[]{:S(2)}, u32[]{:S(2)}) collective-permute-start(f32[64,7168]{1,0:T(8,128)S(1)} %get-tuple-element.142.near_ref), channel_id=1, source_target_pairs={{0,8},{2,10},{4,12},{6,14},{8,16},{10,18},{12,20},{14,22},{16,24},... | collective-permute-start | bytes 5505032 | tf_op jit(solution)/shard_map/ppermute | solution.py:183
  50.0 121.1 %collective-permute-start.6 = (f32[64,7168]{1,0:T(8,128)}, f32[64,7168]{1,0:T(8,128)S(1)}, u32[]{:S(2)}, u32[]{:S(2)}) collective-permute-start(f32[64,7168]{1,0:T(8,128)} %collective-permute-done.1.near_ref), channel_id=1, source_target_pairs={{0,8},{2,10},{4,12},{6,14},{8,16},{10,18},{12,20},{14,22},{16,24},... | collective-permute-start | bytes 5505032 | tf_op jit(solution)/shard_map/ppermute | solution.py:183
  74.5 96.6 %collective-permute-start.7 = (f32[64,7168]{1,0:T(8,128)}, f32[64,7168]{1,0:T(8,128)S(1)}, u32[]{:S(2)}, u32[]{:S(2)}) collective-permute-start(f32[64,7168]{1,0:T(8,128)} %collective-permute-done.1.near_ref), channel_id=1, source_target_pairs={{0,4},{2,6},{4,0},{6,2},{8,12},{10,14},{12,8},{14,10},{16,20},{18,... | collective-permute-start | bytes 5505032 | tf_op jit(solution)/shard_map/ppermute | solution.py:185
  97.4 73.7 %collective-permute-start.10 = (f32[2,128,896]{2,1,0:T(8,128)S(1)}, f32[2,128,896]{2,1,0:T(8,128)S(1)}, u32[]{:S(2)}, u32[]{:S(2)}) collective-permute-start(f32[2,128,896]{2,1,0:T(8,128)S(1)} %first_product.4.mine_ref), channel_id=1, source_target_pairs={{0,1},{1,0},{2,3},{3,2},{4,5},{5,4},{6,7},{7,6},{8,9},{9,8},{10,11... | collective-permute-start | bytes 2752520 | tf_op jit(solution)/shard_map/ppermute | solution.py:165
  102.6 49.3 %collective-permute-start.9 = (f32[2,64,896]{2,1,0:T(8,128)S(1)}, f32[2,64,896]{2,1,0:T(8,128)S(1)}, u32[]{:S(2)}, u32[]{:S(2)}) collective-permute-start(f32[2,64,896]{2,1,0:T(8,128)S(1)} %get-tuple-element.147), channel_id=1, source_target_pairs={{1,21},{3,23},{5,17},{7,19},{9,29},{11,31},{13,25},{15,27},{16,4},... | collective-permute-start | bytes 1376264 | tf_op jit(solution)/shard_map/ppermute | solution.py:162
  125.1 95.0 %collective-permute-start.13 = (f32[2,64,896]{2,1,0:T(8,128)S(1)}, f32[2,64,896]{2,1,0:T(8,128)S(1)}, u32[]{:S(2)}, u32[]{:S(2)}) collective-permute-start(f32[2,64,896]{2,1,0:T(8,128)S(1)} %get-tuple-element.145), channel_id=1, source_target_pairs={{1,25},{3,27},{5,29},{7,31},{8,0},{10,2},{12,4},{14,6},{16,8},{18,... | collective-permute-start | bytes 1376264 | tf_op jit(solution)/shard_map/ppermute | solution.py:162
  151.9 69.1 %collective-permute-start.14 = (f32[2,64,896]{2,1,0:T(8,128)S(1)}, f32[2,64,896]{2,1,0:T(8,128)S(1)}, u32[]{:S(2)}, u32[]{:S(2)}) collective-permute-start(f32[2,64,896]{2,1,0:T(8,128)S(1)} %get-tuple-element.144), channel_id=1, source_target_pairs={{1,29},{3,31},{5,25},{7,27},{8,4},{10,6},{12,0},{14,2},{16,12},{18... | collective-permute-start | bytes 1376264 | tf_op jit(solution)/shard_map/ppermute | solution.py:162
  171.2 49.9 %collective-permute-start.11 = (f32[64,7168]{1,0:T(8,128)S(1)}, f32[64,7168]{1,0:T(8,128)S(1)}, u32[]{:S(2)}, u32[]{:S(2)}) collective-permute-start(f32[64,7168]{1,0:T(8,128)S(1)} %collective-permute-done.6.near_ref), channel_id=1, source_target_pairs={{0,8},{2,10},{4,12},{6,14},{8,16},{10,18},{12,20},{14,22},{16,24},... | collective-permute-start | bytes 5505032 | tf_op jit(solution)/shard_map/ppermute | solution.py:183
  171.2 49.8 %collective-permute-start.12 = (f32[64,7168]{1,0:T(8,128)S(1)}, f32[64,7168]{1,0:T(8,128)S(1)}, u32[]{:S(2)}, u32[]{:S(2)}) collective-permute-start(f32[64,7168]{1,0:T(8,128)S(1)} %collective-permute-done.6.near_ref), channel_id=1, source_target_pairs={{0,4},{2,6},{4,0},{6,2},{8,12},{10,14},{12,8},{14,10},{16,20},{18,... | collective-permute-start | bytes 5505032 | tf_op jit(solution)/shard_map/ppermute | solution.py:185
  220.1 54.3 %collective-permute-start.17 = (f32[2,64,896]{2,1,0:T(8,128)}, f32[2,64,896]{2,1,0:T(8,128)S(1)}, u32[]{:S(2)}, u32[]{:S(2)}) collective-permute-start(f32[2,64,896]{2,1,0:T(8,128)} %get-tuple-element.84), channel_id=1, source_target_pairs={{4,0},{6,2},{0,4},{2,6},{12,8},{14,10},{8,12},{10,14},{21,17},{23,... | collective-permute-start | bytes 1376264 | tf_op jit(solution)/shard_map/ppermute | solution.py:199
  221.0 53.4 %collective-permute-start.16 = (f32[64,7168]{1,0:T(8,128)S(1)}, f32[64,7168]{1,0:T(8,128)S(1)}, u32[]{:S(2)}, u32[]{:S(2)}) collective-permute-start(f32[64,7168]{1,0:T(8,128)S(1)} %collective-permute-done.11.near_ref), channel_id=1, source_target_pairs={{0,4},{2,6},{4,0},{6,2},{8,12},{10,14},{12,8},{14,10},{16,20},{18,... | collective-permute-start | bytes 5505032 | tf_op jit(solution)/shard_map/ppermute | solution.py:185
  273.0 55.9 %collective-permute-start.20 = (f32[2,64,896]{2,1,0:T(8,128)S(1)}, f32[2,64,896]{2,1,0:T(8,128)S(1)}, u32[]{:S(2)}, u32[]{:S(2)}) collective-permute-start(f32[2,64,896]{2,1,0:T(8,128)S(1)} %get-tuple-element.96), channel_id=1, source_target_pairs={{8,0},{10,2},{12,4},{14,6},{17,9},{19,11},{21,13},{23,15},{25,17},... | collective-permute-start | bytes 1376264 | tf_op jit(solution)/shard_map/ppermute | solution.py:199
  273.7 55.2 %collective-permute-start.21 = (f32[2,64,896]{2,1,0:T(8,128)S(1)}, f32[2,64,896]{2,1,0:T(8,128)S(1)}, u32[]{:S(2)}, u32[]{:S(2)}) collective-permute-start(f32[2,64,896]{2,1,0:T(8,128)S(1)} %get-tuple-element.97), channel_id=1, source_target_pairs={{12,0},{14,2},{8,4},{10,6},{21,9},{23,11},{17,13},{19,15},{29,17},... | collective-permute-start | bytes 1376264 | tf_op jit(solution)/shard_map/ppermute | solution.py:199
  275.2 53.7 %collective-permute-start.19 = (f32[64,7168]{1,0:T(8,128)}, f32[64,7168]{1,0:T(8,128)S(1)}, u32[]{:S(2)}, u32[]{:S(2)}) collective-permute-start(f32[64,7168]{1,0:T(8,128)} %get-tuple-element.95), channel_id=1, source_target_pairs={{0,4},{2,6},{4,0},{6,2},{8,12},{10,14},{12,8},{14,10},{16,20},{18,... | collective-permute-start | bytes 5505032 | tf_op jit(solution)/shard_map/ppermute | solution.py:193
  329.8 78.3 %collective-permute-start.23 = (f32[64,7168]{1,0:T(8,128)}, f32[64,7168]{1,0:T(8,128)S(1)}, u32[]{:S(2)}, u32[]{:S(2)}) collective-permute-start(f32[64,7168]{1,0:T(8,128)} %get-tuple-element.108), channel_id=1, source_target_pairs={{0,4},{2,6},{4,0},{6,2},{8,12},{10,14},{12,8},{14,10},{16,20},{18,... | collective-permute-start | bytes 5505032 | tf_op jit(solution)/shard_map/ppermute | solution.py:193
  331.2 76.9 %collective-permute-start.26 = (f32[64,7168]{1,0:T(8,128)S(1)}, f32[64,7168]{1,0:T(8,128)S(1)}, u32[]{:S(2)}, u32[]{:S(2)}) collective-permute-start(f32[64,7168]{1,0:T(8,128)S(1)} %add.196), channel_id=1, source_target_pairs={{0,8},{2,10},{4,12},{6,14},{8,16},{10,18},{12,20},{14,22},{16,24},... | collective-permute-start | bytes 5505032 | tf_op jit(solution)/shard_map/ppermute | solution.py:192
  333.3 64.8 %collective-permute-start.24 = (f32[2,64,896]{2,1,0:T(8,128)S(1)}, f32[2,64,896]{2,1,0:T(8,128)S(1)}, u32[]{:S(2)}, u32[]{:S(2)}) collective-permute-start(f32[2,64,896]{2,1,0:T(8,128)S(1)} %get-tuple-element.109), channel_id=1, source_target_pairs={{17,1},{19,3},{21,5},{23,7},{25,9},{27,11},{29,13},{31,15},{0,16},... | collective-permute-start | bytes 1376264 | tf_op jit(solution)/shard_map/ppermute | solution.py:199
  334.6 73.5 %collective-permute-start.25 = (f32[2,64,896]{2,1,0:T(8,128)S(1)}, f32[2,64,896]{2,1,0:T(8,128)S(1)}, u32[]{:S(2)}, u32[]{:S(2)}) collective-permute-start(f32[2,64,896]{2,1,0:T(8,128)S(1)} %get-tuple-element.110), channel_id=1, source_target_pairs={{21,1},{23,3},{17,5},{19,7},{29,9},{31,11},{25,13},{27,15},{4,16},... | collective-permute-start | bytes 1376264 | tf_op jit(solution)/shard_map/ppermute | solution.py:199
  408.1 66.5 %collective-permute-start.27 = (f32[64,7168]{1,0:T(8,128)}, f32[64,7168]{1,0:T(8,128)}, u32[]{:S(2)}, u32[]{:S(2)}) collective-permute-start(f32[64,7168]{1,0:T(8,128)} %get-tuple-element.120), channel_id=1, source_target_pairs={{0,4},{2,6},{4,0},{6,2},{8,12},{10,14},{12,8},{14,10},{16,20},{18,... | collective-permute-start | bytes 5505032 | tf_op jit(solution)/shard_map/ppermute | solution.py:193
  410.9 63.8 %collective-permute-start.30 = (f32[64,7168]{1,0:T(8,128)}, f32[64,7168]{1,0:T(8,128)}, u32[]{:S(2)}, u32[]{:S(2)}) collective-permute-start(f32[64,7168]{1,0:T(8,128)} %add_add_fusion.1), channel_id=1, source_target_pairs={{0,8},{2,10},{4,12},{6,14},{8,16},{10,18},{12,20},{14,22},{16,24},... | collective-permute-start | bytes 5505032 | tf_op jit(solution)/shard_map/ppermute | solution.py:192
  411.1 88.5 %collective-permute-start.31 = (f32[64,7168]{1,0:T(8,128)}, f32[64,7168]{1,0:T(8,128)}, u32[]{:S(2)}, u32[]{:S(2)}) collective-permute-start(f32[64,7168]{1,0:T(8,128)} %get-tuple-element.128), channel_id=1, source_target_pairs={{0,4},{2,6},{4,0},{6,2},{8,12},{10,14},{12,8},{14,10},{16,20},{18,... | collective-permute-start | bytes 5505032 | tf_op jit(solution)/shard_map/ppermute | solution.py:193
  412.0 53.7 %collective-permute-start.28 = (f32[2,64,896]{2,1,0:T(8,128)S(1)}, f32[2,64,896]{2,1,0:T(8,128)S(1)}, u32[]{:S(2)}, u32[]{:S(2)}) collective-permute-start(f32[2,64,896]{2,1,0:T(8,128)S(1)} %get-tuple-element.121), channel_id=1, source_target_pairs={{25,1},{27,3},{29,5},{31,7},{0,8},{2,10},{4,12},{6,14},{8,16},{10,... | collective-permute-start | bytes 1376264 | tf_op jit(solution)/shard_map/ppermute | solution.py:199
  413.3 61.3 %collective-permute-start.29 = (f32[2,64,896]{2,1,0:T(8,128)S(1)}, f32[2,64,896]{2,1,0:T(8,128)S(1)}, u32[]{:S(2)}, u32[]{:S(2)}) collective-permute-start(f32[2,64,896]{2,1,0:T(8,128)S(1)} %get-tuple-element.122), channel_id=1, source_target_pairs={{29,1},{31,3},{25,5},{27,7},{4,8},{6,10},{0,12},{2,14},{12,16},{14... | collective-permute-start | bytes 1376264 | tf_op jit(solution)/shard_map/ppermute | solution.py:199
  (25 other events, 586.6 us)

commit v2 on v1

--- a/solution.py
+++ b/solution.py
@@ -68,18 +68,15 @@
     )(near, far, own, sib, xnear, xfar)
 
 
-def second_kernel(mine_ref, other_ref, own_ref, sib_ref, near_ref, far_ref, cnear_ref, cfar_ref, parts):
-    _, rows, depth = mine_ref.shape
+def second_kernel(change_ref, own_ref, sib_ref, near_ref, far_ref, parts):
+    _, rows, depth = change_ref.shape
     half = rows // 2
 
     @pl.when(pl.program_id(0) == 0)
     def _():
         for which in range(2):
-            change = mine_ref[which] + other_ref[which]
-            cnear_ref[which] = change[:half]
-            cfar_ref[which] = change[half:]
             places = slice(which * depth, (which + 1) * depth)
-            parts[:rows, places], parts[rows:, places] = split(change)
+            parts[:rows, places], parts[rows:, places] = split(change_ref[which])
 
     rows_of_h = jnp.concatenate([own_ref[...], sib_ref[...]], axis=0)
     product = dot_f32(parts, rows_of_h, rows, (((1,), (0,)), ((), ())))
@@ -87,29 +84,26 @@
     far_ref[...] = product[half:]
 
 
-def second(mine, other, own, sib):
-    _, rows, depth = mine.shape
+def second(change, own, sib):
+    _, rows, depth = change.shape
     half = rows // 2
     columns = own.shape[1]
     tile = next((t for t in (512, 256, 128) if columns % t == 0), columns)
-    whole = pl.BlockSpec((2, rows, depth), lambda i: (0, 0, 0))
     band = pl.BlockSpec((depth, tile), lambda i: (0, i))
     out = pl.BlockSpec((half, tile), lambda i: (0, i))
-    kept = pl.BlockSpec((2, half, depth), lambda i: (0, 0, 0))
-    f32 = jnp.float32
     return pl.pallas_call(
         second_kernel,
         grid=(columns // tile,),
-        in_specs=[whole, whole, band, band],
-        out_specs=[out, out, kept, kept],
-        out_shape=[jax.ShapeDtypeStruct((half, columns), f32)] * 2 + [jax.ShapeDtypeStruct((2, half, depth), f32)] * 2,
+        in_specs=[pl.BlockSpec((2, rows, depth), lambda i: (0, 0, 0)), band, band],
+        out_specs=[out, out],
+        out_shape=[jax.ShapeDtypeStruct((half, columns), jnp.float32)] * 2,
         scratch_shapes=[pltpu.VMEM((2 * rows, 2 * depth), jnp.bfloat16)],
         compiler_params=pltpu.CompilerParams(vmem_limit_bytes=VMEM_BYTES),
         cost_estimate=pl.CostEstimate(
             flops=3 * 2 * 2 * rows * depth * columns, bytes_accessed=8 * depth * columns, transcendentals=0
         ),
         name="second_product",
-    )(mine, other, own, sib)
+    )(change, own, sib)
 
 
 def per_device(rows_of, planes, hessian, dense_weight, start_iterate, start_multiplier, keep_mask):
@@ -133,13 +127,21 @@
     to_next = [(device(z, x, c), device(z + 1, x, c)) for z, x, c in everyone]
 
     def route(shift, flip):
+        turn = cross(shift, flip)
         pairs = []
         for z, x, c in everyone:
             for y in range(planes):
                 chip = ((z + shift) % ring) * PAIR + (x ^ flip)
-                if chip // per_plane == y:
+                if chip // per_plane == (y - turn) % planes:
                     pairs.append((device(z, x, c) * planes + y, device(z + shift, x ^ flip, c) * planes + y))
         return pairs
+
+    def route_back(shift, flip):
+        turn = cross(shift, flip)
+        return [(b, a - a % planes + (a - turn) % planes) for a, b in route(shift, flip)]
+
+    def cross(shift, flip):
+        return 1 if shift and flip else 0
 
     both = ("row", "col")
     permute = lax.ppermute
@@ -155,8 +157,11 @@
     rest = rest.transpose(0, 1, 3, 2)
 
     def piece(shift, flip):
+        turn = cross(shift, flip)
         chip = ((place + shift) % ring) * PAIR + (pair ^ flip)
-        part = lax.dynamic_index_in_dim(rest, jnp.clip(chip - plane * per_plane, 0, per_plane - 1), 0, keepdims=False)
+        first_chip = ((plane - turn) % planes) * per_plane
+        source = rest_by[turn]
+        part = lax.dynamic_index_in_dim(source, jnp.clip(chip - first_chip, 0, per_plane - 1), 0, keepdims=False)
         if shift == 0 and flip == 0:
             return jnp.where(chip // per_plane == plane, part, 0.0)
         return permute(part, both, route(shift, flip))
@@ -165,10 +170,12 @@
         others = [permute(part, "col", [(y, (y + turn) % planes) for y in range(planes)]) for turn in range(1, planes)]
         return functools.reduce(jnp.add, others) if others else jnp.zeros_like(part)
 
+    rest_by = {0: rest}
     near, far, added = {0: change}, {}, {(0, 0): piece(0, 0)}
-    mine, other, kept, sent, changed, swapped, back = {}, {}, {}, {}, {}, {}, {}
+    mine, other, changed, kept, sent, swapped, back = {}, {}, {}, {}, {}, {}, {}
     total = None
     start = max(ring, 4)
+    returns = [(0, 0, 5), (0, 1, 5)] + [(group, flip, group + 2 + (group == 1 and flip)) for group in range(1, ring) for flip in range(PAIR)]
     for window in range(start + ring):
         fresh = []
 
@@ -176,45 +183,48 @@
             where[key] = value
             fresh.append((where, key))
 
-        if window == 0:
-            put(added, (0, 1), piece(0, 1))
-            sibling = permute(hessian, "row", to_sibling)
         if window < ring - 1:
             put(near, window + 1, permute(near[window], "row", to_next))
         if window < ring:
             put(far, window, permute(near[window], "row", to_pair))
-        if window < ring - 1:
+        if window == 0:
+            sibling = permute(hessian, "row", to_sibling)
+            put(rest_by, 1, permute(rest, "col", [(y, (y + 1) % planes) for y in range(planes)]))
+            put(added, (0, 1), piece(0, 1))
+        elif window < ring:
             for flip in range(PAIR):
-                put(added, (window + 1, flip), piece(window + 1, flip))
-        group = window - start + 1
-        if group >= 1:
+                put(added, (window, flip), piece(window, flip))
+        closing = window - start + 1
+        if closing >= 1:
             if total is not None:
                 total = permute(total, "row", to_next)
-            put(swapped, group % ring, permute(sent[group % ring], "row", to_pair))
-        group = window - 3
+            put(swapped, closing % ring, permute(sent[closing % ring], "row", to_pair))
+        group = window - 2
         if 0 <= group < ring:
-            for flip in range(PAIR):
-                part = changed[group][flip]
-                if group or flip:
-                    part = permute(part, both, [(b, a) for a, b in route(group, flip)])
-                put(back, (group, flip), part)
+            put(changed, group, mine[group] + other[group])
         group = window - 1
         if 0 <= group < ring:
             put(mine, group, first(near[group], far[group], hessian, sibling, added[group, 0], added[group, 1]))
             put(other, group, sum_planes(mine[group]))
         group = window - 2
-        if 0 <= group < ring:
-            keep, send, cnear, cfar = second(mine[group], other[group], hessian, sibling)
+        if window == start + ring - 2:
+            group = 0
+        if (1 <= group < ring) or window == start + ring - 2:
+            keep, send = second(changed[group], hessian, sibling)
             put(kept, group, keep)
             put(sent, group, send)
-            changed[group] = (cnear, cfar)
-        group = window - start + 1
+        for group, flip, when in returns:
+            if when == window:
+                part = changed[group][:, flip * half : (flip + 1) * half]
+                if group or flip:
+                    part = permute(part, both, route_back(group, flip))
+                put(back, (group, flip), part)
         values = [where[key] for where, key in fresh]
-        values, sibling, total = lax.optimization_barrier((values, sibling, total))
+        values, sibling, total, rest_by[0] = lax.optimization_barrier((values, sibling, total, rest_by[0]))
         for (where, key), value in zip(fresh, values):
             where[key] = value
-        if group >= 1:
-            part = kept[group % ring] + swapped[group % ring]
+        if closing >= 1:
+            part = kept[closing % ring] + swapped[closing % ring]
             total = part if total is None else total + part
 
     back = jnp.stack([back[shift, flip] for shift in range(ring) for flip in range(PAIR)])

time: 530 us -> 464 us (0.88)
  the two profiles are of different devices: /device:TPU:4 before, /device:TPU:0 now
where the time goes in v2:
time: 464 us
  Pallas kernels  187 us (40%)
  waiting for transfers between devices  149 us (32%)
  starting transfers between devices  74.7 us (16%)
  local copies, waits for them, and re-layouts  26.3 us (6%)
  other arithmetic  25 us (5%)
    pallas_call x4, Pallas kernels, second(): pl.pallas_call(second_kernel, grid=(columns // tile,), in_specs=[pl.Block...  96.7 us
    pallas_call x4, Pallas kernels, first(): pl.pallas_call(first_kernel, grid=(rows // tile,), in_specs=[whole, whole...  90.4 us
    ppermute x7, waiting for transfers between devices, piece(): return permute(part, both, route(shift, flip))  79.6 us
    ppermute x3, waiting for transfers between devices, per_device(): total = permute(total, 'row', to_next)  32.6 us
    ppermute x7, starting transfers between devices, piece(): return permute(part, both, route(shift, flip))  30.3 us
    ppermute x7, waiting for transfers between devices, per_device(): part = permute(part, both, route_back(group, flip))  25.6 us
    ppermute x7, starting transfers between devices, per_device(): part = permute(part, both, route_back(group, flip))  25.5 us
    ppermute x4, waiting for transfers between devices, per_device(): put(swapped, closing % ring, permute(sent[closing % ring], 'row', to_pair))  11.3 us
  transfers between devices with their start and end apart: 34, of which 8 were waited for; matrix products, arithmetic and copies ran while one was open for 8% of the time, Pallas kernels for 40%

profile of v2, /device:TPU:0, one launch (start us, length us, event | category | flops | bytes accessed | tf_op | source)
XLA Modules:
  0.0 463.6 jit_solution(7425082247160313633)
XLA Ops:
  1.1 4.9 %subtract_subtract_fusion = (f32[7168,64]{0,1:T(8,128)}, f32[64,7168]{1,0:T(8,128)S(1)}) fusion(f32[7168,64]{0,1:T(8,128)} %param.6, f32[7168,64]{0,1:T(8,128)} %param.7, f32[7168,64]{0,1:T(8,128)} %param.8, s32[7168,64]{0,1:T(8,128)} %param.9), kind=kLoop, calls=%fused_computation.9 | loop fusion | flops 4128768 | bytes 11010048 | tf_op jit(solution)/shard_map/sub | solution.py:154
  6.1 3.7 reshape.15
  23.9 44.1 %collective-permute-done.3.xfar_ref = f32[2,64,896]{2,1,0:T(8,128)S(1)} collective-permute-done((f32[2,64,896]{2,1,0:T(8,128)S(1)}, f32[2,64,896]{2,1,0:T(8,128)S(1)}, u32[]{:S(2)}, u32[]{:S(2)}) %collective-permute-start.3) | collective-permute-done | bytes 458784 | tf_op jit(solution)/shard_map/ppermute | solution.py:167
  71.1 22.3 %first_product.4 = f32[2,128,896]{2,1,0:T(8,128)S(1)} custom-call(f32[64,7168]{1,0:T(8,128)S(1)} %get-tuple-element.141.near_ref, f32[64,7168]{1,0:T(8,128)} %collective-permute-done.1.far_ref, f32[896,7168]{1,0:T(8,128)} %own_ref.15, f32[896,7168]{1,0:T(8,128)} %collective-permute-done.4.sib_ref, f32[2,64,896]{2,1,0:T(8,128)S(1)} %get-tuple-element.145.xnear_ref, ...), custom_call_target="tpu_custom_call" | custom-call | flops 9865003008 | bytes 51380224 | tf_op jit(solution)/shard_map/first_product/pallas_call | solution.py:56
  94.7 3.9 collective-permute-start.7
  101.6 20.8 %collective-permute-done.7.xnear_ref = f32[2,64,896]{2,1,0:T(8,128)S(1)} collective-permute-done((f32[2,64,896]{2,1,0:T(8,128)S(1)}, f32[2,64,896]{2,1,0:T(8,128)S(1)}, u32[]{:S(2)}, u32[]{:S(2)}) %collective-permute-start.7) | collective-permute-done | bytes 458784 | tf_op jit(solution)/shard_map/ppermute | solution.py:167
  123.0 22.8 %first_product.5 = f32[2,128,896]{2,1,0:T(8,128)S(1)} custom-call(f32[64,7168]{1,0:T(8,128)} %collective-permute-done.near_ref, f32[64,7168]{1,0:T(8,128)} %collective-permute-done.6.far_ref, f32[896,7168]{1,0:T(8,128)} %own_ref.15, f32[896,7168]{1,0:T(8,128)} %collective-permute-done.4.sib_ref, f32[2,64,896]{2,1,0:T(8,128)S(1)} %collective-permute-done.7.xnear_ref, ...), custom_call_target="tpu_custom_call" | custom-call | flops 9865003008 | bytes 51380224 | tf_op jit(solution)/shard_map/first_product/pallas_call | solution.py:56
  147.5 4.2 collective-permute-start.13
  156.1 14.8 %collective-permute-done.13.xfar_ref = f32[2,64,896]{2,1,0:T(8,128)S(1)} collective-permute-done((f32[2,64,896]{2,1,0:T(8,128)}, f32[2,64,896]{2,1,0:T(8,128)S(1)}, u32[]{:S(2)}, u32[]{:S(2)}) %collective-permute-start.13) | collective-permute-done | bytes 458784 | tf_op jit(solution)/shard_map/ppermute | solution.py:167
  170.9 16.3 %collective-permute-start.17 = (f32[2,64,896]{2,1,0:T(8,128)}, f32[2,64,896]{2,1,0:T(8,128)S(1)}, u32[]{:S(2)}, u32[]{:S(2)}) collective-permute-start(f32[2,64,896]{2,1,0:T(8,128)} %get-tuple-element.142), channel_id=1, source_target_pairs={{0,28},{2,30},{4,24},{6,26},{9,5},{11,7},{13,1},{15,3},{17,13},{19... | collective-permute-start | bytes 1376264 | tf_op jit(solution)/shard_map/ppermute | solution.py:167
  193.6 22.9 %first_product.6 = f32[2,128,896]{2,1,0:T(8,128)S(1)} custom-call(f32[64,7168]{1,0:T(8,128)} %collective-permute-done.5.near_ref, f32[64,7168]{1,0:T(8,128)} %collective-permute-done.11.far_ref, f32[896,7168]{1,0:T(8,128)} %own_ref.15, f32[896,7168]{1,0:T(8,128)} %collective-permute-done.4.sib_ref, f32[2,64,896]{2,1,0:T(8,128)} %collective-permute-done.12.xnear_ref, ...), custom_call_target="tpu_custom_call" | custom-call | flops 9865003008 | bytes 51380224 | tf_op jit(solution)/shard_map/first_product/pallas_call | solution.py:56
  218.8 23.7 %second_product.4 = (f32[64,7168]{1,0:T(8,128)S(1)}, f32[64,7168]{1,0:T(8,128)S(1)}) custom-call(f32[2,128,896]{2,1,0:T(8,128)S(1)} %add.224.change_ref, f32[896,7168]{1,0:T(8,128)} %own_ref.15, f32[896,7168]{1,0:T(8,128)} %collective-permute-done.4.sib_ref), custom_call_target="tpu_custom_call" | custom-call | flops 9865003008 | bytes 51380224 | tf_op jit(solution)/shard_map/second_product/pallas_call | solution.py:94
  246.3 13.8 %collective-permute-start.23 = (f32[2,64,896]{2,1,0:T(8,128)S(1)}, f32[2,64,896]{2,1,0:T(8,128)}, u32[]{:S(2)}, u32[]{:S(2)}) collective-permute-start(f32[2,64,896]{2,1,0:T(8,128)S(1)} %get-tuple-element.152), channel_id=1, source_target_pairs={{17,1},{19,3},{21,5},{23,7},{25,9},{27,11},{29,13},{31,15},{0,16},... | collective-permute-start | bytes 1376264 | tf_op jit(solution)/shard_map/ppermute | solution.py:220
  261.6 22.3 %first_product.7 = f32[2,128,896]{2,1,0:T(8,128)S(1)} custom-call(f32[64,7168]{1,0:T(8,128)} %collective-permute-done.10.near_ref, f32[64,7168]{1,0:T(8,128)S(1)} %collective-permute-done.15.far_ref, f32[896,7168]{1,0:T(8,128)} %own_ref.15, f32[896,7168]{1,0:T(8,128)} %collective-permute-done.4.sib_ref, f32[2,64,896]{2,1,0:T(8,128)S(1)} %collective-permute-done.16.xnear_ref, ...), custom_call_target="tpu_custom_call" | custom-call | flops 9865003008 | bytes 51380224 | tf_op jit(solution)/shard_map/first_product/pallas_call | solution.py:56
  284.0 23.7 %second_product.5 = (f32[64,7168]{1,0:T(8,128)S(1)}, f32[64,7168]{1,0:T(8,128)S(1)}) custom-call(f32[2,128,896]{2,1,0:T(8,128)S(1)} %add.225.change_ref, f32[896,7168]{1,0:T(8,128)} %own_ref.15, f32[896,7168]{1,0:T(8,128)} %collective-permute-done.4.sib_ref), custom_call_target="tpu_custom_call" | custom-call | flops 9865003008 | bytes 51380224 | tf_op jit(solution)/shard_map/second_product/pallas_call | solution.py:94
  318.2 24.6 %second_product.6 = (f32[64,7168]{1,0:T(8,128)S(1)}, f32[64,7168]{1,0:T(8,128)}) custom-call(f32[2,128,896]{2,1,0:T(8,128)S(1)} %add.226.change_ref, f32[896,7168]{1,0:T(8,128)} %own_ref.15, f32[896,7168]{1,0:T(8,128)} %collective-permute-done.4.sib_ref), custom_call_target="tpu_custom_call" | custom-call | flops 9865003008 | bytes 51380224 | tf_op jit(solution)/shard_map/second_product/pallas_call | solution.py:94
  342.8 25.6 %collective-permute-done.26 = f32[2,64,896]{2,1,0:T(8,128)} collective-permute-done((f32[2,64,896]{2,1,0:T(8,128)}, f32[2,64,896]{2,1,0:T(8,128)}, u32[]{:S(2)}, u32[]{:S(2)}) %collective-permute-start.26) | collective-permute-done | bytes 458784 | tf_op jit(solution)/shard_map/ppermute | solution.py:220
  372.3 24.8 %second_product.7 = (f32[64,7168]{1,0:T(8,128)S(1)}, f32[64,7168]{1,0:T(8,128)}) custom-call(f32[2,128,896]{2,1,0:T(8,128)S(1)} %add.219.change_ref, f32[896,7168]{1,0:T(8,128)} %own_ref.15, f32[896,7168]{1,0:T(8,128)} %collective-permute-done.4.sib_ref), custom_call_target="tpu_custom_call" | custom-call | flops 9865003008 | bytes 51380224 | tf_op jit(solution)/shard_map/second_product/pallas_call | solution.py:94
  397.1 10.6 %collective-permute-done.30 = f32[64,7168]{1,0:T(8,128)} collective-permute-done((f32[64,7168]{1,0:T(8,128)}, f32[64,7168]{1,0:T(8,128)}, u32[]{:S(2)}, u32[]{:S(2)}) %collective-permute-start.30) | collective-permute-done | bytes 1835040 | tf_op jit(solution)/shard_map/ppermute | solution.py:201
  407.7 4.3 collective-permute-done.31
  412.0 3.6 add_add_fusion
  423.6 3.6 reshape.16
  427.3 28.3 %collective-permute-done.33 = f32[64,7168]{1,0:T(8,128)} collective-permute-done((f32[64,7168]{1,0:T(8,128)}, f32[64,7168]{1,0:T(8,128)}, u32[]{:S(2)}, u32[]{:S(2)}) %collective-permute-start.33) | collective-permute-done | bytes 1835040 | tf_op jit(solution)/shard_map/ppermute | solution.py:200
  455.5 8.0 %fusion.5 = (f32[7168,64]{0,1:T(8,128)}, f32[7168,64]{0,1:T(8,128)}, f32[7168,64]{0,1:T(8,128)}) fusion(s32[7168,64]{0,1:T(8,128)} %param.9, f32[7168,64]{0,1:T(8,128)} %param.8, f32[64,7168]{1,0:T(8,128)} %collective-permute-done.33, f32[64,7168]{1,0:T(8,128)S(1)} %get-tuple-element.131, f32[64,7168]{1,0:T(8,128)} %collective-permute-done.32, ...), kind=kLoop, calls=%fused_computation.35 | loop fusion | flops 6881280 | bytes 18350080 | tf_op jit(solution)/shard_map/sub | solution.py:244
  (108 shorter events, 64.8 us)
Async XLA Ops:
  0.6 67.4 %collective-permute-start.4 = (f32[896,7168]{1,0:T(8,128)}, f32[896,7168]{1,0:T(8,128)}, u32[]{:S(2)}, u32[]{:S(2)}) collective-permute-start(f32[896,7168]{1,0:T(8,128)} %own_ref.15), channel_id=1, source_target_pairs={{0,2},{2,0},{4,6},{6,4},{8,10},{10,8},{12,14},{14,12},{16,18},{18,... | collective-permute-start | bytes 77070344 | tf_op jit(solution)/shard_map/ppermute | solution.py:191
  13.5 54.5 %collective-permute-start.2 = (f32[4,2,64,896]{3,2,1,0:T(8,128)}, f32[4,2,64,896]{3,2,1,0:T(8,128)}, u32[]{:S(2)}, u32[]{:S(2)}) collective-permute-start(f32[4,2,64,896]{3,2,1,0:T(8,128)} %fusion.10), channel_id=1, source_target_pairs={{0,1},{1,0},{2,3},{3,2},{4,5},{5,4},{6,7},{7,6},{8,9},{9,8},{10,11... | collective-permute-start | bytes 5505032 | tf_op jit(solution)/shard_map/ppermute | solution.py:192
  16.0 51.9 %collective-permute-start.1 = (f32[64,7168]{1,0:T(8,128)S(1)}, f32[64,7168]{1,0:T(8,128)}, u32[]{:S(2)}, u32[]{:S(2)}) collective-permute-start(f32[64,7168]{1,0:T(8,128)S(1)} %get-tuple-element.141.near_ref), channel_id=1, source_target_pairs={{0,4},{2,6},{4,0},{6,2},{8,12},{10,14},{12,8},{14,10},{16,20},{18,... | collective-permute-start | bytes 5505032 | tf_op jit(solution)/shard_map/ppermute | solution.py:189
  17.5 50.5 %collective-permute-start = (f32[64,7168]{1,0:T(8,128)S(1)}, f32[64,7168]{1,0:T(8,128)}, u32[]{:S(2)}, u32[]{:S(2)}) collective-permute-start(f32[64,7168]{1,0:T(8,128)S(1)} %get-tuple-element.141.near_ref), channel_id=1, source_target_pairs={{0,8},{2,10},{4,12},{6,14},{8,16},{10,18},{12,20},{14,22},{16,24},... | collective-permute-start | bytes 5505032 | tf_op jit(solution)/shard_map/ppermute | solution.py:187
  21.4 46.5 %collective-permute-start.3 = (f32[2,64,896]{2,1,0:T(8,128)S(1)}, f32[2,64,896]{2,1,0:T(8,128)S(1)}, u32[]{:S(2)}, u32[]{:S(2)}) collective-permute-start(f32[2,64,896]{2,1,0:T(8,128)S(1)} %get-tuple-element.146), channel_id=1, source_target_pairs={{0,4},{2,6},{4,0},{6,2},{8,12},{10,14},{12,8},{14,10},{17,21},{19,... | collective-permute-start | bytes 1376264 | tf_op jit(solution)/shard_map/ppermute | solution.py:167
  68.0 54.4 %collective-permute-start.6 = (f32[64,7168]{1,0:T(8,128)}, f32[64,7168]{1,0:T(8,128)}, u32[]{:S(2)}, u32[]{:S(2)}) collective-permute-start(f32[64,7168]{1,0:T(8,128)} %collective-permute-done.near_ref), channel_id=1, source_target_pairs={{0,4},{2,6},{4,0},{6,2},{8,12},{10,14},{12,8},{14,10},{16,20},{18,... | collective-permute-start | bytes 5505032 | tf_op jit(solution)/shard_map/ppermute | solution.py:189
  69.6 52.9 %collective-permute-start.5 = (f32[64,7168]{1,0:T(8,128)}, f32[64,7168]{1,0:T(8,128)}, u32[]{:S(2)}, u32[]{:S(2)}) collective-permute-start(f32[64,7168]{1,0:T(8,128)} %collective-permute-done.near_ref), channel_id=1, source_target_pairs={{0,8},{2,10},{4,12},{6,14},{8,16},{10,18},{12,20},{14,22},{16,24},... | collective-permute-start | bytes 5505032 | tf_op jit(solution)/shard_map/ppermute | solution.py:187
  122.4 64.8 %collective-permute-start.11 = (f32[64,7168]{1,0:T(8,128)}, f32[64,7168]{1,0:T(8,128)}, u32[]{:S(2)}, u32[]{:S(2)}) collective-permute-start(f32[64,7168]{1,0:T(8,128)} %collective-permute-done.5.near_ref), channel_id=1, source_target_pairs={{0,4},{2,6},{4,0},{6,2},{8,12},{10,14},{12,8},{14,10},{16,20},{18,... | collective-permute-start | bytes 5505032 | tf_op jit(solution)/shard_map/ppermute | solution.py:189
  123.0 64.2 %collective-permute-start.10 = (f32[64,7168]{1,0:T(8,128)}, f32[64,7168]{1,0:T(8,128)}, u32[]{:S(2)}, u32[]{:S(2)}) collective-permute-start(f32[64,7168]{1,0:T(8,128)} %collective-permute-done.5.near_ref), channel_id=1, source_target_pairs={{0,8},{2,10},{4,12},{6,14},{8,16},{10,18},{12,20},{14,22},{16,24},... | collective-permute-start | bytes 5505032 | tf_op jit(solution)/shard_map/ppermute | solution.py:187
  145.9 41.3 %collective-permute-start.14 = (f32[2,128,896]{2,1,0:T(8,128)S(1)}, f32[2,128,896]{2,1,0:T(8,128)}, u32[]{:S(2)}, u32[]{:S(2)}) collective-permute-start(f32[2,128,896]{2,1,0:T(8,128)S(1)} %first_product.5), channel_id=1, source_target_pairs={{0,1},{1,0},{2,3},{3,2},{4,5},{5,4},{6,7},{7,6},{8,9},{9,8},{10,11... | collective-permute-start | bytes 2752520 | tf_op jit(solution)/shard_map/ppermute | solution.py:170
  170.9 71.6 %collective-permute-start.17 = (f32[2,64,896]{2,1,0:T(8,128)}, f32[2,64,896]{2,1,0:T(8,128)S(1)}, u32[]{:S(2)}, u32[]{:S(2)}) collective-permute-start(f32[2,64,896]{2,1,0:T(8,128)} %get-tuple-element.142), channel_id=1, source_target_pairs={{0,28},{2,30},{4,24},{6,26},{9,5},{11,7},{13,1},{15,3},{17,13},{19... | collective-permute-start | bytes 1376264 | tf_op jit(solution)/shard_map/ppermute | solution.py:167
  188.5 53.9 %collective-permute-start.19 = (f32[2,64,896]{2,1,0:T(8,128)S(1)}, f32[2,64,896]{2,1,0:T(8,128)S(1)}, u32[]{:S(2)}, u32[]{:S(2)}) collective-permute-start(f32[2,64,896]{2,1,0:T(8,128)S(1)} %slice.32), channel_id=1, source_target_pairs={{8,0},{10,2},{12,4},{14,6},{17,9},{19,11},{21,13},{23,15},{25,17},... | collective-permute-start | bytes 1376264 | tf_op jit(solution)/shard_map/ppermute | solution.py:220
  191.5 51.0 %collective-permute-start.16 = (f32[2,64,896]{2,1,0:T(8,128)S(1)}, f32[2,64,896]{2,1,0:T(8,128)S(1)}, u32[]{:S(2)}, u32[]{:S(2)}) collective-permute-start(f32[2,64,896]{2,1,0:T(8,128)S(1)} %dynamic-slice_bitcast_fusion.1), channel_id=1, source_target_pairs={{1,25},{3,27},{5,29},{7,31},{8,0},{10,2},{12,4},{14,6},{16,8},{18,... | collective-permute-start | bytes 1376264 | tf_op jit(solution)/shard_map/ppermute | solution.py:167
  193.0 49.5 %collective-permute-start.15 = (f32[64,7168]{1,0:T(8,128)}, f32[64,7168]{1,0:T(8,128)S(1)}, u32[]{:S(2)}, u32[]{:S(2)}) collective-permute-start(f32[64,7168]{1,0:T(8,128)} %collective-permute-done.10.near_ref), channel_id=1, source_target_pairs={{0,4},{2,6},{4,0},{6,2},{8,12},{10,14},{12,8},{14,10},{16,20},{18,... | collective-permute-start | bytes 5505032 | tf_op jit(solution)/shard_map/ppermute | solution.py:189
  243.4 64.3 %collective-permute-start.22 = (f32[2,64,896]{2,1,0:T(8,128)}, f32[2,64,896]{2,1,0:T(8,128)S(1)}, u32[]{:S(2)}, u32[]{:S(2)}) collective-permute-start(f32[2,64,896]{2,1,0:T(8,128)} %slice.25), channel_id=1, source_target_pairs={{13,0},{15,2},{9,4},{11,6},{20,9},{22,11},{16,13},{18,15},{28,17},... | collective-permute-start | bytes 1376264 | tf_op jit(solution)/shard_map/ppermute | solution.py:220
  244.9 62.8 %collective-permute-start.24 = (f32[2,64,896]{2,1,0:T(8,128)S(1)}, f32[2,64,896]{2,1,0:T(8,128)}, u32[]{:S(2)}, u32[]{:S(2)}) collective-permute-start(f32[2,64,896]{2,1,0:T(8,128)S(1)} %get-tuple-element.151), channel_id=1, source_target_pairs={{20,1},{22,3},{16,5},{18,7},{28,9},{30,11},{24,13},{26,15},{5,16},... | collective-permute-start | bytes 1376264 | tf_op jit(solution)/shard_map/ppermute | solution.py:220
  246.3 61.4 %collective-permute-start.23 = (f32[2,64,896]{2,1,0:T(8,128)S(1)}, f32[2,64,896]{2,1,0:T(8,128)}, u32[]{:S(2)}, u32[]{:S(2)}) collective-permute-start(f32[2,64,896]{2,1,0:T(8,128)S(1)} %get-tuple-element.152), channel_id=1, source_target_pairs={{17,1},{19,3},{21,5},{23,7},{25,9},{27,11},{29,13},{31,15},{0,16},... | collective-permute-start | bytes 1376264 | tf_op jit(solution)/shard_map/ppermute | solution.py:220
  260.1 48.3 %collective-permute-start.20 = (f32[64,7168]{1,0:T(8,128)S(1)}, f32[64,7168]{1,0:T(8,128)S(1)}, u32[]{:S(2)}, u32[]{:S(2)}) collective-permute-start(f32[64,7168]{1,0:T(8,128)S(1)} %get-tuple-element.92), channel_id=1, source_target_pairs={{0,4},{2,6},{4,0},{6,2},{8,12},{10,14},{12,8},{14,10},{16,20},{18,... | collective-permute-start | bytes 5505032 | tf_op jit(solution)/shard_map/ppermute | solution.py:201
  308.8 59.6 %collective-permute-start.25 = (f32[64,7168]{1,0:T(8,128)S(1)}, f32[64,7168]{1,0:T(8,128)S(1)}, u32[]{:S(2)}, u32[]{:S(2)}) collective-permute-start(f32[64,7168]{1,0:T(8,128)S(1)} %get-tuple-element.102), channel_id=1, source_target_pairs={{0,4},{2,6},{4,0},{6,2},{8,12},{10,14},{12,8},{14,10},{16,20},{18,... | collective-permute-start | bytes 5505032 | tf_op jit(solution)/shard_map/ppermute | solution.py:201
  310.0 58.4 %collective-permute-start.29 = (f32[64,7168]{1,0:T(8,128)S(1)}, f32[64,7168]{1,0:T(8,128)S(1)}, u32[]{:S(2)}, u32[]{:S(2)}) collective-permute-start(f32[64,7168]{1,0:T(8,128)S(1)} %add.227), channel_id=1, source_target_pairs={{0,8},{2,10},{4,12},{6,14},{8,16},{10,18},{12,20},{14,22},{16,24},... | collective-permute-start | bytes 5505032 | tf_op jit(solution)/shard_map/ppermute | solution.py:200
  310.9 57.4 %collective-permute-start.26 = (f32[2,64,896]{2,1,0:T(8,128)}, f32[2,64,896]{2,1,0:T(8,128)}, u32[]{:S(2)}, u32[]{:S(2)}) collective-permute-start(f32[2,64,896]{2,1,0:T(8,128)} %get-tuple-element.149), channel_id=1, source_target_pairs={{4,0},{6,2},{0,4},{2,6},{12,8},{14,10},{8,12},{10,14},{21,17},{23,... | collective-permute-start | bytes 1376264 | tf_op jit(solution)/shard_map/ppermute | solution.py:220
  314.0 54.4 %collective-permute-start.28 = (f32[2,64,896]{2,1,0:T(8,128)S(1)}, f32[2,64,896]{2,1,0:T(8,128)}, u32[]{:S(2)}, u32[]{:S(2)}) collective-permute-start(f32[2,64,896]{2,1,0:T(8,128)S(1)} %get-tuple-element.147), channel_id=1, source_target_pairs={{28,1},{30,3},{24,5},{26,7},{5,8},{7,10},{1,12},{3,14},{13,16},{15... | collective-permute-start | bytes 1376264 | tf_op jit(solution)/shard_map/ppermute | solution.py:220
  315.5 52.9 %collective-permute-start.27 = (f32[2,64,896]{2,1,0:T(8,128)S(1)}, f32[2,64,896]{2,1,0:T(8,128)}, u32[]{:S(2)}, u32[]{:S(2)}) collective-permute-start(f32[2,64,896]{2,1,0:T(8,128)S(1)} %get-tuple-element.148), channel_id=1, source_target_pairs={{25,1},{27,3},{29,5},{31,7},{0,8},{2,10},{4,12},{6,14},{8,16},{10,... | collective-permute-start | bytes 1376264 | tf_op jit(solution)/shard_map/ppermute | solution.py:220
  371.1 40.9 %collective-permute-start.31 = (f32[64,7168]{1,0:T(8,128)}, f32[64,7168]{1,0:T(8,128)}, u32[]{:S(2)}, u32[]{:S(2)}) collective-permute-start(f32[64,7168]{1,0:T(8,128)} %add_add_fusion.1), channel_id=1, source_target_pairs={{0,8},{2,10},{4,12},{6,14},{8,16},{10,18},{12,20},{14,22},{16,24},... | collective-permute-start | bytes 5505032 | tf_op jit(solution)/shard_map/ppermute | solution.py:200
  (20 other events, 411.2 us)

commit v3 on v2

--- a/solution.py
+++ b/solution.py
@@ -28,7 +28,35 @@
     return both[:rows] + (both[rows:] + cross)
 
 
-def first_kernel(near_ref, far_ref, own_ref, sib_ref, xnear_ref, xfar_ref, out_ref, parts):
+def prepare_kernel(dense_ref, iterate_ref, multiplier_ref, mask_ref, change_ref, rest_ref):
+    iterate, multiplier = iterate_ref[...], multiplier_ref[...]
+    projected = mask_ref[...].astype(jnp.float32) * (iterate + multiplier)
+    change_ref[...] = (iterate - dense_ref[...]).T
+    rest_ref[0] = (iterate - step_size * (penalty * (iterate - projected + multiplier)) - dense_ref[...]).T
+
+
+def prepare(dense, iterate, multiplier, mask, blocks):
+    rows, half = dense.shape
+    tile = rows // blocks
+    band = pl.BlockSpec((tile, half), lambda i: (i, 0))
+    return pl.pallas_call(
+        prepare_kernel,
+        grid=(blocks,),
+        in_specs=[band] * 4,
+        out_specs=[
+            pl.BlockSpec((half, tile), lambda i: (0, i)),
+            pl.BlockSpec((1, half, tile), lambda i: (i, 0, 0)),
+        ],
+        out_shape=[
+            jax.ShapeDtypeStruct((half, rows), jnp.float32),
+            jax.ShapeDtypeStruct((blocks, half, tile), jnp.float32),
+        ],
+        compiler_params=pltpu.CompilerParams(vmem_limit_bytes=VMEM_BYTES),
+        name="prepare",
+    )(dense, iterate, multiplier, mask)
+
+
+def first_kernel(near_ref, far_ref, own_ref, sib_ref, out_ref, parts):
     half = near_ref.shape[0]
     rows = 2 * half
 
@@ -41,22 +69,19 @@
     rows_of_h = jnp.concatenate([own_ref[...], sib_ref[...]], axis=0)
     product = dot_f32(parts, rows_of_h, rows, (((1,), (1,)), ((), ())))
     for which in range(2):
-        part = product[:, which * tile : (which + 1) * tile]
-        out_ref[which, :half] = xnear_ref[which] - step_size * part[:half]
-        out_ref[which, half:] = xfar_ref[which] - step_size * part[half:]
-
-
-def first(near, far, own, sib, xnear, xfar):
+        out_ref[which] = -step_size * product[:, which * tile : (which + 1) * tile]
+
+
+def first(near, far, own, sib):
     half, depth = near.shape
     rows = own.shape[0]
     tile = 128 if rows % 128 == 0 else rows
     whole = pl.BlockSpec((half, depth), lambda i: (0, 0))
     band = pl.BlockSpec((tile, depth), lambda i: (i, 0))
-    piece = pl.BlockSpec((2, half, tile), lambda i: (0, 0, i))
     return pl.pallas_call(
         first_kernel,
         grid=(rows // tile,),
-        in_specs=[whole, whole, band, band, piece, piece],
+        in_specs=[whole, whole, band, band],
         out_specs=pl.BlockSpec((2, 2 * half, tile), lambda i: (0, 0, i)),
         out_shape=jax.ShapeDtypeStruct((2, 2 * half, rows), jnp.float32),
         scratch_shapes=[pltpu.VMEM((4 * half, depth), jnp.bfloat16)],
@@ -65,7 +90,7 @@
             flops=3 * 2 * 4 * half * depth * rows, bytes_accessed=8 * rows * depth, transcendentals=0
         ),
         name="first_product",
-    )(near, far, own, sib, xnear, xfar)
+    )(near, far, own, sib)
 
 
 def second_kernel(change_ref, own_ref, sib_ref, near_ref, far_ref, parts):
@@ -147,14 +172,8 @@
     permute = lax.ppermute
 
     keeping = keep_mask.astype(jnp.float32)
-    projected = keeping * (start_iterate + start_multiplier)
-    change = (start_iterate - dense_weight).T
+    change, rest = prepare(dense_weight, start_iterate, start_multiplier, keep_mask, per_plane)
     sibling = permute(hessian, "row", to_sibling)
-
-    rest = start_iterate - step_size * (penalty * (start_iterate - projected + start_multiplier)) - dense_weight
-    rest = rest.reshape(per_plane, CORES, depth, half)
-    rest = jnp.where(core == 0, rest, rest[:, ::-1])
-    rest = rest.transpose(0, 1, 3, 2)
 
     def piece(shift, flip):
         turn = cross(shift, flip)
@@ -162,6 +181,8 @@
         first_chip = ((plane - turn) % planes) * per_plane
         source = rest_by[turn]
         part = lax.dynamic_index_in_dim(source, jnp.clip(chip - first_chip, 0, per_plane - 1), 0, keepdims=False)
+        part = part.reshape(half, CORES, depth)
+        part = jnp.where(core == 0, part, part[:, ::-1]).transpose(1, 0, 2)
         if shift == 0 and flip == 0:
             return jnp.where(chip // per_plane == plane, part, 0.0)
         return permute(part, both, route(shift, flip))
@@ -171,11 +192,11 @@
         return functools.reduce(jnp.add, others) if others else jnp.zeros_like(part)
 
     rest_by = {0: rest}
-    near, far, added = {0: change}, {}, {(0, 0): piece(0, 0)}
-    mine, other, changed, kept, sent, swapped, back = {}, {}, {}, {}, {}, {}, {}
+    near, far, added = {0: change}, {}, {}
+    product, mine, other, changed, kept, sent, swapped, back = {}, {}, {}, {}, {}, {}, {}, {}
     total = None
     start = max(ring, 4)
-    returns = [(0, 0, 5), (0, 1, 5)] + [(group, flip, group + 2 + (group == 1 and flip)) for group in range(1, ring) for flip in range(PAIR)]
+    returns = [(0, 0, 5), (0, 1, 4)] + [(g, flip, g + 2 + (g == 1 and flip)) for g in range(1, ring) for flip in range(PAIR)]
     for window in range(start + ring):
         fresh = []
 
@@ -188,23 +209,28 @@
         if window < ring:
             put(far, window, permute(near[window], "row", to_pair))
         if window == 0:
-            sibling = permute(hessian, "row", to_sibling)
             put(rest_by, 1, permute(rest, "col", [(y, (y + 1) % planes) for y in range(planes)]))
-            put(added, (0, 1), piece(0, 1))
         elif window < ring:
             for flip in range(PAIR):
-                put(added, (window, flip), piece(window, flip))
+                added[window, flip] = piece(window, flip)
+        if window == 1:
+            for flip in range(PAIR):
+                put(added, (0, flip), piece(0, flip))
         closing = window - start + 1
         if closing >= 1:
             if total is not None:
                 total = permute(total, "row", to_next)
             put(swapped, closing % ring, permute(sent[closing % ring], "row", to_pair))
         group = window - 2
-        if 0 <= group < ring:
+        if 1 <= group < ring:
             put(changed, group, mine[group] + other[group])
+        if group == 1:
+            put(changed, 0, mine[0] + other[0])
         group = window - 1
         if 0 <= group < ring:
-            put(mine, group, first(near[group], far[group], hessian, sibling, added[group, 0], added[group, 1]))
+            put(product, group, first(near[group], far[group], hessian, sibling))
+        for group in (0, 1) if window == 2 else (window - 1,) if 2 < window <= ring else ():
+            put(mine, group, product[group] + jnp.concatenate([added[group, 0], added[group, 1]], axis=1))
             put(other, group, sum_planes(mine[group]))
         group = window - 2
         if window == start + ring - 2:

time: 464 us -> 443 us (0.955)
  waiting for transfers between devices: 149 us -> 103 us
  local copies, waits for them, and re-layouts: 26.3 us -> 42.1 us
  Pallas kernels: 187 us -> 195 us
    ppermute x7, waiting for transfers between devices: 79.6 us -> 2.76 us  [piece(): return permute(part, both, route(shift, flip))]
    ppermute x1, waiting for transfers between devices: 0.01 us -> 37.6 us  [per_device(): permute(rest, 'col', [(y, (y + 1) % planes) for y in range(planes)])]
    unnamed x27 -> x57, local copies, waits for them, and re-layouts: 5.03 us -> 18.2 us
    ppermute x7, starting transfers between devices: 30.3 us -> 18.7 us  [piece(): return permute(part, both, route(shift, flip))]
    ppermute x4, waiting for transfers between devices: 11.3 us -> 1.8 us  [per_device(): put(swapped, closing % ring, permute(sent[closing % ring], 'row', to_pair))]
    ppermute x4, waiting for transfers between devices: 0.01 us -> 8.2 us  [sum_planes(): permute(part, 'col', [(y, (y + turn) % planes) for y in range(planes)])]
    add x0 -> x5, other arithmetic: none -> 8.08 us  [the longest x4 6.53 us: per_device(): product[group] + jnp.concatenate([added[group, 0], added[group, 1]], axis=1)]
    pallas_call x0 -> x1, Pallas kernels: none -> 7.09 us  [prepare(): pl.pallas_call(prepare_kernel, grid=(blocks,), in_specs=[band] * 4, out_s...]
  transfers between devices with their start and end apart: 34 -> 34, of which waited for: 8 -> 10; matrix products, arithmetic and copies ran while one was open for 8% -> 12% of each run, Pallas kernels for 40% -> 44%
where the time goes in v3:
time: 443 us; the launch traced here: 441 us
  Pallas kernels  195 us (44%)
  waiting for transfers between devices  103 us (23%)
  starting transfers between devices  71.5 us (16%)
  local copies, waits for them, and re-layouts  42.1 us (10%)
  other arithmetic  28.7 us (6%)
    pallas_call x4, Pallas kernels, second(): pl.pallas_call(second_kernel, grid=(columns // tile,), in_specs=[pl.Block...  96.7 us
    pallas_call x4, Pallas kernels, first(): pl.pallas_call(first_kernel, grid=(rows // tile,), in_specs=[whole, whole...  91.3 us
    ppermute x1, waiting for transfers between devices, per_device(): permute(rest, 'col', [(y, (y + 1) % planes) for y in range(planes)])  37.6 us
    ppermute x7, starting transfers between devices, per_device(): part = permute(part, both, route_back(group, flip))  26.6 us
    ppermute x3, waiting for transfers between devices, per_device(): total = permute(total, 'row', to_next)  25.8 us
    ppermute x7, waiting for transfers between devices, per_device(): part = permute(part, both, route_back(group, flip))  21.7 us
    ppermute x7, starting transfers between devices, piece(): return permute(part, both, route(shift, flip))  18.7 us
    unnamed x57, local copies, waits for them, and re-layouts  18.2 us
  transfers between devices with their start and end apart: 34, of which 10 were waited for; matrix products, arithmetic and copies ran while one was open for 12% of the time, Pallas kernels for 44%

profile of v3, /device:TPU:0, one launch (start us, length us, event | category | flops | bytes accessed | tf_op | source)
XLA Modules:
  0.0 441.3 jit_solution(17561702663520701158)
XLA Ops:
  7.3 3.7 copy.14.multiplier_ref
  13.5 7.1 %prepare.1 = (f32[64,7168]{1,0:T(8,128)}, f32[4,64,1792]{2,1,0:T(8,128)S(1)}) custom-call(f32[7168,64]{1,0:T(8,128)} %copy.12.dense_ref, f32[7168,64]{1,0:T(8,128)} %copy.13.iterate_ref, f32[7168,64]{1,0:T(8,128)} %copy.14.multiplier_ref, s32[7168,64]{1,0:T(8,128)} %copy.15.mask_ref), custom_call_target="tpu_custom_call" | custom-call | tf_op jit(solution)/shard_map/prepare/pallas_call | solution.py:42
  26.3 37.6 %collective-permute-done.2 = f32[4,64,1792]{2,1,0:T(8,128)} collective-permute-done((f32[4,64,1792]{2,1,0:T(8,128)S(1)}, f32[4,64,1792]{2,1,0:T(8,128)}, u32[]{:S(2)}, u32[]{:S(2)}) %collective-permute-start.2) | collective-permute-done | bytes 1835040 | tf_op jit(solution)/shard_map/ppermute | solution.py:212
  91.0 22.8 %first_product.4 = f32[2,128,896]{2,1,0:T(8,128)S(1)} custom-call(f32[64,7168]{1,0:T(8,128)} %get-tuple-element.66.near_ref, f32[64,7168]{1,0:T(8,128)} %collective-permute-done.1.far_ref, f32[896,7168]{1,0:T(8,128)} %own_ref.15, f32[896,7168]{1,0:T(8,128)} %collective-permute-done.3.sib_ref), custom_call_target="tpu_custom_call" | custom-call | flops 9865003008 | bytes 51380224 | tf_op jit(solution)/shard_map/first_product/pallas_call | solution.py:81
  122.4 22.8 %first_product.5 = f32[2,128,896]{2,1,0:T(8,128)S(1)} custom-call(f32[64,7168]{1,0:T(8,128)} %collective-permute-done.near_ref, f32[64,7168]{1,0:T(8,128)} %collective-permute-done.5.far_ref, f32[896,7168]{1,0:T(8,128)} %own_ref.15, f32[896,7168]{1,0:T(8,128)} %collective-permute-done.3.sib_ref), custom_call_target="tpu_custom_call" | custom-call | flops 9865003008 | bytes 51380224 | tf_op jit(solution)/shard_map/first_product/pallas_call | solution.py:81
  149.4 4.3 collective-permute-start.15
  154.9 3.7 collective-permute-start.20
  158.6 8.2 %collective-permute-done.12 = f32[2,128,896]{2,1,0:T(8,128)} collective-permute-done((f32[2,128,896]{2,1,0:T(8,128)S(1)}, f32[2,128,896]{2,1,0:T(8,128)}, u32[]{:S(2)}, u32[]{:S(2)}) %collective-permute-start.12) | collective-permute-done | bytes 917536 | tf_op jit(solution)/shard_map/ppermute | solution.py:191
  169.8 22.8 %first_product.6 = f32[2,128,896]{2,1,0:T(8,128)S(1)} custom-call(f32[64,7168]{1,0:T(8,128)} %collective-permute-done.4.near_ref, f32[64,7168]{1,0:T(8,128)} %collective-permute-done.8.far_ref, f32[896,7168]{1,0:T(8,128)} %own_ref.15, f32[896,7168]{1,0:T(8,128)} %collective-permute-done.3.sib_ref), custom_call_target="tpu_custom_call" | custom-call | flops 9865003008 | bytes 51380224 | tf_op jit(solution)/shard_map/first_product/pallas_call | solution.py:81
  199.2 23.7 %second_product.4 = (f32[64,7168]{1,0:T(8,128)S(1)}, f32[64,7168]{1,0:T(8,128)S(1)}) custom-call(f32[2,128,896]{2,1,0:T(8,128)S(1)} %add.221.change_ref, f32[896,7168]{1,0:T(8,128)} %own_ref.15, f32[896,7168]{1,0:T(8,128)} %collective-permute-done.3.sib_ref), custom_call_target="tpu_custom_call" | custom-call | flops 9865003008 | bytes 51380224 | tf_op jit(solution)/shard_map/second_product/pallas_call | solution.py:119
  225.3 4.0 collective-permute-start.17
  233.6 9.8 %collective-permute-done.17 = f32[2,64,896]{2,1,0:T(8,128)S(1)} collective-permute-done((f32[2,64,896]{2,1,0:T(8,128)S(1)}, f32[2,64,896]{2,1,0:T(8,128)S(1)}, u32[]{:S(2)}, u32[]{:S(2)}) %collective-permute-start.17) | collective-permute-done | bytes 458784 | tf_op jit(solution)/shard_map/ppermute | solution.py:246
  247.9 22.8 %first_product.7 = f32[2,128,896]{2,1,0:T(8,128)S(1)} custom-call(f32[64,7168]{1,0:T(8,128)} %collective-permute-done.7.near_ref, f32[64,7168]{1,0:T(8,128)} %collective-permute-done.13.far_ref, f32[896,7168]{1,0:T(8,128)} %own_ref.15, f32[896,7168]{1,0:T(8,128)} %collective-permute-done.3.sib_ref), custom_call_target="tpu_custom_call" | custom-call | flops 9865003008 | bytes 51380224 | tf_op jit(solution)/shard_map/first_product/pallas_call | solution.py:81
  270.8 11.1 %collective-permute-start.24 = (f32[2,64,896]{2,1,0:T(8,128)S(1)}, f32[2,64,896]{2,1,0:T(8,128)S(1)}, u32[]{:S(2)}, u32[]{:S(2)}) collective-permute-start(f32[2,64,896]{2,1,0:T(8,128)S(1)} %get-tuple-element.147), channel_id=1, source_target_pairs={{17,1},{19,3},{21,5},{23,7},{25,9},{27,11},{29,13},{31,15},{0,16},... | collective-permute-start | bytes 1376264 | tf_op jit(solution)/shard_map/ppermute | solution.py:246
  286.4 23.7 %second_product.5 = (f32[64,7168]{1,0:T(8,128)S(1)}, f32[64,7168]{1,0:T(8,128)S(1)}) custom-call(f32[2,128,896]{2,1,0:T(8,128)S(1)} %add.228.change_ref, f32[896,7168]{1,0:T(8,128)} %own_ref.15, f32[896,7168]{1,0:T(8,128)} %collective-permute-done.3.sib_ref), custom_call_target="tpu_custom_call" | custom-call | flops 9865003008 | bytes 51380224 | tf_op jit(solution)/shard_map/second_product/pallas_call | solution.py:119
  316.6 5.4 %collective-permute-start.27 = (f32[2,64,896]{2,1,0:T(8,128)S(1)}, f32[2,64,896]{2,1,0:T(8,128)}, u32[]{:S(2)}, u32[]{:S(2)}) collective-permute-start(f32[2,64,896]{2,1,0:T(8,128)S(1)} %get-tuple-element.143), channel_id=1, source_target_pairs={{25,1},{27,3},{29,5},{31,7},{0,8},{2,10},{4,12},{6,14},{8,16},{10,... | collective-permute-start | bytes 1376264 | tf_op jit(solution)/shard_map/ppermute | solution.py:246
  322.0 24.6 %second_product.6 = (f32[64,7168]{1,0:T(8,128)S(1)}, f32[64,7168]{1,0:T(8,128)}) custom-call(f32[2,128,896]{2,1,0:T(8,128)S(1)} %add.234.change_ref, f32[896,7168]{1,0:T(8,128)} %own_ref.15, f32[896,7168]{1,0:T(8,128)} %collective-permute-done.3.sib_ref), custom_call_target="tpu_custom_call" | custom-call | flops 9865003008 | bytes 51380224 | tf_op jit(solution)/shard_map/second_product/pallas_call | solution.py:119
  346.6 11.8 %collective-permute-done.27 = f32[2,64,896]{2,1,0:T(8,128)} collective-permute-done((f32[2,64,896]{2,1,0:T(8,128)S(1)}, f32[2,64,896]{2,1,0:T(8,128)}, u32[]{:S(2)}, u32[]{:S(2)}) %collective-permute-start.27) | collective-permute-done | bytes 458784 | tf_op jit(solution)/shard_map/ppermute | solution.py:246
  365.5 24.8 %second_product.7 = (f32[64,7168]{1,0:T(8,128)S(1)}, f32[64,7168]{1,0:T(8,128)}) custom-call(f32[2,128,896]{2,1,0:T(8,128)S(1)} %add.222.change_ref, f32[896,7168]{1,0:T(8,128)} %own_ref.15, f32[896,7168]{1,0:T(8,128)} %collective-permute-done.3.sib_ref), custom_call_target="tpu_custom_call" | custom-call | flops 9865003008 | bytes 51380224 | tf_op jit(solution)/shard_map/second_product/pallas_call | solution.py:119
  392.1 7.4 %collective-permute-done.31 = f32[64,7168]{1,0:T(8,128)} collective-permute-done((f32[64,7168]{1,0:T(8,128)}, f32[64,7168]{1,0:T(8,128)}, u32[]{:S(2)}, u32[]{:S(2)}) %collective-permute-start.31) | collective-permute-done | bytes 1835040 | tf_op jit(solution)/shard_map/ppermute | solution.py:222
  399.4 3.6 add_add_fusion
  411.2 3.6 reshape.49
  414.8 18.4 %collective-permute-done.33 = f32[64,7168]{1,0:T(8,128)} collective-permute-done((f32[64,7168]{1,0:T(8,128)}, f32[64,7168]{1,0:T(8,128)}, u32[]{:S(2)}, u32[]{:S(2)}) %collective-permute-start.33) | collective-permute-done | bytes 1835040 | tf_op jit(solution)/shard_map/ppermute | solution.py:222
  433.2 8.0 %fusion.14 = (f32[7168,64]{0,1:T(8,128)}, f32[7168,64]{0,1:T(8,128)}, f32[7168,64]{0,1:T(8,128)}) fusion(s32[7168,64]{0,1:T(8,128)} %param.9, f32[7168,64]{0,1:T(8,128)} %param.8, f32[64,7168]{1,0:T(8,128)} %collective-permute-done.33, f32[64,7168]{1,0:T(8,128)S(1)} %get-tuple-element.127, f32[64,7168]{1,0:T(8,128)} %collective-permute-done.32, ...), kind=kLoop, calls=%fused_computation.53 | loop fusion | flops 6881280 | bytes 18350080 | tf_op jit(solution)/shard_map/sub | solution.py:270
  (160 shorter events, 104.1 us)
Async XLA Ops:
  0.6 68.0 %collective-permute-start.3 = (f32[896,7168]{1,0:T(8,128)}, f32[896,7168]{1,0:T(8,128)}, u32[]{:S(2)}, u32[]{:S(2)}) collective-permute-start(f32[896,7168]{1,0:T(8,128)} %own_ref.15), channel_id=1, source_target_pairs={{0,2},{2,0},{4,6},{6,4},{8,10},{10,8},{12,14},{14,12},{16,18},{18,... | collective-permute-start | bytes 77070344 | tf_op jit(solution)/shard_map/ppermute | solution.py:176
  20.6 43.3 %collective-permute-start.2 = (f32[4,64,1792]{2,1,0:T(8,128)S(1)}, f32[4,64,1792]{2,1,0:T(8,128)}, u32[]{:S(2)}, u32[]{:S(2)}) collective-permute-start(f32[4,64,1792]{2,1,0:T(8,128)S(1)} %get-tuple-element.89), channel_id=1, source_target_pairs={{0,1},{1,0},{2,3},{3,2},{4,5},{5,4},{6,7},{7,6},{8,9},{9,8},{10,11... | collective-permute-start | bytes 5505032 | tf_op jit(solution)/shard_map/ppermute | solution.py:212
  23.2 42.3 %collective-permute-start.1 = (f32[64,7168]{1,0:T(8,128)}, f32[64,7168]{1,0:T(8,128)}, u32[]{:S(2)}, u32[]{:S(2)}) collective-permute-start(f32[64,7168]{1,0:T(8,128)} %get-tuple-element.66.near_ref), channel_id=1, source_target_pairs={{0,4},{2,6},{4,0},{6,2},{8,12},{10,14},{12,8},{14,10},{16,20},{18,... | collective-permute-start | bytes 5505032 | tf_op jit(solution)/shard_map/ppermute | solution.py:210
  24.7 43.9 %collective-permute-start = (f32[64,7168]{1,0:T(8,128)}, f32[64,7168]{1,0:T(8,128)}, u32[]{:S(2)}, u32[]{:S(2)}) collective-permute-start(f32[64,7168]{1,0:T(8,128)} %get-tuple-element.66.near_ref), channel_id=1, source_target_pairs={{0,8},{2,10},{4,12},{6,14},{8,16},{10,18},{12,20},{14,22},{16,24},... | collective-permute-start | bytes 5505032 | tf_op jit(solution)/shard_map/ppermute | solution.py:208
  68.7 51.1 %collective-permute-start.5 = (f32[64,7168]{1,0:T(8,128)}, f32[64,7168]{1,0:T(8,128)}, u32[]{:S(2)}, u32[]{:S(2)}) collective-permute-start(f32[64,7168]{1,0:T(8,128)} %collective-permute-done.near_ref), channel_id=1, source_target_pairs={{0,4},{2,6},{4,0},{6,2},{8,12},{10,14},{12,8},{14,10},{16,20},{18,... | collective-permute-start | bytes 5505032 | tf_op jit(solution)/shard_map/ppermute | solution.py:210
  69.2 50.6 %collective-permute-start.4 = (f32[64,7168]{1,0:T(8,128)}, f32[64,7168]{1,0:T(8,128)}, u32[]{:S(2)}, u32[]{:S(2)}) collective-permute-start(f32[64,7168]{1,0:T(8,128)} %collective-permute-done.near_ref), channel_id=1, source_target_pairs={{0,8},{2,10},{4,12},{6,14},{8,16},{10,18},{12,20},{14,22},{16,24},... | collective-permute-start | bytes 5505032 | tf_op jit(solution)/shard_map/ppermute | solution.py:208
  81.5 63.7 %collective-permute-start.10 = (f32[2,64,896]{2,1,0:T(8,128)}, f32[2,64,896]{2,1,0:T(8,128)}, u32[]{:S(2)}, u32[]{:S(2)}) collective-permute-start(f32[2,64,896]{2,1,0:T(8,128)} %fusion.8), channel_id=1, source_target_pairs={{0,8},{2,10},{4,12},{6,14},{9,17},{11,19},{13,21},{15,23},{17,25},... | collective-permute-start | bytes 1376264 | tf_op jit(solution)/shard_map/ppermute | solution.py:188
  85.4 34.3 %collective-permute-start.6 = (f32[2,64,896]{2,1,0:T(8,128)}, f32[2,64,896]{2,1,0:T(8,128)}, u32[]{:S(2)}, u32[]{:S(2)}) collective-permute-start(f32[2,64,896]{2,1,0:T(8,128)} %fusion.7), channel_id=1, source_target_pairs={{0,4},{2,6},{4,0},{6,2},{8,12},{10,14},{12,8},{14,10},{17,21},{19,... | collective-permute-start | bytes 1376264 | tf_op jit(solution)/shard_map/ppermute | solution.py:188
  89.6 55.6 %collective-permute-start.11 = (f32[2,64,896]{2,1,0:T(8,128)}, f32[2,64,896]{2,1,0:T(8,128)}, u32[]{:S(2)}, u32[]{:S(2)}) collective-permute-start(f32[2,64,896]{2,1,0:T(8,128)} %fusion.9), channel_id=1, source_target_pairs={{1,13},{3,15},{5,9},{7,11},{8,20},{10,22},{12,16},{14,18},{16,28},... | collective-permute-start | bytes 1376264 | tf_op jit(solution)/shard_map/ppermute | solution.py:188
  119.8 48.5 %collective-permute-start.8 = (f32[64,7168]{1,0:T(8,128)}, f32[64,7168]{1,0:T(8,128)}, u32[]{:S(2)}, u32[]{:S(2)}) collective-permute-start(f32[64,7168]{1,0:T(8,128)} %collective-permute-done.4.near_ref), channel_id=1, source_target_pairs={{0,4},{2,6},{4,0},{6,2},{8,12},{10,14},{12,8},{14,10},{16,20},{18,... | collective-permute-start | bytes 5505032 | tf_op jit(solution)/shard_map/ppermute | solution.py:210
  120.3 48.0 %collective-permute-start.7 = (f32[64,7168]{1,0:T(8,128)}, f32[64,7168]{1,0:T(8,128)}, u32[]{:S(2)}, u32[]{:S(2)}) collective-permute-start(f32[64,7168]{1,0:T(8,128)} %collective-permute-done.4.near_ref), channel_id=1, source_target_pairs={{0,8},{2,10},{4,12},{6,14},{8,16},{10,18},{12,20},{14,22},{16,24},... | collective-permute-start | bytes 5505032 | tf_op jit(solution)/shard_map/ppermute | solution.py:208
  149.4 43.2 %collective-permute-start.15 = (f32[2,64,896]{2,1,0:T(8,128)}, f32[2,64,896]{2,1,0:T(8,128)}, u32[]{:S(2)}, u32[]{:S(2)}) collective-permute-start(f32[2,64,896]{2,1,0:T(8,128)} %fusion.11), channel_id=1, source_target_pairs={{0,20},{2,22},{4,16},{6,18},{8,28},{10,30},{12,24},{14,26},{17,5},... | collective-permute-start | bytes 1376264 | tf_op jit(solution)/shard_map/ppermute | solution.py:188
  154.9 115.9 %collective-permute-start.20 = (f32[2,64,896]{2,1,0:T(8,128)}, f32[2,64,896]{2,1,0:T(8,128)S(1)}, u32[]{:S(2)}, u32[]{:S(2)}) collective-permute-start(f32[2,64,896]{2,1,0:T(8,128)} %fusion.13), channel_id=1, source_target_pairs={{0,28},{2,30},{4,24},{6,26},{9,5},{11,7},{13,1},{15,3},{17,13},{19... | collective-permute-start | bytes 1376264 | tf_op jit(solution)/shard_map/ppermute | solution.py:188
  168.3 75.2 %collective-permute-start.13 = (f32[64,7168]{1,0:T(8,128)}, f32[64,7168]{1,0:T(8,128)}, u32[]{:S(2)}, u32[]{:S(2)}) collective-permute-start(f32[64,7168]{1,0:T(8,128)} %collective-permute-done.7.near_ref), channel_id=1, source_target_pairs={{0,4},{2,6},{4,0},{6,2},{8,12},{10,14},{12,8},{14,10},{16,20},{18,... | collective-permute-start | bytes 5505032 | tf_op jit(solution)/shard_map/ppermute | solution.py:210
  194.7 48.7 %collective-permute-start.16 = (f32[2,128,896]{2,1,0:T(8,128)}, f32[2,128,896]{2,1,0:T(8,128)}, u32[]{:S(2)}, u32[]{:S(2)}) collective-permute-start(f32[2,128,896]{2,1,0:T(8,128)} %maximum_add_fusion.2), channel_id=1, source_target_pairs={{0,1},{1,0},{2,3},{3,2},{4,5},{5,4},{6,7},{7,6},{8,9},{9,8},{10,11... | collective-permute-start | bytes 2752520 | tf_op jit(solution)/shard_map/ppermute | solution.py:191
  230.8 51.2 %collective-permute-start.19 = (f32[2,64,896]{2,1,0:T(8,128)S(1)}, f32[2,64,896]{2,1,0:T(8,128)S(1)}, u32[]{:S(2)}, u32[]{:S(2)}) collective-permute-start(f32[2,64,896]{2,1,0:T(8,128)S(1)} %fusion.12), channel_id=1, source_target_pairs={{1,25},{3,27},{5,29},{7,31},{8,0},{10,2},{12,4},{14,6},{16,8},{18,... | collective-permute-start | bytes 1376264 | tf_op jit(solution)/shard_map/ppermute | solution.py:188
  243.5 42.0 %collective-permute-start.23 = (f32[2,64,896]{2,1,0:T(8,128)S(1)}, f32[2,64,896]{2,1,0:T(8,128)S(1)}, u32[]{:S(2)}, u32[]{:S(2)}) collective-permute-start(f32[2,64,896]{2,1,0:T(8,128)S(1)} %slice.26), channel_id=1, source_target_pairs={{13,0},{15,2},{9,4},{11,6},{20,9},{22,11},{16,13},{18,15},{28,17},... | collective-permute-start | bytes 1376264 | tf_op jit(solution)/shard_map/ppermute | solution.py:246
  246.6 63.5 %collective-permute-start.25 = (f32[2,64,896]{2,1,0:T(8,128)S(1)}, f32[2,64,896]{2,1,0:T(8,128)S(1)}, u32[]{:S(2)}, u32[]{:S(2)}) collective-permute-start(f32[2,64,896]{2,1,0:T(8,128)S(1)} %get-tuple-element.146), channel_id=1, source_target_pairs={{20,1},{22,3},{16,5},{18,7},{28,9},{30,11},{24,13},{26,15},{5,16},... | collective-permute-start | bytes 1376264 | tf_op jit(solution)/shard_map/ppermute | solution.py:246
  247.3 62.8 %collective-permute-start.18 = (f32[64,7168]{1,0:T(8,128)S(1)}, f32[64,7168]{1,0:T(8,128)S(1)}, u32[]{:S(2)}, u32[]{:S(2)}) collective-permute-start(f32[64,7168]{1,0:T(8,128)S(1)} %copy-done.6), channel_id=1, source_target_pairs={{0,4},{2,6},{4,0},{6,2},{8,12},{10,14},{12,8},{14,10},{16,20},{18,... | collective-permute-start | bytes 5505032 | tf_op jit(solution)/shard_map/ppermute | solution.py:223
  270.8 39.3 %collective-permute-start.24 = (f32[2,64,896]{2,1,0:T(8,128)S(1)}, f32[2,64,896]{2,1,0:T(8,128)S(1)}, u32[]{:S(2)}, u32[]{:S(2)}) collective-permute-start(f32[2,64,896]{2,1,0:T(8,128)S(1)} %get-tuple-element.147), channel_id=1, source_target_pairs={{17,1},{19,3},{21,5},{23,7},{25,9},{27,11},{29,13},{31,15},{0,16},... | collective-permute-start | bytes 1376264 | tf_op jit(solution)/shard_map/ppermute | solution.py:246
  311.5 47.0 %collective-permute-start.26 = (f32[64,7168]{1,0:T(8,128)S(1)}, f32[64,7168]{1,0:T(8,128)S(1)}, u32[]{:S(2)}, u32[]{:S(2)}) collective-permute-start(f32[64,7168]{1,0:T(8,128)S(1)} %get-tuple-element.99), channel_id=1, source_target_pairs={{0,4},{2,6},{4,0},{6,2},{8,12},{10,14},{12,8},{14,10},{16,20},{18,... | collective-permute-start | bytes 5505032 | tf_op jit(solution)/shard_map/ppermute | solution.py:223
  313.1 45.3 %collective-permute-start.29 = (f32[64,7168]{1,0:T(8,128)S(1)}, f32[64,7168]{1,0:T(8,128)S(1)}, u32[]{:S(2)}, u32[]{:S(2)}) collective-permute-start(f32[64,7168]{1,0:T(8,128)S(1)} %add.235), channel_id=1, source_target_pairs={{0,8},{2,10},{4,12},{6,14},{8,16},{10,18},{12,20},{14,22},{16,24},... | collective-permute-start | bytes 5505032 | tf_op jit(solution)/shard_map/ppermute | solution.py:222
  316.6 41.9 %collective-permute-start.27 = (f32[2,64,896]{2,1,0:T(8,128)S(1)}, f32[2,64,896]{2,1,0:T(8,128)}, u32[]{:S(2)}, u32[]{:S(2)}) collective-permute-start(f32[2,64,896]{2,1,0:T(8,128)S(1)} %get-tuple-element.143), channel_id=1, source_target_pairs={{25,1},{27,3},{29,5},{31,7},{0,8},{2,10},{4,12},{6,14},{8,16},{10,... | collective-permute-start | bytes 1376264 | tf_op jit(solution)/shard_map/ppermute | solution.py:246
  362.8 36.7 %collective-permute-start.31 = (f32[64,7168]{1,0:T(8,128)}, f32[64,7168]{1,0:T(8,128)}, u32[]{:S(2)}, u32[]{:S(2)}) collective-permute-start(f32[64,7168]{1,0:T(8,128)} %add_add_fusion.1), channel_id=1, source_target_pairs={{0,8},{2,10},{4,12},{6,14},{8,16},{10,18},{12,20},{14,22},{16,24},... | collective-permute-start | bytes 5505032 | tf_op jit(solution)/shard_map/ppermute | solution.py:222
  (33 other events, 549.2 us)

commit v4 on v2

v4 whole, which is shorter than its diff:
```python
import functools

import jax
import jax.numpy as jnp
from jax import lax
from jax.experimental import pallas as pl
from jax.experimental.pallas import tpu as pltpu
from jax.sharding import PartitionSpec as P

step_size = 0.25
penalty = 1.0

CORES = 2
PAIR = 2
VMEM_BYTES = 48 * 1024 * 1024


def split(value):
    high = value.astype(jnp.bfloat16)
    low = (value - high.astype(jnp.float32)).astype(jnp.bfloat16)
    return high, low


def dot_f32(left, right, rows, dims):
    high, low = split(right)
    both = lax.dot_general(left[...], high, dims, preferred_element_type=jnp.float32)
    cross = lax.dot_general(left[:rows], low, dims, preferred_element_type=jnp.float32)
    return both[:rows] + (both[rows:] + cross)


def first_kernel(near_ref, far_ref, own_ref, sib_ref, out_ref, parts):
    half = near_ref.shape[0]
    rows = 2 * half

    @pl.when(pl.program_id(0) == 0)
    def _():
        parts[:half], parts[rows : rows + half] = split(near_ref[...])
        parts[half:rows], parts[rows + half :] = split(far_ref[...])

    tile = own_ref.shape[0]
    rows_of_h = jnp.concatenate([own_ref[...], sib_ref[...]], axis=0)
    product = dot_f32(parts, rows_of_h, rows, (((1,), (1,)), ((), ())))
    for which in range(2):
        out_ref[which] = -step_size * product[:, which * tile : (which + 1) * tile]


def first(near, far, own, sib):
    half, depth = near.shape
    rows = own.shape[0]
    tile = 128 if rows % 128 == 0 else rows
    whole = pl.BlockSpec((half, depth), lambda i: (0, 0))
    band = pl.BlockSpec((tile, depth), lambda i: (i, 0))
    return pl.pallas_call(
        first_kernel,
        grid=(rows // tile,),
        in_specs=[whole, whole, band, band],
        out_specs=pl.BlockSpec((2, 2 * half, tile), lambda i: (0, 0, i)),
        out_shape=jax.ShapeDtypeStruct((2, 2 * half, rows), jnp.float32),
        scratch_shapes=[pltpu.VMEM((4 * half, depth), jnp.bfloat16)],
        compiler_params=pltpu.CompilerParams(vmem_limit_bytes=VMEM_BYTES),
        cost_estimate=pl.CostEstimate(
            flops=rows * depth, bytes_accessed=rows * depth, transcendentals=0
        ),
        name="first_product",
    )(near, far, own, sib)


def second_kernel(change_ref, own_ref, sib_ref, near_ref, far_ref, parts):
    _, rows, depth = change_ref.shape
    half = rows // 2

    @pl.when(pl.program_id(0) == 0)
    def _():
        for which in range(2):
            places = slice(which * depth, (which + 1) * depth)
            parts[:rows, places], parts[rows:, places] = split(change_ref[which])

    rows_of_h = jnp.concatenate([own_ref[...], sib_ref[...]], axis=0)
    product = dot_f32(parts, rows_of_h, rows, (((1,), (0,)), ((), ())))
    near_ref[...] = product[:half]
    far_ref[...] = product[half:]


def second(change, own, sib):
    _, rows, depth = change.shape
    half = rows // 2
    columns = own.shape[1]
    tile = next((t for t in (512, 256, 128) if columns % t == 0), columns)
    band = pl.BlockSpec((depth, tile), lambda i: (0, i))
    out = pl.BlockSpec((half, tile), lambda i: (0, i))
    return pl.pallas_call(
        second_kernel,
        grid=(columns // tile,),
        in_specs=[pl.BlockSpec((2, rows, depth), lambda i: (0, 0, 0)), band, band],
        out_specs=[out, out],
        out_shape=[jax.ShapeDtypeStruct((half, columns), jnp.float32)] * 2,
        scratch_shapes=[pltpu.VMEM((2 * rows, 2 * depth), jnp.bfloat16)],
        compiler_params=pltpu.CompilerParams(vmem_limit_bytes=VMEM_BYTES),
        cost_estimate=pl.CostEstimate(
            flops=depth * columns, bytes_accessed=depth * columns, transcendentals=0
        ),
        name="second_product",
    )(change, own, sib)


def per_device(rows_of, planes, hessian, dense_weight, start_iterate, start_multiplier, keep_mask):
    ring = rows_of // (CORES * PAIR)
    chips = ring * PAIR
    per_plane = chips // planes
    depth, columns = hessian.shape
    half = dense_weight.shape[1]
    row = lax.axis_index("row")
    plane = lax.axis_index("col")
    core = row % CORES
    pair = (row // CORES) % PAIR
    place = row // (CORES * PAIR)

    def device(z, x, c):
        return ((z % ring) * PAIR + x) * CORES + c

    everyone = [(z, x, c) for z in range(ring) for x in range(PAIR) for c in range(CORES)]
    to_sibling = [(device(z, x, c), device(z, x, 1 - c)) for z, x, c in everyone]
    to_pair = [(device(z, x, c), device(z, x ^ 1, c)) for z, x, c in everyone]
    to_next = [(device(z, x, c), device(z + 1, x, c)) for z, x, c in everyone]

    def route(shift, flip):
        turn = cross(shift, flip)
        pairs = []
        for z, x, c in everyone:
            for y in range(planes):
                chip = ((z + shift) % ring) * PAIR + (x ^ flip)
                if chip // per_plane == (y - turn) % planes:
                    pairs.append((device(z, x, c) * planes + y, device(z + shift, x ^ flip, c) * planes + y))
        return pairs

    def route_back(shift, flip):
        turn = cross(shift, flip)
        return [(b, a - a % planes + (a - turn) % planes) for a, b in route(shift, flip)]

    def cross(shift, flip):
        return 1 if shift and flip else 0

    both = ("row", "col")
    permute = lax.ppermute

    dense, begun, dual = dense_weight.T, start_iterate.T, start_multiplier.T
    keeping = keep_mask.T.astype(jnp.float32)
    change = begun - dense
    sibling = permute(hessian, "row", to_sibling)
    rest = begun - step_size * (penalty * (begun - keeping * (begun + dual) + dual)) - dense
    rest_by = [rest, permute(rest, "col", [(y, (y + 1) % planes) for y in range(planes)])]

    def piece(shift, flip):
        turn = cross(shift, flip)
        chip = ((place + shift) % ring) * PAIR + (pair ^ flip)
        at = jnp.clip(chip - ((plane - turn) % planes) * per_plane, 0, per_plane - 1)
        part = lax.dynamic_slice_in_dim(rest_by[turn], at * CORES * depth, CORES * depth, 1)
        part = part.reshape(half, CORES, depth)
        part = jnp.where(core == 0, part, part[:, ::-1]).transpose(1, 0, 2)
        if shift == 0 and flip == 0:
            return jnp.where(chip // per_plane == plane, part, 0.0)
        return permute(part, both, route(shift, flip))

    def sum_planes(part):
        others = [permute(part, "col", [(y, (y + turn) % planes) for y in range(planes)]) for turn in range(1, planes)]
        return functools.reduce(jnp.add, others) if others else jnp.zeros_like(part)

    near = {0: change, 1: permute(change, "row", to_next)}
    far = {0: permute(change, "row", to_pair)}
    rest_by = dict(enumerate(rest_by))
    added, mine, other, changed, kept, sums, swapped, back = {}, {}, {}, {}, {}, {}, {}, {}
    last = (near, 0)

    def meet(*entries):
        entries = list(dict.fromkeys([(id(where), key) for where, key in entries + (last,)]))
        wheres = {id(where): where for where in (near, far, rest_by, added, mine, other, changed, kept, sums, swapped, back)}
        values = lax.optimization_barrier([wheres[which][key] for which, key in entries])
        for (which, key), value in zip(entries, values):
            wheres[which][key] = value

    def flips(where, group):
        return [(where, (group, flip)) for flip in range(PAIR)]

    def add_pieces(group):
        if group < ring:
            meet(*((rest_by, turn) for turn in rest_by))
            for flip in range(PAIR):
                added[group, flip] = piece(group, flip)

    def send_back(group):
        meet((changed, group))
        for flip in range(PAIR):
            rows = changed[group][:, flip * half : (flip + 1) * half]
            back[group, flip] = permute(rows, both, route_back(group, flip)) if group or flip else rows

    def run_first(group):
        nonlocal last
        after = group + 1
        if after < ring:
            meet((far, group), (near, after))
            far[after] = permute(near[after], "row", to_pair)
            if after + 1 < ring:
                near[after + 1] = permute(near[after], "row", to_next)
        if group == 0:
            add_pieces(1)
        meet((far, group), (near, group))
        mine[group] = first(near[group], far[group], hessian, sibling)
        last = (mine, group)

    def run_join(group):
        meet(*flips(added, group))
        mine[group] = mine[group] + jnp.concatenate([added[group, flip] for flip in range(PAIR)], axis=1)
        other[group] = sum_planes(mine[group])
        if group:
            add_pieces(group + 1)

    def run_change(group):
        nonlocal last
        meet((other, group), (mine, group))
        changed[group] = mine[group] + other[group]
        last = (changed, group)

    def run_second(group):
        nonlocal last
        meet((changed, group))
        kept[group], sent = second(changed[group], hessian, sibling)
        swapped[group] = permute(sent, "row", to_pair)
        last = (kept, group)

    def run_add(group, total, *following):
        meet((swapped, group), (kept, group))
        part = kept[group] + swapped[group]
        sums[group] = part if total is None else total + part
        if following:
            meet((sums, group), following)
        return permute(sums[group], "row", to_next)

    added[0, 1] = piece(0, 1)
    added[0, 0] = piece(0, 0)
    total = None
    for group in range(ring):
        run_first(group)
        if group >= 3:
            meet(*flips(back, group - 2))
        run_join(group)
        if group >= 3:
            send_back(group - 1)
        if group == 1:
            run_change(0)
        if group == 2:
            run_change(1)
        if group >= 2:
            run_second(group - 1)
            run_change(group)
            if group == 2:
                send_back(1)
        if group >= 3:
            total = run_add(group - 2, total, *((changed, group) if group == ring - 1 else (near, group + 1)))
    meet(*flips(back, ring - 2))
    send_back(ring - 1)
    run_second(ring - 1)
    meet(*flips(back, ring - 1))
    total = run_add(ring - 2, total, changed, 0)
    run_second(0)
    send_back(0)
    total = run_add(ring - 1, total)
    gradient = total + (kept[0] + swapped[0])

    back = jnp.stack([back[shift, flip] for shift in range(ring) for flip in range(PAIR)])
    blocks = []
    for block in range(per_plane):
        chip = plane * per_plane + block
        slot = ((chip // PAIR - place) % ring) * PAIR + ((chip % PAIR) ^ pair)
        part = lax.dynamic_index_in_dim(back, slot, 0, keepdims=False)
        part = jnp.where(core == 0, part, part[::-1])
        blocks += [part[0], part[1]]
    iterate = jnp.concatenate(blocks, axis=1) + dense

    projected = keeping * (iterate + dual)
    multiplier = dual + iterate - projected
    iterate = iterate - step_size * (gradient + penalty * (iterate - projected + multiplier))
    projected = keeping * (iterate + multiplier)
    multiplier = multiplier + iterate - projected
    return (iterate.T, projected.T, multiplier.T)


def solution(mesh):
    return jax.shard_map(
        functools.partial(per_device, mesh.shape["row"], mesh.shape["col"]),
        mesh=mesh,
        in_specs=(
            P("row", "col"),
            P("col", "row"),
            P("col", "row"),
            P("col", "row"),
            P("col", "row"),
        ),
        out_specs=(P("col", "row"), P("col", "row"), P("col", "row")),
        check_vma=False,
    )
```

time: 464 us -> 499 us (1.075)
  waiting for transfers between devices: 149 us -> 190 us
  local copies, waits for them, and re-layouts: 26.3 us -> 15.8 us
  starting transfers between devices: 74.7 us -> 80.9 us
    ppermute x21, waiting for transfers between devices: 69.5 us -> 175 us  [the longest x3 80.3 us: run_add(): return permute(sums[group], 'row', to_next)]
    ppermute x7, waiting for transfers between devices: 79.6 us -> 15 us  [piece(): return permute(part, both, route(shift, flip))]
    ppermute x21, starting transfers between devices: 37.4 us -> 54.6 us  [the longest x7 33.2 us: send_back(): permute(rows, both, route_back(group, flip))]
    ppermute x7, starting transfers between devices: 30.3 us -> 20.3 us  [piece(): return permute(part, both, route(shift, flip))]
    reshape x3 -> x8, local copies, waits for them, and re-layouts: 9.2 us -> 0.25 us  [piece(): part = part.reshape(half, CORES, depth)]
    sub x2 -> x1, other arithmetic: 12.9 us -> 4.92 us  [per_device(): change = begun - dense]
    dynamic_slice x1 -> x6, local copies, waits for them, and re-layouts: 0.13 us -> 6.66 us  [piece(): lax.dynamic_slice_in_dim(rest_by[turn], at * CORES * depth, CORES * depth...]
    squeeze x4 -> x1, local copies, waits for them, and re-layouts: 6.28 us -> 0.15 us  [per_device(): part = lax.dynamic_index_in_dim(back, slot, 0, keepdims=False)]
  transfers between devices with their start and end apart: 34 -> 34, of which waited for: 8 -> 9; matrix products, arithmetic and copies ran while one was open for 8% -> 6% of each run, Pallas kernels for 40% -> 37%
where the time goes in v4:
time: 499 us; the launch traced here: 498 us
  waiting for transfers between devices  190 us (38%)
  Pallas kernels  185 us (37%)
  starting transfers between devices  80.9 us (16%)
  other arithmetic  25.2 us (5%)
  local copies, waits for them, and re-layouts  15.8 us (3%)
    pallas_call x4, Pallas kernels, second(): pl.pallas_call(second_kernel, grid=(columns // tile,), in_specs=[pl.Block...  95.7 us
    pallas_call x4, Pallas kernels, first(): pl.pallas_call(first_kernel, grid=(rows // tile,), in_specs=[whole, whole...  89.7 us
    ppermute x3, waiting for transfers between devices, run_add(): return permute(sums[group], 'row', to_next)  80.3 us
    ppermute x7, waiting for transfers between devices, send_back(): permute(rows, both, route_back(group, flip))  39.7 us
    ppermute x1, waiting for transfers between devices, per_device(): far = {0: permute(change, 'row', to_pair)}  37.6 us
    ppermute x7, starting transfers between devices, send_back(): permute(rows, both, route_back(group, flip))  33.2 us
    ppermute x7, starting transfers between devices, piece(): return permute(part, both, route(shift, flip))  20.3 us
    ppermute x7, waiting for transfers between devices, piece(): return permute(part, both, route(shift, flip))  15 us
  transfers between devices with their start and end apart: 34, of which 9 were waited for; matrix products, arithmetic and copies ran while one was open for 6% of the time, Pallas kernels for 37%

profile of v4, /device:TPU:0, one launch (start us, length us, event | category | flops | bytes accessed | tf_op | source)
XLA Modules:
  0.0 498.4 jit_solution(3102167915468790690)
XLA Ops:
  1.1 4.9 bitcast_subtract_fusion
  11.7 37.6 %collective-permute-done.1.far_ref = f32[64,7168]{1,0:T(8,128)S(1)} collective-permute-done((f32[64,7168]{1,0:T(8,128)S(1)}, f32[64,7168]{1,0:T(8,128)S(1)}, u32[]{:S(2)}, u32[]{:S(2)}) %collective-permute-start.1) | collective-permute-done | bytes 1835040 | tf_op jit(solution)/shard_map/ppermute | solution.py:169
  55.1 2.8 collective-permute-start.7
  62.5 4.9 collective-permute-start.3
  67.4 21.8 %first_product.4 = f32[2,128,896]{2,1,0:T(8,128)S(1)} custom-call(f32[64,7168]{1,0:T(8,128)S(1)} %get-tuple-element.102.near_ref, f32[64,7168]{1,0:T(8,128)S(1)} %copy-done.3, f32[896,7168]{1,0:T(8,128)} %own_ref.15, f32[896,7168]{1,0:T(8,128)} %collective-permute-done.8.sib_ref), custom_call_target="tpu_custom_call" | custom-call | flops 6422528 | bytes 6422528 | tf_op jit(solution)/shard_map/first_product/pallas_call | solution.py:53
  89.2 15.0 %collective-permute-done.7 = f32[2,64,896]{2,1,0:T(8,128)} collective-permute-done((f32[2,64,896]{2,1,0:T(8,128)S(1)}, f32[2,64,896]{2,1,0:T(8,128)}, u32[]{:S(2)}, u32[]{:S(2)}) %collective-permute-start.7) | collective-permute-done | bytes 458784 | tf_op jit(solution)/shard_map/ppermute | solution.py:162
  106.9 22.8 %first_product.5 = f32[2,128,896]{2,1,0:T(8,128)S(1)} custom-call(f32[64,7168]{1,0:T(8,128)} %collective-permute-done.2.near_ref, f32[64,7168]{1,0:T(8,128)} %collective-permute-done.5.far_ref, f32[896,7168]{1,0:T(8,128)} %own_ref.15, f32[896,7168]{1,0:T(8,128)} %collective-permute-done.8.sib_ref), custom_call_target="tpu_custom_call" | custom-call | flops 6422528 | bytes 6422528 | tf_op jit(solution)/shard_map/first_product/pallas_call | solution.py:53
  133.1 6.1 %collective-permute-start.12 = (f32[2,64,896]{2,1,0:T(8,128)S(1)}, f32[2,64,896]{2,1,0:T(8,128)S(1)}, u32[]{:S(2)}, u32[]{:S(2)}) collective-permute-start(f32[2,64,896]{2,1,0:T(8,128)S(1)} %fusion.13), channel_id=1, source_target_pairs={{0,20},{2,22},{4,16},{6,18},{8,28},{10,30},{12,24},{14,26},{17,5},... | collective-permute-start | bytes 1376264 | tf_op jit(solution)/shard_map/ppermute | solution.py:162
  143.3 2.8 collective-permute-done.13.far_ref
  146.2 5.1 %collective-permute-done.14.near_ref = f32[64,7168]{1,0:T(8,128)S(1)} collective-permute-done((f32[64,7168]{1,0:T(8,128)}, f32[64,7168]{1,0:T(8,128)S(1)}, u32[]{:S(2)}, u32[]{:S(2)}) %collective-permute-start.14) | collective-permute-done | bytes 1835040 | tf_op jit(solution)/shard_map/ppermute | solution.py:203
  152.5 22.8 %first_product.6 = f32[2,128,896]{2,1,0:T(8,128)S(1)} custom-call(f32[64,7168]{1,0:T(8,128)} %collective-permute-done.6.near_ref, f32[64,7168]{1,0:T(8,128)} %collective-permute-done.13.far_ref, f32[896,7168]{1,0:T(8,128)} %own_ref.15, f32[896,7168]{1,0:T(8,128)} %collective-permute-done.8.sib_ref), custom_call_target="tpu_custom_call" | custom-call | flops 6422528 | bytes 6422528 | tf_op jit(solution)/shard_map/first_product/pallas_call | solution.py:53
  182.5 23.7 %second_product.4 = (f32[64,7168]{1,0:T(8,128)S(1)}, f32[64,7168]{1,0:T(8,128)S(1)}) custom-call(f32[2,128,896]{2,1,0:T(8,128)S(1)} %add.256.change_ref, f32[896,7168]{1,0:T(8,128)} %own_ref.15, f32[896,7168]{1,0:T(8,128)} %collective-permute-done.8.sib_ref), custom_call_target="tpu_custom_call" | custom-call | flops 6422528 | bytes 6422528 | tf_op jit(solution)/shard_map/second_product/pallas_call | solution.py:91
  208.7 14.2 %collective-permute-start.19 = (f32[2,64,896]{2,1,0:T(8,128)S(1)}, f32[2,64,896]{2,1,0:T(8,128)S(1)}, u32[]{:S(2)}, u32[]{:S(2)}) collective-permute-start(f32[2,64,896]{2,1,0:T(8,128)S(1)} %get-tuple-element.204), channel_id=1, source_target_pairs={{8,0},{10,2},{12,4},{14,6},{17,9},{19,11},{21,13},{23,15},{25,17},... | collective-permute-start | bytes 1376264 | tf_op jit(solution)/shard_map/ppermute | solution.py:194
  225.6 22.3 %first_product.7 = f32[2,128,896]{2,1,0:T(8,128)S(1)} custom-call(f32[64,7168]{1,0:T(8,128)S(1)} %collective-permute-done.14.near_ref, f32[64,7168]{1,0:T(8,128)} %collective-permute-done.21.far_ref, f32[896,7168]{1,0:T(8,128)} %own_ref.15, f32[896,7168]{1,0:T(8,128)} %collective-permute-done.8.sib_ref), custom_call_target="tpu_custom_call" | custom-call | flops 6422528 | bytes 6422528 | tf_op jit(solution)/shard_map/first_product/pallas_call | solution.py:53
  251.1 23.7 %second_product.5 = (f32[64,7168]{1,0:T(8,128)S(1)}, f32[64,7168]{1,0:T(8,128)S(1)}) custom-call(f32[2,128,896]{2,1,0:T(8,128)S(1)} %add.263.change_ref, f32[896,7168]{1,0:T(8,128)} %own_ref.15, f32[896,7168]{1,0:T(8,128)} %collective-permute-done.8.sib_ref), custom_call_target="tpu_custom_call" | custom-call | flops 6422528 | bytes 6422528 | tf_op jit(solution)/shard_map/second_product/pallas_call | solution.py:91
  275.5 2.9 add.266
  283.3 39.7 %collective-permute-done.25 = f32[2,64,896]{2,1,0:T(8,128)S(1)} collective-permute-done((f32[2,64,896]{2,1,0:T(8,128)S(1)}, f32[2,64,896]{2,1,0:T(8,128)S(1)}, u32[]{:S(2)}, u32[]{:S(2)}) %collective-permute-start.25) | collective-permute-done | bytes 458784 | tf_op jit(solution)/shard_map/ppermute | solution.py:194
  323.8 12.0 %collective-permute-start.27 = (f32[2,64,896]{2,1,0:T(8,128)S(1)}, f32[2,64,896]{2,1,0:T(8,128)S(1)}, u32[]{:S(2)}, u32[]{:S(2)}) collective-permute-start(f32[2,64,896]{2,1,0:T(8,128)S(1)} %get-tuple-element.200), channel_id=1, source_target_pairs={{25,1},{27,3},{29,5},{31,7},{0,8},{2,10},{4,12},{6,14},{8,16},{10,... | collective-permute-start | bytes 1376264 | tf_op jit(solution)/shard_map/ppermute | solution.py:194
  336.5 24.6 %second_product.6 = (f32[64,7168]{1,0:T(8,128)S(1)}, f32[64,7168]{1,0:T(8,128)}) custom-call(f32[2,128,896]{2,1,0:T(8,128)S(1)} %add.265.change_ref, f32[896,7168]{1,0:T(8,128)} %own_ref.15, f32[896,7168]{1,0:T(8,128)} %collective-permute-done.8.sib_ref), custom_call_target="tpu_custom_call" | custom-call | flops 6422528 | bytes 6422528 | tf_op jit(solution)/shard_map/second_product/pallas_call | solution.py:91
  364.4 23.7 %second_product.7 = (f32[64,7168]{1,0:T(8,128)S(1)}, f32[64,7168]{1,0:T(8,128)S(1)}) custom-call(f32[2,128,896]{2,1,0:T(8,128)S(1)} %add.254.change_ref, f32[896,7168]{1,0:T(8,128)} %own_ref.15, f32[896,7168]{1,0:T(8,128)} %collective-permute-done.8.sib_ref), custom_call_target="tpu_custom_call" | custom-call | flops 6422528 | bytes 6422528 | tf_op jit(solution)/shard_map/second_product/pallas_call | solution.py:91
  393.7 6.8 %collective-permute-done.31 = f32[64,7168]{1,0:T(8,128)} collective-permute-done((f32[64,7168]{1,0:T(8,128)}, f32[64,7168]{1,0:T(8,128)}, u32[]{:S(2)}, u32[]{:S(2)}) %collective-permute-start.31) | collective-permute-done | bytes 1835040 | tf_op jit(solution)/shard_map/ppermute | solution.py:227
  400.5 6.0 %collective-permute-start.30 = (f32[64,7168]{1,0:T(8,128)}, f32[64,7168]{1,0:T(8,128)S(1)}, u32[]{:S(2)}, u32[]{:S(2)}) collective-permute-start(f32[64,7168]{1,0:T(8,128)} %add_add_fusion.1), channel_id=1, source_target_pairs={{0,8},{2,10},{4,12},{6,14},{8,16},{10,18},{12,20},{14,22},{16,24},... | collective-permute-start | bytes 5505032 | tf_op jit(solution)/shard_map/ppermute | solution.py:236
  411.0 39.1 %collective-permute-done.30 = f32[64,7168]{1,0:T(8,128)S(1)} collective-permute-done((f32[64,7168]{1,0:T(8,128)}, f32[64,7168]{1,0:T(8,128)S(1)}, u32[]{:S(2)}, u32[]{:S(2)}) %collective-permute-start.30) | collective-permute-done | bytes 1835040 | tf_op jit(solution)/shard_map/ppermute | solution.py:236
  453.0 41.2 %collective-permute-done.32 = f32[64,7168]{1,0:T(8,128)S(1)} collective-permute-done((f32[64,7168]{1,0:T(8,128)S(1)}, f32[64,7168]{1,0:T(8,128)S(1)}, u32[]{:S(2)}, u32[]{:S(2)}) %collective-permute-start.32) | collective-permute-done | bytes 1835040 | tf_op jit(solution)/shard_map/ppermute | solution.py:236
  (151 shorter events, 70.2 us)
Async XLA Ops:
  0.6 61.9 %collective-permute-start.8 = (f32[896,7168]{1,0:T(8,128)}, f32[896,7168]{1,0:T(8,128)}, u32[]{:S(2)}, u32[]{:S(2)}) collective-permute-start(f32[896,7168]{1,0:T(8,128)} %own_ref.15), channel_id=1, source_target_pairs={{0,2},{2,0},{4,6},{6,4},{8,10},{10,8},{12,14},{14,12},{16,18},{18,... | collective-permute-start | bytes 77070344 | tf_op jit(solution)/shard_map/ppermute | solution.py:149
  6.1 43.2 %collective-permute-start.1 = (f32[64,7168]{1,0:T(8,128)S(1)}, f32[64,7168]{1,0:T(8,128)S(1)}, u32[]{:S(2)}, u32[]{:S(2)}) collective-permute-start(f32[64,7168]{1,0:T(8,128)S(1)} %get-tuple-element.102.near_ref), channel_id=1, source_target_pairs={{0,4},{2,6},{4,0},{6,2},{8,12},{10,14},{12,8},{14,10},{16,20},{18,... | collective-permute-start | bytes 5505032 | tf_op jit(solution)/shard_map/ppermute | solution.py:169
  8.6 44.1 %collective-permute-start.2 = (f32[64,7168]{1,0:T(8,128)S(1)}, f32[64,7168]{1,0:T(8,128)}, u32[]{:S(2)}, u32[]{:S(2)}) collective-permute-start(f32[64,7168]{1,0:T(8,128)S(1)} %get-tuple-element.102.near_ref), channel_id=1, source_target_pairs={{0,8},{2,10},{4,12},{6,14},{8,16},{10,18},{12,20},{14,22},{16,24},... | collective-permute-start | bytes 5505032 | tf_op jit(solution)/shard_map/ppermute | solution.py:168
  10.2 48.0 %collective-permute-start = (f32[64,7168]{1,0:T(8,128)}, f32[64,7168]{1,0:T(8,128)}, u32[]{:S(2)}, u32[]{:S(2)}) collective-permute-start(f32[64,7168]{1,0:T(8,128)} %get-tuple-element.136), channel_id=1, source_target_pairs={{0,1},{1,0},{2,3},{3,2},{4,5},{5,4},{6,7},{7,6},{8,9},{9,8},{10,11... | collective-permute-start | bytes 5505032 | tf_op jit(solution)/shard_map/ppermute | solution.py:151
  52.7 52.7 %collective-permute-start.5 = (f32[64,7168]{1,0:T(8,128)}, f32[64,7168]{1,0:T(8,128)}, u32[]{:S(2)}, u32[]{:S(2)}) collective-permute-start(f32[64,7168]{1,0:T(8,128)} %collective-permute-done.2.near_ref), channel_id=1, source_target_pairs={{0,4},{2,6},{4,0},{6,2},{8,12},{10,14},{12,8},{14,10},{16,20},{18,... | collective-permute-start | bytes 5505032 | tf_op jit(solution)/shard_map/ppermute | solution.py:201
  53.2 52.1 %collective-permute-start.6 = (f32[64,7168]{1,0:T(8,128)}, f32[64,7168]{1,0:T(8,128)}, u32[]{:S(2)}, u32[]{:S(2)}) collective-permute-start(f32[64,7168]{1,0:T(8,128)} %collective-permute-done.2.near_ref), channel_id=1, source_target_pairs={{0,8},{2,10},{4,12},{6,14},{8,16},{10,18},{12,20},{14,22},{16,24},... | collective-permute-start | bytes 5505032 | tf_op jit(solution)/shard_map/ppermute | solution.py:203
  55.1 49.1 %collective-permute-start.7 = (f32[2,64,896]{2,1,0:T(8,128)S(1)}, f32[2,64,896]{2,1,0:T(8,128)}, u32[]{:S(2)}, u32[]{:S(2)}) collective-permute-start(f32[2,64,896]{2,1,0:T(8,128)S(1)} %fusion.11), channel_id=1, source_target_pairs={{0,4},{2,6},{4,0},{6,2},{8,12},{10,14},{12,8},{14,10},{17,21},{19,... | collective-permute-start | bytes 1376264 | tf_op jit(solution)/shard_map/ppermute | solution.py:162
  60.2 69.5 %collective-permute-start.4 = (f32[2,64,896]{2,1,0:T(8,128)}, f32[2,64,896]{2,1,0:T(8,128)}, u32[]{:S(2)}, u32[]{:S(2)}) collective-permute-start(f32[2,64,896]{2,1,0:T(8,128)} %fusion.8), channel_id=1, source_target_pairs={{1,13},{3,15},{5,9},{7,11},{8,20},{10,22},{12,16},{14,18},{16,28},... | collective-permute-start | bytes 1376264 | tf_op jit(solution)/shard_map/ppermute | solution.py:162
  62.5 67.2 %collective-permute-start.3 = (f32[2,64,896]{2,1,0:T(8,128)}, f32[2,64,896]{2,1,0:T(8,128)}, u32[]{:S(2)}, u32[]{:S(2)}) collective-permute-start(f32[2,64,896]{2,1,0:T(8,128)} %fusion.7), channel_id=1, source_target_pairs={{0,8},{2,10},{4,12},{6,14},{9,17},{11,19},{13,21},{15,23},{17,25},... | collective-permute-start | bytes 1376264 | tf_op jit(solution)/shard_map/ppermute | solution.py:162
  105.3 40.8 %collective-permute-start.13 = (f32[64,7168]{1,0:T(8,128)}, f32[64,7168]{1,0:T(8,128)}, u32[]{:S(2)}, u32[]{:S(2)}) collective-permute-start(f32[64,7168]{1,0:T(8,128)} %collective-permute-done.6.near_ref), channel_id=1, source_target_pairs={{0,4},{2,6},{4,0},{6,2},{8,12},{10,14},{12,8},{14,10},{16,20},{18,... | collective-permute-start | bytes 5505032 | tf_op jit(solution)/shard_map/ppermute | solution.py:201
  106.2 45.1 %collective-permute-start.14 = (f32[64,7168]{1,0:T(8,128)}, f32[64,7168]{1,0:T(8,128)S(1)}, u32[]{:S(2)}, u32[]{:S(2)}) collective-permute-start(f32[64,7168]{1,0:T(8,128)} %collective-permute-done.6.near_ref), channel_id=1, source_target_pairs={{0,8},{2,10},{4,12},{6,14},{8,16},{10,18},{12,20},{14,22},{16,24},... | collective-permute-start | bytes 5505032 | tf_op jit(solution)/shard_map/ppermute | solution.py:203
  133.1 42.2 %collective-permute-start.12 = (f32[2,64,896]{2,1,0:T(8,128)S(1)}, f32[2,64,896]{2,1,0:T(8,128)S(1)}, u32[]{:S(2)}, u32[]{:S(2)}) collective-permute-start(f32[2,64,896]{2,1,0:T(8,128)S(1)} %fusion.13), channel_id=1, source_target_pairs={{0,20},{2,22},{4,16},{6,18},{8,28},{10,30},{12,24},{14,26},{17,5},... | collective-permute-start | bytes 1376264 | tf_op jit(solution)/shard_map/ppermute | solution.py:162
  151.2 73.0 %collective-permute-start.21 = (f32[64,7168]{1,0:T(8,128)S(1)}, f32[64,7168]{1,0:T(8,128)}, u32[]{:S(2)}, u32[]{:S(2)}) collective-permute-start(f32[64,7168]{1,0:T(8,128)S(1)} %collective-permute-done.14.near_ref), channel_id=1, source_target_pairs={{0,4},{2,6},{4,0},{6,2},{8,12},{10,14},{12,8},{14,10},{16,20},{18,... | collective-permute-start | bytes 5505032 | tf_op jit(solution)/shard_map/ppermute | solution.py:201
  179.0 68.9 %collective-permute-start.18 = (f32[2,64,896]{2,1,0:T(8,128)S(1)}, f32[2,64,896]{2,1,0:T(8,128)S(1)}, u32[]{:S(2)}, u32[]{:S(2)}) collective-permute-start(f32[2,64,896]{2,1,0:T(8,128)S(1)} %fusion.15), channel_id=1, source_target_pairs={{0,28},{2,30},{4,24},{6,26},{9,5},{11,7},{13,1},{15,3},{17,13},{19... | collective-permute-start | bytes 1376264 | tf_op jit(solution)/shard_map/ppermute | solution.py:162
  206.2 69.3 %collective-permute-start.15 = (f32[64,7168]{1,0:T(8,128)S(1)}, f32[64,7168]{1,0:T(8,128)}, u32[]{:S(2)}, u32[]{:S(2)}) collective-permute-start(f32[64,7168]{1,0:T(8,128)S(1)} %get-tuple-element.132), channel_id=1, source_target_pairs={{0,4},{2,6},{4,0},{6,2},{8,12},{10,14},{12,8},{14,10},{16,20},{18,... | collective-permute-start | bytes 5505032 | tf_op jit(solution)/shard_map/ppermute | solution.py:227
  208.7 39.2 %collective-permute-start.19 = (f32[2,64,896]{2,1,0:T(8,128)S(1)}, f32[2,64,896]{2,1,0:T(8,128)S(1)}, u32[]{:S(2)}, u32[]{:S(2)}) collective-permute-start(f32[2,64,896]{2,1,0:T(8,128)S(1)} %get-tuple-element.204), channel_id=1, source_target_pairs={{8,0},{10,2},{12,4},{14,6},{17,9},{19,11},{21,13},{23,15},{25,17},... | collective-permute-start | bytes 1376264 | tf_op jit(solution)/shard_map/ppermute | solution.py:194
  274.8 88.1 %collective-permute-start.24 = (f32[64,7168]{1,0:T(8,128)S(1)}, f32[64,7168]{1,0:T(8,128)S(1)}, u32[]{:S(2)}, u32[]{:S(2)}) collective-permute-start(f32[64,7168]{1,0:T(8,128)S(1)} %get-tuple-element.159), channel_id=1, source_target_pairs={{0,4},{2,6},{4,0},{6,2},{8,12},{10,14},{12,8},{14,10},{16,20},{18,... | collective-permute-start | bytes 5505032 | tf_op jit(solution)/shard_map/ppermute | solution.py:227
  278.4 84.4 %collective-permute-start.23 = (f32[64,7168]{1,0:T(8,128)}, f32[64,7168]{1,0:T(8,128)S(1)}, u32[]{:S(2)}, u32[]{:S(2)}) collective-permute-start(f32[64,7168]{1,0:T(8,128)} %add.266), channel_id=1, source_target_pairs={{0,8},{2,10},{4,12},{6,14},{8,16},{10,18},{12,20},{14,22},{16,24},... | collective-permute-start | bytes 5505032 | tf_op jit(solution)/shard_map/ppermute | solution.py:236
  280.5 42.5 %collective-permute-start.25 = (f32[2,64,896]{2,1,0:T(8,128)S(1)}, f32[2,64,896]{2,1,0:T(8,128)S(1)}, u32[]{:S(2)}, u32[]{:S(2)}) collective-permute-start(f32[2,64,896]{2,1,0:T(8,128)S(1)} %get-tuple-element.202), channel_id=1, source_target_pairs={{17,1},{19,3},{21,5},{23,7},{25,9},{27,11},{29,13},{31,15},{0,16},... | collective-permute-start | bytes 1376264 | tf_op jit(solution)/shard_map/ppermute | solution.py:194
  281.8 41.9 %collective-permute-start.26 = (f32[2,64,896]{2,1,0:T(8,128)S(1)}, f32[2,64,896]{2,1,0:T(8,128)}, u32[]{:S(2)}, u32[]{:S(2)}) collective-permute-start(f32[2,64,896]{2,1,0:T(8,128)S(1)} %get-tuple-element.201), channel_id=1, source_target_pairs={{20,1},{22,3},{16,5},{18,7},{28,9},{30,11},{24,13},{26,15},{5,16},... | collective-permute-start | bytes 1376264 | tf_op jit(solution)/shard_map/ppermute | solution.py:194
  361.1 39.4 %collective-permute-start.31 = (f32[64,7168]{1,0:T(8,128)}, f32[64,7168]{1,0:T(8,128)}, u32[]{:S(2)}, u32[]{:S(2)}) collective-permute-start(f32[64,7168]{1,0:T(8,128)} %get-tuple-element.182), channel_id=1, source_target_pairs={{0,4},{2,6},{4,0},{6,2},{8,12},{10,14},{12,8},{14,10},{16,20},{18,... | collective-permute-start | bytes 5505032 | tf_op jit(solution)/shard_map/ppermute | solution.py:227
  400.5 49.7 %collective-permute-start.30 = (f32[64,7168]{1,0:T(8,128)}, f32[64,7168]{1,0:T(8,128)S(1)}, u32[]{:S(2)}, u32[]{:S(2)}) collective-permute-start(f32[64,7168]{1,0:T(8,128)} %add_add_fusion.1), channel_id=1, source_target_pairs={{0,8},{2,10},{4,12},{6,14},{8,16},{10,18},{12,20},{14,22},{16,24},... | collective-permute-start | bytes 5505032 | tf_op jit(solution)/shard_map/ppermute | solution.py:236
  406.6 46.4 %collective-permute-start.33 = (f32[64,7168]{1,0:T(8,128)}, f32[64,7168]{1,0:T(8,128)S(1)}, u32[]{:S(2)}, u32[]{:S(2)}) collective-permute-start(f32[64,7168]{1,0:T(8,128)} %copy-done.4), channel_id=1, source_target_pairs={{0,4},{2,6},{4,0},{6,2},{8,12},{10,14},{12,8},{14,10},{16,20},{18,... | collective-permute-start | bytes 5505032 | tf_op jit(solution)/shard_map/ppermute | solution.py:227
  452.2 42.0 %collective-permute-start.32 = (f32[64,7168]{1,0:T(8,128)S(1)}, f32[64,7168]{1,0:T(8,128)S(1)}, u32[]{:S(2)}, u32[]{:S(2)}) collective-permute-start(f32[64,7168]{1,0:T(8,128)S(1)} %add_add_fusion), channel_id=1, source_target_pairs={{0,8},{2,10},{4,12},{6,14},{8,16},{10,18},{12,20},{14,22},{16,24},... | collective-permute-start | bytes 5505032 | tf_op jit(solution)/shard_map/ppermute | solution.py:236
  (29 other events, 538.2 us)

commit v5 on v3

--- a/solution.py
+++ b/solution.py
@@ -26,34 +26,6 @@
     both = lax.dot_general(left[...], high, dims, preferred_element_type=jnp.float32)
     cross = lax.dot_general(left[:rows], low, dims, preferred_element_type=jnp.float32)
     return both[:rows] + (both[rows:] + cross)
-
-
-def prepare_kernel(dense_ref, iterate_ref, multiplier_ref, mask_ref, change_ref, rest_ref):
-    iterate, multiplier = iterate_ref[...], multiplier_ref[...]
-    projected = mask_ref[...].astype(jnp.float32) * (iterate + multiplier)
-    change_ref[...] = (iterate - dense_ref[...]).T
-    rest_ref[0] = (iterate - step_size * (penalty * (iterate - projected + multiplier)) - dense_ref[...]).T
-
-
-def prepare(dense, iterate, multiplier, mask, blocks):
-    rows, half = dense.shape
-    tile = rows // blocks
-    band = pl.BlockSpec((tile, half), lambda i: (i, 0))
-    return pl.pallas_call(
-        prepare_kernel,
-        grid=(blocks,),
-        in_specs=[band] * 4,
-        out_specs=[
-            pl.BlockSpec((half, tile), lambda i: (0, i)),
-            pl.BlockSpec((1, half, tile), lambda i: (i, 0, 0)),
-        ],
-        out_shape=[
-            jax.ShapeDtypeStruct((half, rows), jnp.float32),
-            jax.ShapeDtypeStruct((blocks, half, tile), jnp.float32),
-        ],
-        compiler_params=pltpu.CompilerParams(vmem_limit_bytes=VMEM_BYTES),
-        name="prepare",
-    )(dense, iterate, multiplier, mask)
 
 
 def first_kernel(near_ref, far_ref, own_ref, sib_ref, out_ref, parts):
@@ -171,16 +143,16 @@
     both = ("row", "col")
     permute = lax.ppermute
 
-    keeping = keep_mask.astype(jnp.float32)
-    change, rest = prepare(dense_weight, start_iterate, start_multiplier, keep_mask, per_plane)
+    dense, begun, dual = dense_weight.T, start_iterate.T, start_multiplier.T
+    keeping = keep_mask.T.astype(jnp.float32)
+    change = begun - dense
     sibling = permute(hessian, "row", to_sibling)
-
+    rest = begun - step_size * (penalty * (begun - keeping * (begun + dual) + dual)) - dense
     def piece(shift, flip):
         turn = cross(shift, flip)
         chip = ((place + shift) % ring) * PAIR + (pair ^ flip)
-        first_chip = ((plane - turn) % planes) * per_plane
-        source = rest_by[turn]
-        part = lax.dynamic_index_in_dim(source, jnp.clip(chip - first_chip, 0, per_plane - 1), 0, keepdims=False)
+        at = jnp.clip(chip - ((plane - turn) % planes) * per_plane, 0, per_plane - 1)
+        part = lax.dynamic_slice_in_dim(rest_by[turn], at * CORES * depth, CORES * depth, 1)
         part = part.reshape(half, CORES, depth)
         part = jnp.where(core == 0, part, part[:, ::-1]).transpose(1, 0, 2)
         if shift == 0 and flip == 0:
@@ -196,7 +168,10 @@
     product, mine, other, changed, kept, sent, swapped, back = {}, {}, {}, {}, {}, {}, {}, {}
     total = None
     start = max(ring, 4)
-    returns = [(0, 0, 5), (0, 1, 4)] + [(g, flip, g + 2 + (g == 1 and flip)) for g in range(1, ring) for flip in range(PAIR)]
+    returns = {group + 2: [(group, 0), (group, 1)] for group in range(2, ring - 1)}
+    returns.setdefault(3, []).append((1, 0))
+    returns.setdefault(start + 1, []).extend([(1, 1), (ring - 1, 0)])
+    returns.setdefault(start + 2, []).extend([(ring - 1, 1), (0, 0), (0, 1)])
     for window in range(start + ring):
         fresh = []
 
@@ -213,9 +188,8 @@
         elif window < ring:
             for flip in range(PAIR):
                 added[window, flip] = piece(window, flip)
-        if window == 1:
-            for flip in range(PAIR):
-                put(added, (0, flip), piece(0, flip))
+                if window == ring - 1:
+                    fresh.append((added, (window, flip)))
         closing = window - start + 1
         if closing >= 1:
             if total is not None:
@@ -224,27 +198,28 @@
         group = window - 2
         if 1 <= group < ring:
             put(changed, group, mine[group] + other[group])
-        if group == 1:
+        if window == start:
+            for flip in range(PAIR):
+                put(added, (0, flip), piece(0, flip))
+        if window == start + 1:
+            put(mine, 0, product[0] + jnp.concatenate([added[0, 0], added[0, 1]], axis=1))
+            put(other, 0, sum_planes(mine[0]))
+        if window == start + 2:
             put(changed, 0, mine[0] + other[0])
         group = window - 1
         if 0 <= group < ring:
             put(product, group, first(near[group], far[group], hessian, sibling))
-        for group in (0, 1) if window == 2 else (window - 1,) if 2 < window <= ring else ():
-            put(mine, group, product[group] + jnp.concatenate([added[group, 0], added[group, 1]], axis=1))
-            put(other, group, sum_planes(mine[group]))
-        group = window - 2
-        if window == start + ring - 2:
-            group = 0
-        if (1 <= group < ring) or window == start + ring - 2:
+            if group:
+                put(mine, group, product[group] + jnp.concatenate([added[group, 0], added[group, 1]], axis=1))
+                put(other, group, sum_planes(mine[group]))
+        group = 0 if window == start + ring - 2 else window - 2
+        if 1 <= group < ring or window == start + ring - 2:
             keep, send = second(changed[group], hessian, sibling)
             put(kept, group, keep)
             put(sent, group, send)
-        for group, flip, when in returns:
-            if when == window:
-                part = changed[group][:, flip * half : (flip + 1) * half]
-                if group or flip:
-                    part = permute(part, both, route_back(group, flip))
-                put(back, (group, flip), part)
+        for group, flip in returns.get(window, []):
+            rows = changed[group][:, flip * half : (flip + 1) * half]
+            put(back, (group, flip), permute(rows, both, route_back(group, flip)) if group or flip else rows)
         values = [where[key] for where, key in fresh]
         values, sibling, total, rest_by[0] = lax.optimization_barrier((values, sibling, total, rest_by[0]))
         for (where, key), value in zip(fresh, values):
@@ -252,23 +227,24 @@
         if closing >= 1:
             part = kept[closing % ring] + swapped[closing % ring]
             total = part if total is None else total + part
+    gradient = total
 
     back = jnp.stack([back[shift, flip] for shift in range(ring) for flip in range(PAIR)])
     blocks = []
     for block in range(per_plane):
         chip = plane * per_plane + block
         slot = ((chip // PAIR - place) % ring) * PAIR + ((chip % PAIR) ^ pair)
-        blocks.append(lax.dynamic_index_in_dim(back, slot, 0, keepdims=False))
-    blocks = jnp.stack(blocks)
-    blocks = jnp.where(core == 0, blocks, blocks[:, ::-1])
-    iterate = blocks.transpose(0, 1, 3, 2).reshape(columns, half) + dense_weight
-
-    projected = keeping * (iterate + start_multiplier)
-    multiplier = start_multiplier + iterate - projected
-    iterate = iterate - step_size * (total.T + penalty * (iterate - projected + multiplier))
+        part = lax.dynamic_index_in_dim(back, slot, 0, keepdims=False)
+        part = jnp.where(core == 0, part, part[::-1])
+        blocks += [part[0], part[1]]
+    iterate = jnp.concatenate(blocks, axis=1) + dense
+
+    projected = keeping * (iterate + dual)
+    multiplier = dual + iterate - projected
+    iterate = iterate - step_size * (gradient + penalty * (iterate - projected + multiplier))
     projected = keeping * (iterate + multiplier)
     multiplier = multiplier + iterate - projected
-    return (iterate, projected, multiplier)
+    return (iterate.T, projected.T, multiplier.T)
 
 
 def solution(mesh):

time: 443 us -> 485 us (1.095)
  waiting for transfers between devices: 103 us -> 172 us
  local copies, waits for them, and re-layouts: 42.1 us -> 6.74 us
  starting transfers between devices: 71.5 us -> 99.3 us
  Pallas kernels: 195 us -> 184 us
  other arithmetic: 28.7 us -> 19.9 us
    ppermute x7, waiting for transfers between devices: 21.7 us -> 60.3 us  [per_device(): permute(rows, both, route_back(group, flip))]
    ppermute x4, waiting for transfers between devices: 1.8 us -> 33.5 us  [per_device(): put(swapped, closing % ring, permute(sent[closing % ring], 'row', to_pair))]
    ppermute x4, starting transfers between devices: 5.23 us -> 26.3 us  [per_device(): put(swapped, closing % ring, permute(sent[closing % ring], 'row', to_pair))]
    ppermute x3, waiting for transfers between devices: 25.8 us -> 5.54 us  [per_device(): total = permute(total, 'row', to_next)]
    unnamed x57 -> x50, local copies, waits for them, and re-layouts: 18.2 us -> 4.29 us
    reshape x16 -> x8, local copies, waits for them, and re-layouts: 12.5 us -> 0.25 us  [piece(): part = part.reshape(half, CORES, depth)]
    ppermute x4, waiting for transfers between devices: 1.68 us -> 13.7 us  [per_device(): put(far, window, permute(near[window], 'row', to_pair))]
    ppermute x7, starting transfers between devices: 26.6 us -> 37.6 us  [per_device(): permute(rows, both, route_back(group, flip))]
  transfers between devices with their start and end apart: 34 -> 34, of which waited for: 10 -> 11; matrix products, arithmetic and copies ran while one was open for 12% -> 4% of each run, Pallas kernels for 44% -> 38%
where the time goes in v5:
time: 485 us; the launch traced here: 484 us
  Pallas kernels  184 us (38%)
  waiting for transfers between devices  172 us (35%)
  starting transfers between devices  99.3 us (20%)
  other arithmetic  19.9 us (4%)
  local copies, waits for them, and re-layouts  6.74 us (1%)
    pallas_call x4, Pallas kernels, second(): pl.pallas_call(second_kernel, grid=(columns // tile,), in_specs=[pl.Block...  95.6 us
    pallas_call x4, Pallas kernels, first(): pl.pallas_call(first_kernel, grid=(rows // tile,), in_specs=[whole, whole...  88.7 us
    ppermute x7, waiting for transfers between devices, per_device(): permute(rows, both, route_back(group, flip))  60.3 us
    ppermute x1, waiting for transfers between devices, per_device(): permute(rest, 'col', [(y, (y + 1) % planes) for y in range(planes)])  37.6 us
    ppermute x7, starting transfers between devices, per_device(): permute(rows, both, route_back(group, flip))  37.6 us
    ppermute x4, waiting for transfers between devices, per_device(): put(swapped, closing % ring, permute(sent[closing % ring], 'row', to_pair))  33.5 us
    ppermute x4, starting transfers between devices, per_device(): put(swapped, closing % ring, permute(sent[closing % ring], 'row', to_pair))  26.3 us
    ppermute x7, starting transfers between devices, piece(): return permute(part, both, route(shift, flip))  17.5 us
  transfers between devices with their start and end apart: 34, of which 11 were waited for; matrix products, arithmetic and copies ran while one was open for 4% of the time, Pallas kernels for 38%

profile of v5, /device:TPU:0, one launch (start us, length us, event | category | flops | bytes accessed | tf_op | source)
XLA Modules:
  0.0 484.2 jit_solution(3360624292929552817)
XLA Ops:
  1.1 3.7 fusion.4
  10.5 37.6 %collective-permute-done.2 = f32[64,7168]{1,0:T(8,128)S(1)} collective-permute-done((f32[64,7168]{1,0:T(8,128)S(1)}, f32[64,7168]{1,0:T(8,128)S(1)}, u32[]{:S(2)}, u32[]{:S(2)}) %collective-permute-start.2) | collective-permute-done | bytes 1835040 | tf_op jit(solution)/shard_map/ppermute | solution.py:187
  55.8 3.6 collective-permute-start.8
  60.2 21.8 %first_product.4 = f32[2,128,896]{2,1,0:T(8,128)S(1)} custom-call(f32[64,7168]{1,0:T(8,128)S(1)} %get-tuple-element.138.near_ref, f32[64,7168]{1,0:T(8,128)S(1)} %copy-done.1, f32[896,7168]{1,0:T(8,128)} %own_ref.15, f32[896,7168]{1,0:T(8,128)} %collective-permute-done.3.sib_ref), custom_call_target="tpu_custom_call" | custom-call | flops 9865003008 | bytes 51380224 | tf_op jit(solution)/shard_map/first_product/pallas_call | solution.py:53
  82.0 12.2 %collective-permute-done.5.far_ref = f32[64,7168]{1,0:T(8,128)} collective-permute-done((f32[64,7168]{1,0:T(8,128)}, f32[64,7168]{1,0:T(8,128)}, u32[]{:S(2)}, u32[]{:S(2)}) %collective-permute-start.5) | collective-permute-done | bytes 1835040 | tf_op jit(solution)/shard_map/ppermute | solution.py:185
  94.2 4.2 collective-permute-done.4.near_ref
  99.9 22.8 %first_product.5 = f32[2,128,896]{2,1,0:T(8,128)S(1)} custom-call(f32[64,7168]{1,0:T(8,128)} %collective-permute-done.near_ref, f32[64,7168]{1,0:T(8,128)} %collective-permute-done.5.far_ref, f32[896,7168]{1,0:T(8,128)} %own_ref.15, f32[896,7168]{1,0:T(8,128)} %collective-permute-done.3.sib_ref), custom_call_target="tpu_custom_call" | custom-call | flops 9865003008 | bytes 51380224 | tf_op jit(solution)/shard_map/first_product/pallas_call | solution.py:53
  123.5 5.7 %collective-permute-start.13 = (f32[2,64,896]{2,1,0:T(8,128)S(1)}, f32[2,64,896]{2,1,0:T(8,128)S(1)}, u32[]{:S(2)}, u32[]{:S(2)}) collective-permute-start(f32[2,64,896]{2,1,0:T(8,128)S(1)} %fusion.11), channel_id=1, source_target_pairs={{0,28},{2,30},{4,24},{6,26},{9,5},{11,7},{13,1},{15,3},{17,13},{19... | collective-permute-start | bytes 1376264 | tf_op jit(solution)/shard_map/ppermute | solution.py:160
  130.7 10.0 %collective-permute-done.10 = f32[2,128,896]{2,1,0:T(8,128)S(1)} collective-permute-done((f32[2,128,896]{2,1,0:T(8,128)S(1)}, f32[2,128,896]{2,1,0:T(8,128)S(1)}, u32[]{:S(2)}, u32[]{:S(2)}) %collective-permute-start.10) | collective-permute-done | bytes 917536 | tf_op jit(solution)/shard_map/ppermute | solution.py:163
  142.0 5.5 %collective-permute-done.6.near_ref = f32[64,7168]{1,0:T(8,128)S(1)} collective-permute-done((f32[64,7168]{1,0:T(8,128)}, f32[64,7168]{1,0:T(8,128)S(1)}, u32[]{:S(2)}, u32[]{:S(2)}) %collective-permute-start.6) | collective-permute-done | bytes 1835040 | tf_op jit(solution)/shard_map/ppermute | solution.py:183
  147.7 10.9 %collective-permute-start.17 = (f32[2,64,896]{2,1,0:T(8,128)S(1)}, f32[2,64,896]{2,1,0:T(8,128)S(1)}, u32[]{:S(2)}, u32[]{:S(2)}) collective-permute-start(f32[2,64,896]{2,1,0:T(8,128)S(1)} %slice.64), channel_id=1, source_target_pairs={{8,0},{10,2},{12,4},{14,6},{17,9},{19,11},{21,13},{23,15},{25,17},... | collective-permute-start | bytes 1376264 | tf_op jit(solution)/shard_map/ppermute | solution.py:222
  159.2 22.3 %first_product.6 = f32[2,128,896]{2,1,0:T(8,128)S(1)} custom-call(f32[64,7168]{1,0:T(8,128)} %collective-permute-done.4.near_ref, f32[64,7168]{1,0:T(8,128)S(1)} %collective-permute-done.7.far_ref, f32[896,7168]{1,0:T(8,128)} %own_ref.15, f32[896,7168]{1,0:T(8,128)} %collective-permute-done.3.sib_ref), custom_call_target="tpu_custom_call" | custom-call | flops 9865003008 | bytes 51380224 | tf_op jit(solution)/shard_map/first_product/pallas_call | solution.py:53
  184.2 3.6 collective-permute-start.16
  187.8 23.7 %second_product.4 = (f32[64,7168]{1,0:T(8,128)S(1)}, f32[64,7168]{1,0:T(8,128)S(1)}) custom-call(f32[2,128,896]{2,1,0:T(8,128)S(1)} %add.248.change_ref, f32[896,7168]{1,0:T(8,128)} %own_ref.15, f32[896,7168]{1,0:T(8,128)} %collective-permute-done.3.sib_ref), custom_call_target="tpu_custom_call" | custom-call | flops 9865003008 | bytes 51380224 | tf_op jit(solution)/shard_map/second_product/pallas_call | solution.py:91
  217.5 17.8 %collective-permute-start.21 = (f32[2,64,896]{2,1,0:T(8,128)S(1)}, f32[2,64,896]{2,1,0:T(8,128)}, u32[]{:S(2)}, u32[]{:S(2)}) collective-permute-start(f32[2,64,896]{2,1,0:T(8,128)S(1)} %get-tuple-element.147), channel_id=1, source_target_pairs={{17,1},{19,3},{21,5},{23,7},{25,9},{27,11},{29,13},{31,15},{0,16},... | collective-permute-start | bytes 1376264 | tf_op jit(solution)/shard_map/ppermute | solution.py:222
  236.8 21.8 %first_product.7 = f32[2,128,896]{2,1,0:T(8,128)S(1)} custom-call(f32[64,7168]{1,0:T(8,128)S(1)} %collective-permute-done.6.near_ref, f32[64,7168]{1,0:T(8,128)S(1)} %collective-permute-done.11.far_ref, f32[896,7168]{1,0:T(8,128)} %own_ref.15, f32[896,7168]{1,0:T(8,128)} %collective-permute-done.3.sib_ref), custom_call_target="tpu_custom_call" | custom-call | flops 9865003008 | bytes 51380224 | tf_op jit(solution)/shard_map/first_product/pallas_call | solution.py:53
  258.8 23.7 %second_product.5 = (f32[64,7168]{1,0:T(8,128)S(1)}, f32[64,7168]{1,0:T(8,128)S(1)}) custom-call(f32[2,128,896]{2,1,0:T(8,128)S(1)} %add.256.change_ref, f32[896,7168]{1,0:T(8,128)} %own_ref.15, f32[896,7168]{1,0:T(8,128)} %collective-permute-done.3.sib_ref), custom_call_target="tpu_custom_call" | custom-call | flops 9865003008 | bytes 51380224 | tf_op jit(solution)/shard_map/second_product/pallas_call | solution.py:91
  296.7 24.6 %second_product.6 = (f32[64,7168]{1,0:T(8,128)S(1)}, f32[64,7168]{1,0:T(8,128)}) custom-call(f32[2,128,896]{2,1,0:T(8,128)S(1)} %add.263.change_ref, f32[896,7168]{1,0:T(8,128)} %own_ref.15, f32[896,7168]{1,0:T(8,128)} %collective-permute-done.3.sib_ref), custom_call_target="tpu_custom_call" | custom-call | flops 9865003008 | bytes 51380224 | tf_op jit(solution)/shard_map/second_product/pallas_call | solution.py:91
  321.3 30.1 %collective-permute-done.25 = f32[2,64,896]{2,1,0:T(8,128)S(1)} collective-permute-done((f32[2,64,896]{2,1,0:T(8,128)S(1)}, f32[2,64,896]{2,1,0:T(8,128)S(1)}, u32[]{:S(2)}, u32[]{:S(2)}) %collective-permute-start.25) | collective-permute-done | bytes 458784 | tf_op jit(solution)/shard_map/ppermute | solution.py:222
  351.4 21.4 %collective-permute-start.28 = (f32[64,7168]{1,0:T(8,128)}, f32[64,7168]{1,0:T(8,128)}, u32[]{:S(2)}, u32[]{:S(2)}) collective-permute-start(f32[64,7168]{1,0:T(8,128)} %get-tuple-element.106), channel_id=1, source_target_pairs={{0,4},{2,6},{4,0},{6,2},{8,12},{10,14},{12,8},{14,10},{16,20},{18,... | collective-permute-start | bytes 5505032 | tf_op jit(solution)/shard_map/ppermute | solution.py:197
  379.0 23.7 %second_product.7 = (f32[64,7168]{1,0:T(8,128)S(1)}, f32[64,7168]{1,0:T(8,128)S(1)}) custom-call(f32[2,128,896]{2,1,0:T(8,128)S(1)} %add.266.change_ref, f32[896,7168]{1,0:T(8,128)} %own_ref.15, f32[896,7168]{1,0:T(8,128)} %collective-permute-done.3.sib_ref), custom_call_target="tpu_custom_call" | custom-call | flops 9865003008 | bytes 51380224 | tf_op jit(solution)/shard_map/second_product/pallas_call | solution.py:91
  402.7 30.2 %collective-permute-done.30 = f32[2,64,896]{2,1,0:T(8,128)S(1)} collective-permute-done((f32[2,64,896]{2,1,0:T(8,128)S(1)}, f32[2,64,896]{2,1,0:T(8,128)S(1)}, u32[]{:S(2)}, u32[]{:S(2)}) %collective-permute-start.30) | collective-permute-done | bytes 458784 | tf_op jit(solution)/shard_map/ppermute | solution.py:222
  440.8 33.5 %collective-permute-done.32 = f32[64,7168]{1,0:T(8,128)S(1)} collective-permute-done((f32[64,7168]{1,0:T(8,128)S(1)}, f32[64,7168]{1,0:T(8,128)S(1)}, u32[]{:S(2)}, u32[]{:S(2)}) %collective-permute-start.32) | collective-permute-done | bytes 1835040 | tf_op jit(solution)/shard_map/ppermute | solution.py:197
  474.3 5.5 %collective-permute-done.33 = f32[64,7168]{1,0:T(8,128)S(1)} collective-permute-done((f32[64,7168]{1,0:T(8,128)S(1)}, f32[64,7168]{1,0:T(8,128)S(1)}, u32[]{:S(2)}, u32[]{:S(2)}) %collective-permute-start.33) | collective-permute-done | bytes 1835040 | tf_op jit(solution)/shard_map/ppermute | solution.py:196
  (149 shorter events, 62.7 us)
Async XLA Ops:
  0.6 52.1 %collective-permute-start.3 = (f32[896,7168]{1,0:T(8,128)}, f32[896,7168]{1,0:T(8,128)}, u32[]{:S(2)}, u32[]{:S(2)}) collective-permute-start(f32[896,7168]{1,0:T(8,128)} %own_ref.15), channel_id=1, source_target_pairs={{0,2},{2,0},{4,6},{6,4},{8,10},{10,8},{12,14},{14,12},{16,18},{18,... | collective-permute-start | bytes 77070344 | tf_op jit(solution)/shard_map/ppermute | solution.py:149
  4.9 43.3 %collective-permute-start.2 = (f32[64,7168]{1,0:T(8,128)S(1)}, f32[64,7168]{1,0:T(8,128)S(1)}, u32[]{:S(2)}, u32[]{:S(2)}) collective-permute-start(f32[64,7168]{1,0:T(8,128)S(1)} %get-tuple-element.87), channel_id=1, source_target_pairs={{0,1},{1,0},{2,3},{3,2},{4,5},{5,4},{6,7},{7,6},{8,9},{9,8},{10,11... | collective-permute-start | bytes 5505032 | tf_op jit(solution)/shard_map/ppermute | solution.py:187
  8.9 43.8 %collective-permute-start = (f32[64,7168]{1,0:T(8,128)S(1)}, f32[64,7168]{1,0:T(8,128)}, u32[]{:S(2)}, u32[]{:S(2)}) collective-permute-start(f32[64,7168]{1,0:T(8,128)S(1)} %get-tuple-element.138.near_ref), channel_id=1, source_target_pairs={{0,8},{2,10},{4,12},{6,14},{8,16},{10,18},{12,20},{14,22},{16,24},... | collective-permute-start | bytes 5505032 | tf_op jit(solution)/shard_map/ppermute | solution.py:183
  53.4 45.1 %collective-permute-start.4 = (f32[64,7168]{1,0:T(8,128)}, f32[64,7168]{1,0:T(8,128)}, u32[]{:S(2)}, u32[]{:S(2)}) collective-permute-start(f32[64,7168]{1,0:T(8,128)} %collective-permute-done.near_ref), channel_id=1, source_target_pairs={{0,8},{2,10},{4,12},{6,14},{8,16},{10,18},{12,20},{14,22},{16,24},... | collective-permute-start | bytes 5505032 | tf_op jit(solution)/shard_map/ppermute | solution.py:183
  55.8 67.0 %collective-permute-start.8 = (f32[2,64,896]{2,1,0:T(8,128)S(1)}, f32[2,64,896]{2,1,0:T(8,128)S(1)}, u32[]{:S(2)}, u32[]{:S(2)}) collective-permute-start(f32[2,64,896]{2,1,0:T(8,128)S(1)} %fusion.8), channel_id=1, source_target_pairs={{0,8},{2,10},{4,12},{6,14},{9,17},{11,19},{13,21},{15,23},{17,25},... | collective-permute-start | bytes 1376264 | tf_op jit(solution)/shard_map/ppermute | solution.py:160
  59.5 63.3 %collective-permute-start.9 = (f32[2,64,896]{2,1,0:T(8,128)S(1)}, f32[2,64,896]{2,1,0:T(8,128)S(1)}, u32[]{:S(2)}, u32[]{:S(2)}) collective-permute-start(f32[2,64,896]{2,1,0:T(8,128)S(1)} %fusion.9), channel_id=1, source_target_pairs={{1,13},{3,15},{5,9},{7,11},{8,20},{10,22},{12,16},{14,18},{16,28},... | collective-permute-start | bytes 1376264 | tf_op jit(solution)/shard_map/ppermute | solution.py:160
  98.4 43.5 %collective-permute-start.7 = (f32[64,7168]{1,0:T(8,128)}, f32[64,7168]{1,0:T(8,128)S(1)}, u32[]{:S(2)}, u32[]{:S(2)}) collective-permute-start(f32[64,7168]{1,0:T(8,128)} %collective-permute-done.4.near_ref), channel_id=1, source_target_pairs={{0,4},{2,6},{4,0},{6,2},{8,12},{10,14},{12,8},{14,10},{16,20},{18,... | collective-permute-start | bytes 5505032 | tf_op jit(solution)/shard_map/ppermute | solution.py:185
  99.9 47.6 %collective-permute-start.6 = (f32[64,7168]{1,0:T(8,128)}, f32[64,7168]{1,0:T(8,128)S(1)}, u32[]{:S(2)}, u32[]{:S(2)}) collective-permute-start(f32[64,7168]{1,0:T(8,128)} %collective-permute-done.4.near_ref), channel_id=1, source_target_pairs={{0,8},{2,10},{4,12},{6,14},{8,16},{10,18},{12,20},{14,22},{16,24},... | collective-permute-start | bytes 5505032 | tf_op jit(solution)/shard_map/ppermute | solution.py:183
  123.5 88.0 %collective-permute-start.13 = (f32[2,64,896]{2,1,0:T(8,128)S(1)}, f32[2,64,896]{2,1,0:T(8,128)S(1)}, u32[]{:S(2)}, u32[]{:S(2)}) collective-permute-start(f32[2,64,896]{2,1,0:T(8,128)S(1)} %fusion.11), channel_id=1, source_target_pairs={{0,28},{2,30},{4,24},{6,26},{9,5},{11,7},{13,1},{15,3},{17,13},{19... | collective-permute-start | bytes 1376264 | tf_op jit(solution)/shard_map/ppermute | solution.py:160
  129.3 52.3 %collective-permute-start.15 = (f32[2,64,896]{2,1,0:T(8,128)S(1)}, f32[2,64,896]{2,1,0:T(8,128)S(1)}, u32[]{:S(2)}, u32[]{:S(2)}) collective-permute-start(f32[2,64,896]{2,1,0:T(8,128)S(1)} %fusion.13), channel_id=1, source_target_pairs={{0,20},{2,22},{4,16},{6,18},{8,28},{10,30},{12,24},{14,26},{17,5},... | collective-permute-start | bytes 1376264 | tf_op jit(solution)/shard_map/ppermute | solution.py:160
  147.7 63.8 %collective-permute-start.17 = (f32[2,64,896]{2,1,0:T(8,128)S(1)}, f32[2,64,896]{2,1,0:T(8,128)S(1)}, u32[]{:S(2)}, u32[]{:S(2)}) collective-permute-start(f32[2,64,896]{2,1,0:T(8,128)S(1)} %slice.64), channel_id=1, source_target_pairs={{8,0},{10,2},{12,4},{14,6},{17,9},{19,11},{21,13},{23,15},{25,17},... | collective-permute-start | bytes 1376264 | tf_op jit(solution)/shard_map/ppermute | solution.py:222
  158.6 53.0 %collective-permute-start.11 = (f32[64,7168]{1,0:T(8,128)S(1)}, f32[64,7168]{1,0:T(8,128)S(1)}, u32[]{:S(2)}, u32[]{:S(2)}) collective-permute-start(f32[64,7168]{1,0:T(8,128)S(1)} %collective-permute-done.6.near_ref), channel_id=1, source_target_pairs={{0,4},{2,6},{4,0},{6,2},{8,12},{10,14},{12,8},{14,10},{16,20},{18,... | collective-permute-start | bytes 5505032 | tf_op jit(solution)/shard_map/ppermute | solution.py:185
  212.5 70.1 %collective-permute-start.19 = (f32[2,64,896]{2,1,0:T(8,128)}, f32[2,64,896]{2,1,0:T(8,128)}, u32[]{:S(2)}, u32[]{:S(2)}) collective-permute-start(f32[2,64,896]{2,1,0:T(8,128)} %fusion.16), channel_id=1, source_target_pairs={{0,4},{2,6},{4,0},{6,2},{8,12},{10,14},{12,8},{14,10},{17,21},{19,... | collective-permute-start | bytes 1376264 | tf_op jit(solution)/shard_map/ppermute | solution.py:160
  216.1 66.6 %collective-permute-start.22 = (f32[2,64,896]{2,1,0:T(8,128)S(1)}, f32[2,64,896]{2,1,0:T(8,128)}, u32[]{:S(2)}, u32[]{:S(2)}) collective-permute-start(f32[2,64,896]{2,1,0:T(8,128)S(1)} %get-tuple-element.146), channel_id=1, source_target_pairs={{20,1},{22,3},{16,5},{18,7},{28,9},{30,11},{24,13},{26,15},{5,16},... | collective-permute-start | bytes 1376264 | tf_op jit(solution)/shard_map/ppermute | solution.py:222
  217.5 65.1 %collective-permute-start.21 = (f32[2,64,896]{2,1,0:T(8,128)S(1)}, f32[2,64,896]{2,1,0:T(8,128)}, u32[]{:S(2)}, u32[]{:S(2)}) collective-permute-start(f32[2,64,896]{2,1,0:T(8,128)S(1)} %get-tuple-element.147), channel_id=1, source_target_pairs={{17,1},{19,3},{21,5},{23,7},{25,9},{27,11},{29,13},{31,15},{0,16},... | collective-permute-start | bytes 1376264 | tf_op jit(solution)/shard_map/ppermute | solution.py:222
  235.3 47.4 %collective-permute-start.18 = (f32[64,7168]{1,0:T(8,128)S(1)}, f32[64,7168]{1,0:T(8,128)S(1)}, u32[]{:S(2)}, u32[]{:S(2)}) collective-permute-start(f32[64,7168]{1,0:T(8,128)S(1)} %get-tuple-element.84), channel_id=1, source_target_pairs={{0,4},{2,6},{4,0},{6,2},{8,12},{10,14},{12,8},{14,10},{16,20},{18,... | collective-permute-start | bytes 5505032 | tf_op jit(solution)/shard_map/ppermute | solution.py:197
  282.7 68.8 %collective-permute-start.23 = (f32[64,7168]{1,0:T(8,128)S(1)}, f32[64,7168]{1,0:T(8,128)S(1)}, u32[]{:S(2)}, u32[]{:S(2)}) collective-permute-start(f32[64,7168]{1,0:T(8,128)S(1)} %get-tuple-element.94), channel_id=1, source_target_pairs={{0,4},{2,6},{4,0},{6,2},{8,12},{10,14},{12,8},{14,10},{16,20},{18,... | collective-permute-start | bytes 5505032 | tf_op jit(solution)/shard_map/ppermute | solution.py:197
  285.7 65.7 %collective-permute-start.27 = (f32[64,7168]{1,0:T(8,128)}, f32[64,7168]{1,0:T(8,128)S(1)}, u32[]{:S(2)}, u32[]{:S(2)}) collective-permute-start(f32[64,7168]{1,0:T(8,128)} %add.265), channel_id=1, source_target_pairs={{0,8},{2,10},{4,12},{6,14},{8,16},{10,18},{12,20},{14,22},{16,24},... | collective-permute-start | bytes 5505032 | tf_op jit(solution)/shard_map/ppermute | solution.py:196
  288.5 62.9 %collective-permute-start.25 = (f32[2,64,896]{2,1,0:T(8,128)S(1)}, f32[2,64,896]{2,1,0:T(8,128)S(1)}, u32[]{:S(2)}, u32[]{:S(2)}) collective-permute-start(f32[2,64,896]{2,1,0:T(8,128)S(1)} %slice.51), channel_id=1, source_target_pairs={{13,0},{15,2},{9,4},{11,6},{20,9},{22,11},{16,13},{18,15},{28,17},... | collective-permute-start | bytes 1376264 | tf_op jit(solution)/shard_map/ppermute | solution.py:222
  291.1 60.3 %collective-permute-start.26 = (f32[2,64,896]{2,1,0:T(8,128)S(1)}, f32[2,64,896]{2,1,0:T(8,128)S(1)}, u32[]{:S(2)}, u32[]{:S(2)}) collective-permute-start(f32[2,64,896]{2,1,0:T(8,128)S(1)} %slice.67), channel_id=1, source_target_pairs={{25,1},{27,3},{29,5},{31,7},{0,8},{2,10},{4,12},{6,14},{8,16},{10,... | collective-permute-start | bytes 1376264 | tf_op jit(solution)/shard_map/ppermute | solution.py:222
  295.6 55.8 %collective-permute-start.24 = (f32[2,128,896]{2,1,0:T(8,128)S(1)}, f32[2,128,896]{2,1,0:T(8,128)S(1)}, u32[]{:S(2)}, u32[]{:S(2)}) collective-permute-start(f32[2,128,896]{2,1,0:T(8,128)S(1)} %maximum_add_fusion.3), channel_id=1, source_target_pairs={{0,1},{1,0},{2,3},{3,2},{4,5},{5,4},{6,7},{7,6},{8,9},{9,8},{10,11... | collective-permute-start | bytes 2752520 | tf_op jit(solution)/shard_map/ppermute | solution.py:163
  351.4 81.5 %collective-permute-start.28 = (f32[64,7168]{1,0:T(8,128)}, f32[64,7168]{1,0:T(8,128)}, u32[]{:S(2)}, u32[]{:S(2)}) collective-permute-start(f32[64,7168]{1,0:T(8,128)} %get-tuple-element.106), channel_id=1, source_target_pairs={{0,4},{2,6},{4,0},{6,2},{8,12},{10,14},{12,8},{14,10},{16,20},{18,... | collective-permute-start | bytes 5505032 | tf_op jit(solution)/shard_map/ppermute | solution.py:197
  374.3 58.6 %collective-permute-start.31 = (f32[64,7168]{1,0:T(8,128)}, f32[64,7168]{1,0:T(8,128)}, u32[]{:S(2)}, u32[]{:S(2)}) collective-permute-start(f32[64,7168]{1,0:T(8,128)} %add_add_fusion.1), channel_id=1, source_target_pairs={{0,8},{2,10},{4,12},{6,14},{8,16},{10,18},{12,20},{14,22},{16,24},... | collective-permute-start | bytes 5505032 | tf_op jit(solution)/shard_map/ppermute | solution.py:196
  376.9 56.0 %collective-permute-start.30 = (f32[2,64,896]{2,1,0:T(8,128)S(1)}, f32[2,64,896]{2,1,0:T(8,128)S(1)}, u32[]{:S(2)}, u32[]{:S(2)}) collective-permute-start(f32[2,64,896]{2,1,0:T(8,128)S(1)} %get-tuple-element.144), channel_id=1, source_target_pairs={{4,0},{6,2},{0,4},{2,6},{12,8},{14,10},{8,12},{10,14},{21,17},{23,... | collective-permute-start | bytes 1376264 | tf_op jit(solution)/shard_map/ppermute | solution.py:222
  (28 other events, 666.8 us)

commit v6 on v5

--- a/solution.py
+++ b/solution.py
@@ -168,10 +168,10 @@
     product, mine, other, changed, kept, sent, swapped, back = {}, {}, {}, {}, {}, {}, {}, {}
     total = None
     start = max(ring, 4)
-    returns = {group + 2: [(group, 0), (group, 1)] for group in range(2, ring - 1)}
+    returns = {group + 2: [(group, 0), (group, 1)] for group in range(2, ring)}
     returns.setdefault(3, []).append((1, 0))
-    returns.setdefault(start + 1, []).extend([(1, 1), (ring - 1, 0)])
-    returns.setdefault(start + 2, []).extend([(ring - 1, 1), (0, 0), (0, 1)])
+    returns.setdefault(4, []).append((1, 1))
+    returns.setdefault(start + 2, []).extend([(0, 0), (0, 1)])
     for window in range(start + ring):
         fresh = []
 
@@ -184,12 +184,14 @@
         if window < ring:
             put(far, window, permute(near[window], "row", to_pair))
         if window == 0:
-            put(rest_by, 1, permute(rest, "col", [(y, (y + 1) % planes) for y in range(planes)]))
+            rest_by[1] = (permute(rest, "col", [(y, (y + 1) % planes) for y in range(planes)]))
         elif window < ring:
             for flip in range(PAIR):
                 added[window, flip] = piece(window, flip)
                 if window == ring - 1:
                     fresh.append((added, (window, flip)))
+                if window == 1:
+                    added[0, flip] = piece(0, flip)
         closing = window - start + 1
         if closing >= 1:
             if total is not None:
@@ -198,9 +200,8 @@
         group = window - 2
         if 1 <= group < ring:
             put(changed, group, mine[group] + other[group])
-        if window == start:
-            for flip in range(PAIR):
-                put(added, (0, flip), piece(0, flip))
+        if window == 2:
+            fresh += [(added, (0, flip)) for flip in range(PAIR)]
         if window == start + 1:
             put(mine, 0, product[0] + jnp.concatenate([added[0, 0], added[0, 1]], axis=1))
             put(other, 0, sum_planes(mine[0]))
@@ -221,7 +222,7 @@
             rows = changed[group][:, flip * half : (flip + 1) * half]
             put(back, (group, flip), permute(rows, both, route_back(group, flip)) if group or flip else rows)
         values = [where[key] for where, key in fresh]
-        values, sibling, total, rest_by[0] = lax.optimization_barrier((values, sibling, total, rest_by[0]))
+        values, sibling, total, rest_by = lax.optimization_barrier((values, sibling, total, rest_by))
         for (where, key), value in zip(fresh, values):
             where[key] = value
         if closing >= 1:

time: 485 us -> 424 us (0.87)
  waiting for transfers between devices: 172 us -> 114 us
  starting transfers between devices: 99.3 us -> 92.3 us
    ppermute x7, waiting for transfers between devices: 60.3 us -> 23.4 us  [per_device(): permute(rows, both, route_back(group, flip))]
    ppermute x4, starting transfers between devices: 26.3 us -> 6.18 us  [per_device(): put(swapped, closing % ring, permute(sent[closing % ring], 'row', to_pair))]
    ppermute x4, waiting for transfers between devices: 33.5 us -> 19.9 us  [per_device(): put(swapped, closing % ring, permute(sent[closing % ring], 'row', to_pair))]
    ppermute x4, starting transfers between devices: 5.36 us -> 13.4 us  [sum_planes(): permute(part, 'col', [(y, (y + turn) % planes) for y in range(planes)])]
  transfers between devices with their start and end apart: 34 -> 34, of which waited for: 11 -> 13; matrix products, arithmetic and copies ran while one was open for 4% -> 5% of each run, Pallas kernels for 38% -> 44%
where the time goes in v6:
time: 424 us; the launch traced here: 422 us
  Pallas kernels  184 us (43%)
  waiting for transfers between devices  114 us (27%)
  starting transfers between devices  92.3 us (22%)
  other arithmetic  19 us (4%)
  local copies, waits for them, and re-layouts  10.8 us (3%)
    pallas_call x4, Pallas kernels, second(): pl.pallas_call(second_kernel, grid=(columns // tile,), in_specs=[pl.Block...  95.7 us
    pallas_call x4, Pallas kernels, first(): pl.pallas_call(first_kernel, grid=(rows // tile,), in_specs=[whole, whole...  88.1 us
    ppermute x1, waiting for transfers between devices, per_device(): permute(rest, 'col', [(y, (y + 1) % planes) for y in range(planes)])  37.9 us
    ppermute x7, starting transfers between devices, per_device(): permute(rows, both, route_back(group, flip))  37.4 us
    ppermute x7, waiting for transfers between devices, per_device(): permute(rows, both, route_back(group, flip))  23.4 us
    ppermute x7, starting transfers between devices, piece(): return permute(part, both, route(shift, flip))  20.1 us
    ppermute x4, waiting for transfers between devices, per_device(): put(swapped, closing % ring, permute(sent[closing % ring], 'row', to_pair))  19.9 us
    ppermute x4, starting transfers between devices, sum_planes(): permute(part, 'col', [(y, (y + turn) % planes) for y in range(planes)])  13.4 us
  transfers between devices with their start and end apart: 34, of which 13 were waited for; matrix products, arithmetic and copies ran while one was open for 5% of the time, Pallas kernels for 44%

profile of v6, /device:TPU:0, one launch (start us, length us, event | category | flops | bytes accessed | tf_op | source)
XLA Modules:
  0.0 421.8 jit_solution(6856076991854919138)
XLA Ops:
  1.1 4.9 %fusion.4 = (f32[64,7168]{1,0:T(8,128)}, f32[64,7168]{1,0:T(8,128)S(1)}) fusion(f32[7168,64]{0,1:T(8,128)} %param.8, f32[7168,64]{0,1:T(8,128)} %param.6, f32[7168,64]{0,1:T(8,128)} %param.7, s32[7168,64]{0,1:T(8,128)} %param.9), kind=kLoop, calls=%fused_computation.7 | loop fusion | flops 4128768 | bytes 11010048 | tf_op jit(solution)/shard_map/sub | solution.py:150
  11.7 37.9 %collective-permute-done.3 = f32[64,7168]{1,0:T(8,128)} collective-permute-done((f32[64,7168]{1,0:T(8,128)}, f32[64,7168]{1,0:T(8,128)}, u32[]{:S(2)}, u32[]{:S(2)}) %collective-permute-start.3) | collective-permute-done | bytes 1835040 | tf_op jit(solution)/shard_map/ppermute | solution.py:187
  57.0 3.4 collective-permute-start.8
  60.4 6.0 %collective-permute-start.9 = (f32[2,64,896]{2,1,0:T(8,128)S(1)}, f32[2,64,896]{2,1,0:T(8,128)}, u32[]{:S(2)}, u32[]{:S(2)}) collective-permute-start(f32[2,64,896]{2,1,0:T(8,128)S(1)} %fusion.11), channel_id=1, source_target_pairs={{0,8},{2,10},{4,12},{6,14},{9,17},{11,19},{13,21},{15,23},{17,25},... | collective-permute-start | bytes 1376264 | tf_op jit(solution)/shard_map/ppermute | solution.py:160
  66.5 22.3 %first_product.4 = f32[2,128,896]{2,1,0:T(8,128)S(1)} custom-call(f32[64,7168]{1,0:T(8,128)S(1)} %get-tuple-element.138.near_ref, f32[64,7168]{1,0:T(8,128)} %collective-permute-done.1.far_ref, f32[896,7168]{1,0:T(8,128)} %own_ref.15, f32[896,7168]{1,0:T(8,128)} %collective-permute-done.2.sib_ref), custom_call_target="tpu_custom_call" | custom-call | flops 9865003008 | bytes 51380224 | tf_op jit(solution)/shard_map/first_product/pallas_call | solution.py:53
  88.8 8.3 %collective-permute-done.5.far_ref = f32[64,7168]{1,0:T(8,128)S(1)} collective-permute-done((f32[64,7168]{1,0:T(8,128)}, f32[64,7168]{1,0:T(8,128)S(1)}, u32[]{:S(2)}, u32[]{:S(2)}) %collective-permute-start.5) | collective-permute-done | bytes 1835040 | tf_op jit(solution)/shard_map/ppermute | solution.py:185
  102.4 22.3 %first_product.5 = f32[2,128,896]{2,1,0:T(8,128)S(1)} custom-call(f32[64,7168]{1,0:T(8,128)} %collective-permute-done.near_ref, f32[64,7168]{1,0:T(8,128)S(1)} %copy-done.1, f32[896,7168]{1,0:T(8,128)} %own_ref.15, f32[896,7168]{1,0:T(8,128)} %collective-permute-done.2.sib_ref), custom_call_target="tpu_custom_call" | custom-call | flops 9865003008 | bytes 51380224 | tf_op jit(solution)/shard_map/first_product/pallas_call | solution.py:53
  129.2 5.5 %collective-permute-start.16 = (f32[2,64,896]{2,1,0:T(8,128)S(1)}, f32[2,64,896]{2,1,0:T(8,128)S(1)}, u32[]{:S(2)}, u32[]{:S(2)}) collective-permute-start(f32[2,64,896]{2,1,0:T(8,128)S(1)} %fusion.16), channel_id=1, source_target_pairs={{0,20},{2,22},{4,16},{6,18},{8,28},{10,30},{12,24},{14,26},{17,5},... | collective-permute-start | bytes 1376264 | tf_op jit(solution)/shard_map/ppermute | solution.py:160
  134.6 9.0 %collective-permute-done.11 = f32[2,128,896]{2,1,0:T(8,128)S(1)} collective-permute-done((f32[2,128,896]{2,1,0:T(8,128)S(1)}, f32[2,128,896]{2,1,0:T(8,128)S(1)}, u32[]{:S(2)}, u32[]{:S(2)}) %collective-permute-start.11) | collective-permute-done | bytes 917536 | tf_op jit(solution)/shard_map/ppermute | solution.py:163
  144.3 4.3 %collective-permute-done.6.near_ref = f32[64,7168]{1,0:T(8,128)S(1)} collective-permute-done((f32[64,7168]{1,0:T(8,128)S(1)}, f32[64,7168]{1,0:T(8,128)S(1)}, u32[]{:S(2)}, u32[]{:S(2)}) %collective-permute-start.6) | collective-permute-done | bytes 1835040 | tf_op jit(solution)/shard_map/ppermute | solution.py:183
  154.8 21.8 %first_product.6 = f32[2,128,896]{2,1,0:T(8,128)S(1)} custom-call(f32[64,7168]{1,0:T(8,128)S(1)} %collective-permute-done.4.near_ref, f32[64,7168]{1,0:T(8,128)S(1)} %collective-permute-done.7.far_ref, f32[896,7168]{1,0:T(8,128)} %own_ref.15, f32[896,7168]{1,0:T(8,128)} %collective-permute-done.2.sib_ref), custom_call_target="tpu_custom_call" | custom-call | flops 9865003008 | bytes 51380224 | tf_op jit(solution)/shard_map/first_product/pallas_call | solution.py:53
  179.3 10.7 %collective-permute-start.17 = (f32[2,128,896]{2,1,0:T(8,128)S(1)}, f32[2,128,896]{2,1,0:T(8,128)S(1)}, u32[]{:S(2)}, u32[]{:S(2)}) collective-permute-start(f32[2,128,896]{2,1,0:T(8,128)S(1)} %maximum_add_fusion.1), channel_id=1, source_target_pairs={{0,1},{1,0},{2,3},{3,2},{4,5},{5,4},{6,7},{7,6},{8,9},{9,8},{10,11... | collective-permute-start | bytes 2752520 | tf_op jit(solution)/shard_map/ppermute | solution.py:163
  190.0 23.7 %second_product.4 = (f32[64,7168]{1,0:T(8,128)S(1)}, f32[64,7168]{1,0:T(8,128)S(1)}) custom-call(f32[2,128,896]{2,1,0:T(8,128)S(1)} %add.253.change_ref, f32[896,7168]{1,0:T(8,128)} %own_ref.15, f32[896,7168]{1,0:T(8,128)} %collective-permute-done.2.sib_ref), custom_call_target="tpu_custom_call" | custom-call | flops 9865003008 | bytes 51380224 | tf_op jit(solution)/shard_map/second_product/pallas_call | solution.py:91
  216.9 26.4 %collective-permute-start.21 = (f32[2,64,896]{2,1,0:T(8,128)S(1)}, f32[2,64,896]{2,1,0:T(8,128)S(1)}, u32[]{:S(2)}, u32[]{:S(2)}) collective-permute-start(f32[2,64,896]{2,1,0:T(8,128)S(1)} %get-tuple-element.147), channel_id=1, source_target_pairs={{17,1},{19,3},{21,5},{23,7},{25,9},{27,11},{29,13},{31,15},{0,16},... | collective-permute-start | bytes 1376264 | tf_op jit(solution)/shard_map/ppermute | solution.py:223
  244.9 21.8 %first_product.7 = f32[2,128,896]{2,1,0:T(8,128)S(1)} custom-call(f32[64,7168]{1,0:T(8,128)S(1)} %collective-permute-done.6.near_ref, f32[64,7168]{1,0:T(8,128)S(1)} %collective-permute-done.12.far_ref, f32[896,7168]{1,0:T(8,128)} %own_ref.15, f32[896,7168]{1,0:T(8,128)} %collective-permute-done.2.sib_ref), custom_call_target="tpu_custom_call" | custom-call | flops 9865003008 | bytes 51380224 | tf_op jit(solution)/shard_map/first_product/pallas_call | solution.py:53
  268.0 23.7 %second_product.5 = (f32[64,7168]{1,0:T(8,128)S(1)}, f32[64,7168]{1,0:T(8,128)S(1)}) custom-call(f32[2,128,896]{2,1,0:T(8,128)S(1)} %add.261.change_ref, f32[896,7168]{1,0:T(8,128)} %own_ref.15, f32[896,7168]{1,0:T(8,128)} %collective-permute-done.2.sib_ref), custom_call_target="tpu_custom_call" | custom-call | flops 9865003008 | bytes 51380224 | tf_op jit(solution)/shard_map/second_product/pallas_call | solution.py:91
  299.3 24.6 %second_product.6 = (f32[64,7168]{1,0:T(8,128)S(1)}, f32[64,7168]{1,0:T(8,128)}) custom-call(f32[2,128,896]{2,1,0:T(8,128)S(1)} %add.263.change_ref, f32[896,7168]{1,0:T(8,128)} %own_ref.15, f32[896,7168]{1,0:T(8,128)} %collective-permute-done.2.sib_ref), custom_call_target="tpu_custom_call" | custom-call | flops 9865003008 | bytes 51380224 | tf_op jit(solution)/shard_map/second_product/pallas_call | solution.py:91
  324.0 9.1 %collective-permute-done.26 = f32[2,64,896]{2,1,0:T(8,128)S(1)} collective-permute-done((f32[2,64,896]{2,1,0:T(8,128)S(1)}, f32[2,64,896]{2,1,0:T(8,128)S(1)}, u32[]{:S(2)}, u32[]{:S(2)}) %collective-permute-start.26) | collective-permute-done | bytes 458784 | tf_op jit(solution)/shard_map/ppermute | solution.py:223
  340.5 5.0 %collective-permute-start.31 = (f32[64,7168]{1,0:T(8,128)}, f32[64,7168]{1,0:T(8,128)}, u32[]{:S(2)}, u32[]{:S(2)}) collective-permute-start(f32[64,7168]{1,0:T(8,128)} %add_add_fusion.1), channel_id=1, source_target_pairs={{0,8},{2,10},{4,12},{6,14},{8,16},{10,18},{12,20},{14,22},{16,24},... | collective-permute-start | bytes 5505032 | tf_op jit(solution)/shard_map/ppermute | solution.py:198
  346.8 3.9 collective-permute-start.30
  350.8 23.7 %second_product.7 = (f32[64,7168]{1,0:T(8,128)S(1)}, f32[64,7168]{1,0:T(8,128)S(1)}) custom-call(f32[2,128,896]{2,1,0:T(8,128)S(1)} %add.266.change_ref, f32[896,7168]{1,0:T(8,128)} %own_ref.15, f32[896,7168]{1,0:T(8,128)} %collective-permute-done.2.sib_ref), custom_call_target="tpu_custom_call" | custom-call | flops 9865003008 | bytes 51380224 | tf_op jit(solution)/shard_map/second_product/pallas_call | solution.py:91
  374.5 14.3 %collective-permute-done.30 = f32[2,64,896]{2,1,0:T(8,128)S(1)} collective-permute-done((f32[2,64,896]{2,1,0:T(8,128)S(1)}, f32[2,64,896]{2,1,0:T(8,128)S(1)}, u32[]{:S(2)}, u32[]{:S(2)}) %collective-permute-start.30) | collective-permute-done | bytes 458784 | tf_op jit(solution)/shard_map/ppermute | solution.py:223
  394.9 17.0 %collective-permute-done.32 = f32[64,7168]{1,0:T(8,128)S(1)} collective-permute-done((f32[64,7168]{1,0:T(8,128)S(1)}, f32[64,7168]{1,0:T(8,128)S(1)}, u32[]{:S(2)}, u32[]{:S(2)}) %collective-permute-start.32) | collective-permute-done | bytes 1835040 | tf_op jit(solution)/shard_map/ppermute | solution.py:199
  411.9 5.5 %collective-permute-done.33 = f32[64,7168]{1,0:T(8,128)S(1)} collective-permute-done((f32[64,7168]{1,0:T(8,128)S(1)}, f32[64,7168]{1,0:T(8,128)S(1)}, u32[]{:S(2)}, u32[]{:S(2)}) %collective-permute-start.33) | collective-permute-done | bytes 1835040 | tf_op jit(solution)/shard_map/ppermute | solution.py:198
  (154 shorter events, 65.2 us)
Async XLA Ops:
  0.6 53.3 %collective-permute-start.2 = (f32[896,7168]{1,0:T(8,128)}, f32[896,7168]{1,0:T(8,128)}, u32[]{:S(2)}, u32[]{:S(2)}) collective-permute-start(f32[896,7168]{1,0:T(8,128)} %own_ref.15), channel_id=1, source_target_pairs={{0,2},{2,0},{4,6},{6,4},{8,10},{10,8},{12,14},{14,12},{16,18},{18,... | collective-permute-start | bytes 77070344 | tf_op jit(solution)/shard_map/ppermute | solution.py:149
  6.1 43.5 %collective-permute-start.3 = (f32[64,7168]{1,0:T(8,128)}, f32[64,7168]{1,0:T(8,128)}, u32[]{:S(2)}, u32[]{:S(2)}) collective-permute-start(f32[64,7168]{1,0:T(8,128)} %get-tuple-element.78), channel_id=1, source_target_pairs={{0,1},{1,0},{2,3},{3,2},{4,5},{5,4},{6,7},{7,6},{8,9},{9,8},{10,11... | collective-permute-start | bytes 5505032 | tf_op jit(solution)/shard_map/ppermute | solution.py:187
  8.6 42.2 %collective-permute-start.1 = (f32[64,7168]{1,0:T(8,128)S(1)}, f32[64,7168]{1,0:T(8,128)}, u32[]{:S(2)}, u32[]{:S(2)}) collective-permute-start(f32[64,7168]{1,0:T(8,128)S(1)} %get-tuple-element.138.near_ref), channel_id=1, source_target_pairs={{0,4},{2,6},{4,0},{6,2},{8,12},{10,14},{12,8},{14,10},{16,20},{18,... | collective-permute-start | bytes 5505032 | tf_op jit(solution)/shard_map/ppermute | solution.py:185
  10.1 43.8 %collective-permute-start = (f32[64,7168]{1,0:T(8,128)S(1)}, f32[64,7168]{1,0:T(8,128)}, u32[]{:S(2)}, u32[]{:S(2)}) collective-permute-start(f32[64,7168]{1,0:T(8,128)S(1)} %get-tuple-element.138.near_ref), channel_id=1, source_target_pairs={{0,8},{2,10},{4,12},{6,14},{8,16},{10,18},{12,20},{14,22},{16,24},... | collective-permute-start | bytes 5505032 | tf_op jit(solution)/shard_map/ppermute | solution.py:183
  53.9 43.2 %collective-permute-start.5 = (f32[64,7168]{1,0:T(8,128)}, f32[64,7168]{1,0:T(8,128)S(1)}, u32[]{:S(2)}, u32[]{:S(2)}) collective-permute-start(f32[64,7168]{1,0:T(8,128)} %collective-permute-done.near_ref), channel_id=1, source_target_pairs={{0,4},{2,6},{4,0},{6,2},{8,12},{10,14},{12,8},{14,10},{16,20},{18,... | collective-permute-start | bytes 5505032 | tf_op jit(solution)/shard_map/ppermute | solution.py:185
  54.4 45.0 %collective-permute-start.4 = (f32[64,7168]{1,0:T(8,128)}, f32[64,7168]{1,0:T(8,128)S(1)}, u32[]{:S(2)}, u32[]{:S(2)}) collective-permute-start(f32[64,7168]{1,0:T(8,128)} %collective-permute-done.near_ref), channel_id=1, source_target_pairs={{0,8},{2,10},{4,12},{6,14},{8,16},{10,18},{12,20},{14,22},{16,24},... | collective-permute-start | bytes 5505032 | tf_op jit(solution)/shard_map/ppermute | solution.py:183
  56.3 68.4 %collective-permute-start.10 = (f32[2,64,896]{2,1,0:T(8,128)S(1)}, f32[2,64,896]{2,1,0:T(8,128)S(1)}, u32[]{:S(2)}, u32[]{:S(2)}) collective-permute-start(f32[2,64,896]{2,1,0:T(8,128)S(1)} %fusion.12), channel_id=1, source_target_pairs={{1,13},{3,15},{5,9},{7,11},{8,20},{10,22},{12,16},{14,18},{16,28},... | collective-permute-start | bytes 1376264 | tf_op jit(solution)/shard_map/ppermute | solution.py:160
  57.0 72.1 %collective-permute-start.8 = (f32[2,64,896]{2,1,0:T(8,128)S(1)}, f32[2,64,896]{2,1,0:T(8,128)S(1)}, u32[]{:S(2)}, u32[]{:S(2)}) collective-permute-start(f32[2,64,896]{2,1,0:T(8,128)S(1)} %fusion.10), channel_id=1, source_target_pairs={{0,4},{2,6},{4,0},{6,2},{8,12},{10,14},{12,8},{14,10},{17,21},{19,... | collective-permute-start | bytes 1376264 | tf_op jit(solution)/shard_map/ppermute | solution.py:160
  60.4 64.3 %collective-permute-start.9 = (f32[2,64,896]{2,1,0:T(8,128)S(1)}, f32[2,64,896]{2,1,0:T(8,128)}, u32[]{:S(2)}, u32[]{:S(2)}) collective-permute-start(f32[2,64,896]{2,1,0:T(8,128)S(1)} %fusion.11), channel_id=1, source_target_pairs={{0,8},{2,10},{4,12},{6,14},{9,17},{11,19},{13,21},{15,23},{17,25},... | collective-permute-start | bytes 1376264 | tf_op jit(solution)/shard_map/ppermute | solution.py:160
  99.4 44.9 %collective-permute-start.7 = (f32[64,7168]{1,0:T(8,128)S(1)}, f32[64,7168]{1,0:T(8,128)S(1)}, u32[]{:S(2)}, u32[]{:S(2)}) collective-permute-start(f32[64,7168]{1,0:T(8,128)S(1)} %collective-permute-done.4.near_ref), channel_id=1, source_target_pairs={{0,4},{2,6},{4,0},{6,2},{8,12},{10,14},{12,8},{14,10},{16,20},{18,... | collective-permute-start | bytes 5505032 | tf_op jit(solution)/shard_map/ppermute | solution.py:185
  100.9 47.8 %collective-permute-start.6 = (f32[64,7168]{1,0:T(8,128)S(1)}, f32[64,7168]{1,0:T(8,128)S(1)}, u32[]{:S(2)}, u32[]{:S(2)}) collective-permute-start(f32[64,7168]{1,0:T(8,128)S(1)} %collective-permute-done.4.near_ref), channel_id=1, source_target_pairs={{0,8},{2,10},{4,12},{6,14},{8,16},{10,18},{12,20},{14,22},{16,24},... | collective-permute-start | bytes 5505032 | tf_op jit(solution)/shard_map/ppermute | solution.py:183
  127.8 49.9 %collective-permute-start.15 = (f32[2,64,896]{2,1,0:T(8,128)S(1)}, f32[2,64,896]{2,1,0:T(8,128)S(1)}, u32[]{:S(2)}, u32[]{:S(2)}) collective-permute-start(f32[2,64,896]{2,1,0:T(8,128)S(1)} %fusion.15), channel_id=1, source_target_pairs={{1,17},{3,19},{5,21},{7,23},{9,25},{11,27},{13,29},{15,31},{16,0},... | collective-permute-start | bytes 1376264 | tf_op jit(solution)/shard_map/ppermute | solution.py:160
  129.2 50.0 %collective-permute-start.16 = (f32[2,64,896]{2,1,0:T(8,128)S(1)}, f32[2,64,896]{2,1,0:T(8,128)S(1)}, u32[]{:S(2)}, u32[]{:S(2)}) collective-permute-start(f32[2,64,896]{2,1,0:T(8,128)S(1)} %fusion.16), channel_id=1, source_target_pairs={{0,20},{2,22},{4,16},{6,18},{8,28},{10,30},{12,24},{14,26},{17,5},... | collective-permute-start | bytes 1376264 | tf_op jit(solution)/shard_map/ppermute | solution.py:160
  150.0 63.7 %collective-permute-start.18 = (f32[2,64,896]{2,1,0:T(8,128)S(1)}, f32[2,64,896]{2,1,0:T(8,128)S(1)}, u32[]{:S(2)}, u32[]{:S(2)}) collective-permute-start(f32[2,64,896]{2,1,0:T(8,128)S(1)} %slice.64), channel_id=1, source_target_pairs={{8,0},{10,2},{12,4},{14,6},{17,9},{19,11},{21,13},{23,15},{25,17},... | collective-permute-start | bytes 1376264 | tf_op jit(solution)/shard_map/ppermute | solution.py:223
  151.9 61.8 %collective-permute-start.14 = (f32[2,64,896]{2,1,0:T(8,128)S(1)}, f32[2,64,896]{2,1,0:T(8,128)S(1)}, u32[]{:S(2)}, u32[]{:S(2)}) collective-permute-start(f32[2,64,896]{2,1,0:T(8,128)S(1)} %fusion.14), channel_id=1, source_target_pairs={{0,28},{2,30},{4,24},{6,26},{9,5},{11,7},{13,1},{15,3},{17,13},{19... | collective-permute-start | bytes 1376264 | tf_op jit(solution)/shard_map/ppermute | solution.py:160
  153.6 60.1 %collective-permute-start.12 = (f32[64,7168]{1,0:T(8,128)S(1)}, f32[64,7168]{1,0:T(8,128)S(1)}, u32[]{:S(2)}, u32[]{:S(2)}) collective-permute-start(f32[64,7168]{1,0:T(8,128)S(1)} %collective-permute-done.6.near_ref), channel_id=1, source_target_pairs={{0,4},{2,6},{4,0},{6,2},{8,12},{10,14},{12,8},{14,10},{16,20},{18,... | collective-permute-start | bytes 5505032 | tf_op jit(solution)/shard_map/ppermute | solution.py:185
  214.7 77.0 %collective-permute-start.23 = (f32[2,64,896]{2,1,0:T(8,128)}, f32[2,64,896]{2,1,0:T(8,128)S(1)}, u32[]{:S(2)}, u32[]{:S(2)}) collective-permute-start(f32[2,64,896]{2,1,0:T(8,128)} %slice.51), channel_id=1, source_target_pairs={{13,0},{15,2},{9,4},{11,6},{20,9},{22,11},{16,13},{18,15},{28,17},... | collective-permute-start | bytes 1376264 | tf_op jit(solution)/shard_map/ppermute | solution.py:223
  216.2 75.5 %collective-permute-start.22 = (f32[2,64,896]{2,1,0:T(8,128)S(1)}, f32[2,64,896]{2,1,0:T(8,128)S(1)}, u32[]{:S(2)}, u32[]{:S(2)}) collective-permute-start(f32[2,64,896]{2,1,0:T(8,128)S(1)} %get-tuple-element.146), channel_id=1, source_target_pairs={{20,1},{22,3},{16,5},{18,7},{28,9},{30,11},{24,13},{26,15},{5,16},... | collective-permute-start | bytes 1376264 | tf_op jit(solution)/shard_map/ppermute | solution.py:223
  216.9 74.9 %collective-permute-start.21 = (f32[2,64,896]{2,1,0:T(8,128)S(1)}, f32[2,64,896]{2,1,0:T(8,128)S(1)}, u32[]{:S(2)}, u32[]{:S(2)}) collective-permute-start(f32[2,64,896]{2,1,0:T(8,128)S(1)} %get-tuple-element.147), channel_id=1, source_target_pairs={{17,1},{19,3},{21,5},{23,7},{25,9},{27,11},{29,13},{31,15},{0,16},... | collective-permute-start | bytes 1376264 | tf_op jit(solution)/shard_map/ppermute | solution.py:223
  243.3 48.4 %collective-permute-start.19 = (f32[64,7168]{1,0:T(8,128)S(1)}, f32[64,7168]{1,0:T(8,128)S(1)}, u32[]{:S(2)}, u32[]{:S(2)}) collective-permute-start(f32[64,7168]{1,0:T(8,128)S(1)} %get-tuple-element.86), channel_id=1, source_target_pairs={{0,4},{2,6},{4,0},{6,2},{8,12},{10,14},{12,8},{14,10},{16,20},{18,... | collective-permute-start | bytes 5505032 | tf_op jit(solution)/shard_map/ppermute | solution.py:199
  291.8 44.2 %collective-permute-start.24 = (f32[64,7168]{1,0:T(8,128)S(1)}, f32[64,7168]{1,0:T(8,128)S(1)}, u32[]{:S(2)}, u32[]{:S(2)}) collective-permute-start(f32[64,7168]{1,0:T(8,128)S(1)} %get-tuple-element.96), channel_id=1, source_target_pairs={{0,4},{2,6},{4,0},{6,2},{8,12},{10,14},{12,8},{14,10},{16,20},{18,... | collective-permute-start | bytes 5505032 | tf_op jit(solution)/shard_map/ppermute | solution.py:199
  293.8 42.2 %collective-permute-start.28 = (f32[64,7168]{1,0:T(8,128)}, f32[64,7168]{1,0:T(8,128)S(1)}, u32[]{:S(2)}, u32[]{:S(2)}) collective-permute-start(f32[64,7168]{1,0:T(8,128)} %add.265), channel_id=1, source_target_pairs={{0,8},{2,10},{4,12},{6,14},{8,16},{10,18},{12,20},{14,22},{16,24},... | collective-permute-start | bytes 5505032 | tf_op jit(solution)/shard_map/ppermute | solution.py:198
  336.0 52.7 %collective-permute-start.29 = (f32[64,7168]{1,0:T(8,128)}, f32[64,7168]{1,0:T(8,128)}, u32[]{:S(2)}, u32[]{:S(2)}) collective-permute-start(f32[64,7168]{1,0:T(8,128)} %get-tuple-element.107), channel_id=1, source_target_pairs={{0,4},{2,6},{4,0},{6,2},{8,12},{10,14},{12,8},{14,10},{16,20},{18,... | collective-permute-start | bytes 5505032 | tf_op jit(solution)/shard_map/ppermute | solution.py:199
  340.5 48.3 %collective-permute-start.31 = (f32[64,7168]{1,0:T(8,128)}, f32[64,7168]{1,0:T(8,128)}, u32[]{:S(2)}, u32[]{:S(2)}) collective-permute-start(f32[64,7168]{1,0:T(8,128)} %add_add_fusion.1), channel_id=1, source_target_pairs={{0,8},{2,10},{4,12},{6,14},{8,16},{10,18},{12,20},{14,22},{16,24},... | collective-permute-start | bytes 5505032 | tf_op jit(solution)/shard_map/ppermute | solution.py:198
  (31 other events, 476.2 us)

commit v7 on v6

--- a/solution.py
+++ b/solution.py
@@ -168,10 +168,8 @@
     product, mine, other, changed, kept, sent, swapped, back = {}, {}, {}, {}, {}, {}, {}, {}
     total = None
     start = max(ring, 4)
-    returns = {group + 2: [(group, 0), (group, 1)] for group in range(2, ring)}
-    returns.setdefault(3, []).append((1, 0))
-    returns.setdefault(4, []).append((1, 1))
-    returns.setdefault(start + 2, []).extend([(0, 0), (0, 1)])
+    returns = {group + 2: [(group, 0), (group, 1)] for group in range(1, ring)}
+    returns.setdefault(start + ring - 2, []).extend([(0, 0), (0, 1)])
     for window in range(start + ring):
         fresh = []
 
@@ -185,37 +183,36 @@
             put(far, window, permute(near[window], "row", to_pair))
         if window == 0:
             rest_by[1] = (permute(rest, "col", [(y, (y + 1) % planes) for y in range(planes)]))
-        elif window < ring:
+        for group in (0, 1) if window == 1 else (window - 1,) if 2 < window <= ring else ():
             for flip in range(PAIR):
-                added[window, flip] = piece(window, flip)
-                if window == ring - 1:
-                    fresh.append((added, (window, flip)))
-                if window == 1:
-                    added[0, flip] = piece(0, flip)
+                added[group, flip] = piece(group, flip)
+        if window == 2:
+            fresh += [(added, (0, flip)) for flip in range(PAIR)]
         closing = window - start + 1
         if closing >= 1:
             if total is not None:
                 total = permute(total, "row", to_next)
             put(swapped, closing % ring, permute(sent[closing % ring], "row", to_pair))
-        group = window - 2
-        if 1 <= group < ring:
-            put(changed, group, mine[group] + other[group])
-        if window == 2:
-            fresh += [(added, (0, flip)) for flip in range(PAIR)]
-        if window == start + 1:
-            put(mine, 0, product[0] + jnp.concatenate([added[0, 0], added[0, 1]], axis=1))
-            put(other, 0, sum_planes(mine[0]))
-        if window == start + 2:
-            put(changed, 0, mine[0] + other[0])
+        def join(group):
+            put(mine, group, product[group] + jnp.concatenate([added[group, 0], added[group, 1]], axis=1))
+            other[group] = sum_planes(mine[group])
+
         group = window - 1
         if 0 <= group < ring:
             put(product, group, first(near[group], far[group], hessian, sibling))
-            if group:
-                put(mine, group, product[group] + jnp.concatenate([added[group, 0], added[group, 1]], axis=1))
-                put(other, group, sum_planes(mine[group]))
+            if group in (1, ring - 1):
+                join(group)
+        if window == start + 1:
+            join(0)
         group = 0 if window == start + ring - 2 else window - 2
         if 1 <= group < ring or window == start + ring - 2:
+            if 2 <= group < ring - 1:
+                product[group + 1], other[group] = lax.optimization_barrier((product[group + 1], other[group]))
+            put(changed, group, mine[group] + other[group])
             keep, send = second(changed[group], hessian, sibling)
+            if 2 <= window - 1 < ring - 1:
+                keep, product[window - 1] = lax.optimization_barrier((keep, product[window - 1]))
+                join(window - 1)
             put(kept, group, keep)
             put(sent, group, send)
         for group, flip in returns.get(window, []):

time: 424 us -> 438 us (1.033)
  waiting for transfers between devices: 114 us -> 162 us
  starting transfers between devices: 92.3 us -> 61 us
    ppermute x7, waiting for transfers between devices: 0.02 us -> 21.5 us  [piece(): return permute(part, both, route(shift, flip))]
    ppermute x7, starting transfers between devices: 37.4 us -> 18.9 us  [per_device(): permute(rows, both, route_back(group, flip))]
    ppermute x4, waiting for transfers between devices: 19.9 us -> 31.6 us  [per_device(): put(swapped, closing % ring, permute(sent[closing % ring], 'row', to_pair))]
    ppermute x4, starting transfers between devices: 13.4 us -> 2.29 us  [sum_planes(): permute(part, 'col', [(y, (y + turn) % planes) for y in range(planes)])]
    ppermute x7, waiting for transfers between devices: 23.4 us -> 34.3 us  [per_device(): permute(rows, both, route_back(group, flip))]
    ppermute x4, waiting for transfers between devices: 10.2 us -> 16.8 us  [per_device(): put(far, window, permute(near[window], 'row', to_pair))]
    ppermute x3, starting transfers between devices: 5.9 us -> 10.5 us  [per_device(): total = permute(total, 'row', to_next)]
    ppermute x3, waiting for transfers between devices: 8.5 us -> 4 us  [per_device(): put(near, window + 1, permute(near[window], 'row', to_next))]
  transfers between devices with their start and end apart: 34 -> 34, of which waited for: 13 -> 11; matrix products, arithmetic and copies ran while one was open for 5% -> 5% of each run, Pallas kernels for 44% -> 42%
where the time goes in v7:
time: 438 us; the launch traced here: 437 us
  Pallas kernels  184 us (42%)
  waiting for transfers between devices  162 us (37%)
  starting transfers between devices  61 us (14%)
  other arithmetic  19.4 us (4%)
  local copies, waits for them, and re-layouts  8.62 us (2%)
    pallas_call x4, Pallas kernels, second(): pl.pallas_call(second_kernel, grid=(columns // tile,), in_specs=[pl.Block...  95.6 us
    pallas_call x4, Pallas kernels, first(): pl.pallas_call(first_kernel, grid=(rows // tile,), in_specs=[whole, whole...  88.7 us
    ppermute x1, waiting for transfers between devices, per_device(): permute(rest, 'col', [(y, (y + 1) % planes) for y in range(planes)])  37.6 us
    ppermute x7, waiting for transfers between devices, per_device(): permute(rows, both, route_back(group, flip))  34.3 us
    ppermute x4, waiting for transfers between devices, per_device(): put(swapped, closing % ring, permute(sent[closing % ring], 'row', to_pair))  31.6 us
    ppermute x7, waiting for transfers between devices, piece(): return permute(part, both, route(shift, flip))  21.5 us
    ppermute x7, starting transfers between devices, per_device(): permute(rows, both, route_back(group, flip))  18.9 us
    ppermute x4, waiting for transfers between devices, per_device(): put(far, window, permute(near[window], 'row', to_pair))  16.8 us
  transfers between devices with their start and end apart: 34, of which 11 were waited for; matrix products, arithmetic and copies ran while one was open for 5% of the time, Pallas kernels for 42%

profile of v7, /device:TPU:0, one launch (start us, length us, event | category | flops | bytes accessed | tf_op | source)
XLA Modules:
  0.0 437.0 jit_solution(964245098484353045)
XLA Ops:
  1.1 3.7 fusion.4
  10.5 37.6 %collective-permute-done.3 = f32[64,7168]{1,0:T(8,128)S(1)} collective-permute-done((f32[64,7168]{1,0:T(8,128)S(1)}, f32[64,7168]{1,0:T(8,128)S(1)}, u32[]{:S(2)}, u32[]{:S(2)}) %collective-permute-start.3) | collective-permute-done | bytes 1835040 | tf_op jit(solution)/shard_map/ppermute | solution.py:185
  57.1 21.8 %first_product.4 = f32[2,128,896]{2,1,0:T(8,128)S(1)} custom-call(f32[64,7168]{1,0:T(8,128)S(1)} %get-tuple-element.134.near_ref, f32[64,7168]{1,0:T(8,128)S(1)} %copy-done.1, f32[896,7168]{1,0:T(8,128)} %own_ref.15, f32[896,7168]{1,0:T(8,128)} %collective-permute-done.2.sib_ref), custom_call_target="tpu_custom_call" | custom-call | flops 9865003008 | bytes 51380224 | tf_op jit(solution)/shard_map/first_product/pallas_call | solution.py:53
  78.9 15.3 %collective-permute-done.5.far_ref = f32[64,7168]{1,0:T(8,128)} collective-permute-done((f32[64,7168]{1,0:T(8,128)}, f32[64,7168]{1,0:T(8,128)}, u32[]{:S(2)}, u32[]{:S(2)}) %collective-permute-start.5) | collective-permute-done | bytes 1835040 | tf_op jit(solution)/shard_map/ppermute | solution.py:183
  100.4 4.4 %collective-permute-start.9 = (f32[2,64,896]{2,1,0:T(8,128)S(1)}, f32[2,64,896]{2,1,0:T(8,128)S(1)}, u32[]{:S(2)}, u32[]{:S(2)}) collective-permute-start(f32[2,64,896]{2,1,0:T(8,128)S(1)} %fusion.11), channel_id=1, source_target_pairs={{0,8},{2,10},{4,12},{6,14},{9,17},{11,19},{13,21},{15,23},{17,25},... | collective-permute-start | bytes 1376264 | tf_op jit(solution)/shard_map/ppermute | solution.py:160
  104.8 22.8 %first_product.5 = f32[2,128,896]{2,1,0:T(8,128)S(1)} custom-call(f32[64,7168]{1,0:T(8,128)} %collective-permute-done.near_ref, f32[64,7168]{1,0:T(8,128)} %collective-permute-done.5.far_ref, f32[896,7168]{1,0:T(8,128)} %own_ref.15, f32[896,7168]{1,0:T(8,128)} %collective-permute-done.2.sib_ref), custom_call_target="tpu_custom_call" | custom-call | flops 9865003008 | bytes 51380224 | tf_op jit(solution)/shard_map/first_product/pallas_call | solution.py:53
  127.7 21.5 %collective-permute-done.9 = f32[2,64,896]{2,1,0:T(8,128)S(1)} collective-permute-done((f32[2,64,896]{2,1,0:T(8,128)S(1)}, f32[2,64,896]{2,1,0:T(8,128)S(1)}, u32[]{:S(2)}, u32[]{:S(2)}) %collective-permute-start.9) | collective-permute-done | bytes 458784 | tf_op jit(solution)/shard_map/ppermute | solution.py:160
  151.4 2.8 collective-permute-start.14
  156.3 12.0 %collective-permute-done.12 = f32[2,128,896]{2,1,0:T(8,128)S(1)} collective-permute-done((f32[2,128,896]{2,1,0:T(8,128)S(1)}, f32[2,128,896]{2,1,0:T(8,128)S(1)}, u32[]{:S(2)}, u32[]{:S(2)}) %collective-permute-start.12) | collective-permute-done | bytes 917536 | tf_op jit(solution)/shard_map/ppermute | solution.py:163
  169.8 4.4 %collective-permute-start.15 = (f32[2,64,896]{2,1,0:T(8,128)S(1)}, f32[2,64,896]{2,1,0:T(8,128)}, u32[]{:S(2)}, u32[]{:S(2)}) collective-permute-start(f32[2,64,896]{2,1,0:T(8,128)S(1)} %get-tuple-element.145), channel_id=1, source_target_pairs={{8,0},{10,2},{12,4},{14,6},{17,9},{19,11},{21,13},{23,15},{25,17},... | collective-permute-start | bytes 1376264 | tf_op jit(solution)/shard_map/ppermute | solution.py:220
  174.9 23.7 %second_product.4 = (f32[64,7168]{1,0:T(8,128)S(1)}, f32[64,7168]{1,0:T(8,128)S(1)}) custom-call(f32[2,128,896]{2,1,0:T(8,128)S(1)} %add.247.change_ref, f32[896,7168]{1,0:T(8,128)} %own_ref.15, f32[896,7168]{1,0:T(8,128)} %collective-permute-done.2.sib_ref), custom_call_target="tpu_custom_call" | custom-call | flops 9865003008 | bytes 51380224 | tf_op jit(solution)/shard_map/second_product/pallas_call | solution.py:91
  198.6 22.3 %first_product.6 = f32[2,128,896]{2,1,0:T(8,128)S(1)} custom-call(f32[64,7168]{1,0:T(8,128)} %collective-permute-done.4.near_ref, f32[64,7168]{1,0:T(8,128)S(1)} %collective-permute-done.7.far_ref, f32[896,7168]{1,0:T(8,128)} %own_ref.15, f32[896,7168]{1,0:T(8,128)} %collective-permute-done.2.sib_ref), custom_call_target="tpu_custom_call" | custom-call | flops 9865003008 | bytes 51380224 | tf_op jit(solution)/shard_map/first_product/pallas_call | solution.py:53
  223.5 3.1 collective-permute-start.19
  229.4 21.8 %first_product.7 = f32[2,128,896]{2,1,0:T(8,128)S(1)} custom-call(f32[64,7168]{1,0:T(8,128)S(1)} %collective-permute-done.6.near_ref, f32[64,7168]{1,0:T(8,128)S(1)} %collective-permute-done.11.far_ref, f32[896,7168]{1,0:T(8,128)} %own_ref.15, f32[896,7168]{1,0:T(8,128)} %collective-permute-done.2.sib_ref), custom_call_target="tpu_custom_call" | custom-call | flops 9865003008 | bytes 51380224 | tf_op jit(solution)/shard_map/first_product/pallas_call | solution.py:53
  252.1 6.6 %collective-permute-start.21 = (f32[2,64,896]{2,1,0:T(8,128)S(1)}, f32[2,64,896]{2,1,0:T(8,128)S(1)}, u32[]{:S(2)}, u32[]{:S(2)}) collective-permute-start(f32[2,64,896]{2,1,0:T(8,128)S(1)} %get-tuple-element.143), channel_id=1, source_target_pairs={{17,1},{19,3},{21,5},{23,7},{25,9},{27,11},{29,13},{31,15},{0,16},... | collective-permute-start | bytes 1376264 | tf_op jit(solution)/shard_map/ppermute | solution.py:220
  260.6 23.7 %second_product.5 = (f32[64,7168]{1,0:T(8,128)S(1)}, f32[64,7168]{1,0:T(8,128)S(1)}) custom-call(f32[2,128,896]{2,1,0:T(8,128)S(1)} %add.262.change_ref, f32[896,7168]{1,0:T(8,128)} %own_ref.15, f32[896,7168]{1,0:T(8,128)} %collective-permute-done.2.sib_ref), custom_call_target="tpu_custom_call" | custom-call | flops 9865003008 | bytes 51380224 | tf_op jit(solution)/shard_map/second_product/pallas_call | solution.py:91
  294.2 24.6 %second_product.6 = (f32[64,7168]{1,0:T(8,128)S(1)}, f32[64,7168]{1,0:T(8,128)}) custom-call(f32[2,128,896]{2,1,0:T(8,128)S(1)} %add.264.change_ref, f32[896,7168]{1,0:T(8,128)} %own_ref.15, f32[896,7168]{1,0:T(8,128)} %collective-permute-done.2.sib_ref), custom_call_target="tpu_custom_call" | custom-call | flops 9865003008 | bytes 51380224 | tf_op jit(solution)/shard_map/second_product/pallas_call | solution.py:91
  318.9 17.0 %collective-permute-done.25 = f32[2,64,896]{2,1,0:T(8,128)S(1)} collective-permute-done((f32[2,64,896]{2,1,0:T(8,128)S(1)}, f32[2,64,896]{2,1,0:T(8,128)S(1)}, u32[]{:S(2)}, u32[]{:S(2)}) %collective-permute-start.25) | collective-permute-done | bytes 458784 | tf_op jit(solution)/shard_map/ppermute | solution.py:220
  338.0 4.7 %collective-permute-start.31 = (f32[64,7168]{1,0:T(8,128)}, f32[64,7168]{1,0:T(8,128)}, u32[]{:S(2)}, u32[]{:S(2)}) collective-permute-start(f32[64,7168]{1,0:T(8,128)} %add_add_fusion.1), channel_id=1, source_target_pairs={{0,8},{2,10},{4,12},{6,14},{8,16},{10,18},{12,20},{14,22},{16,24},... | collective-permute-start | bytes 5505032 | tf_op jit(solution)/shard_map/ppermute | solution.py:194
  346.7 23.7 %second_product.7 = (f32[64,7168]{1,0:T(8,128)S(1)}, f32[64,7168]{1,0:T(8,128)S(1)}) custom-call(f32[2,128,896]{2,1,0:T(8,128)S(1)} %add.266.change_ref, f32[896,7168]{1,0:T(8,128)} %own_ref.15, f32[896,7168]{1,0:T(8,128)} %collective-permute-done.2.sib_ref), custom_call_target="tpu_custom_call" | custom-call | flops 9865003008 | bytes 51380224 | tf_op jit(solution)/shard_map/second_product/pallas_call | solution.py:91
  370.4 17.2 %collective-permute-done.30 = f32[2,64,896]{2,1,0:T(8,128)S(1)} collective-permute-done((f32[2,64,896]{2,1,0:T(8,128)S(1)}, f32[2,64,896]{2,1,0:T(8,128)S(1)}, u32[]{:S(2)}, u32[]{:S(2)}) %collective-permute-start.30) | collective-permute-done | bytes 458784 | tf_op jit(solution)/shard_map/ppermute | solution.py:220
  390.4 3.4 collective-permute-start.33
  396.7 31.6 %collective-permute-done.32 = f32[64,7168]{1,0:T(8,128)S(1)} collective-permute-done((f32[64,7168]{1,0:T(8,128)S(1)}, f32[64,7168]{1,0:T(8,128)S(1)}, u32[]{:S(2)}, u32[]{:S(2)}) %collective-permute-start.32) | collective-permute-done | bytes 1835040 | tf_op jit(solution)/shard_map/ppermute | solution.py:195
  428.3 4.4 %collective-permute-done.33 = f32[64,7168]{1,0:T(8,128)S(1)} collective-permute-done((f32[64,7168]{1,0:T(8,128)S(1)}, f32[64,7168]{1,0:T(8,128)S(1)}, u32[]{:S(2)}, u32[]{:S(2)}) %collective-permute-start.33) | collective-permute-done | bytes 1835040 | tf_op jit(solution)/shard_map/ppermute | solution.py:194
  (150 shorter events, 61.4 us)
Async XLA Ops:
  0.6 52.1 %collective-permute-start.2 = (f32[896,7168]{1,0:T(8,128)}, f32[896,7168]{1,0:T(8,128)}, u32[]{:S(2)}, u32[]{:S(2)}) collective-permute-start(f32[896,7168]{1,0:T(8,128)} %own_ref.15), channel_id=1, source_target_pairs={{0,2},{2,0},{4,6},{6,4},{8,10},{10,8},{12,14},{14,12},{16,18},{18,... | collective-permute-start | bytes 77070344 | tf_op jit(solution)/shard_map/ppermute | solution.py:149
  4.9 43.3 %collective-permute-start.3 = (f32[64,7168]{1,0:T(8,128)S(1)}, f32[64,7168]{1,0:T(8,128)S(1)}, u32[]{:S(2)}, u32[]{:S(2)}) collective-permute-start(f32[64,7168]{1,0:T(8,128)S(1)} %get-tuple-element.88), channel_id=1, source_target_pairs={{0,1},{1,0},{2,3},{3,2},{4,5},{5,4},{6,7},{7,6},{8,9},{9,8},{10,11... | collective-permute-start | bytes 5505032 | tf_op jit(solution)/shard_map/ppermute | solution.py:185
  7.5 42.1 %collective-permute-start.1 = (f32[64,7168]{1,0:T(8,128)S(1)}, f32[64,7168]{1,0:T(8,128)S(1)}, u32[]{:S(2)}, u32[]{:S(2)}) collective-permute-start(f32[64,7168]{1,0:T(8,128)S(1)} %get-tuple-element.134.near_ref), channel_id=1, source_target_pairs={{0,4},{2,6},{4,0},{6,2},{8,12},{10,14},{12,8},{14,10},{16,20},{18,... | collective-permute-start | bytes 5505032 | tf_op jit(solution)/shard_map/ppermute | solution.py:183
  8.9 43.8 %collective-permute-start = (f32[64,7168]{1,0:T(8,128)S(1)}, f32[64,7168]{1,0:T(8,128)}, u32[]{:S(2)}, u32[]{:S(2)}) collective-permute-start(f32[64,7168]{1,0:T(8,128)S(1)} %get-tuple-element.134.near_ref), channel_id=1, source_target_pairs={{0,8},{2,10},{4,12},{6,14},{8,16},{10,18},{12,20},{14,22},{16,24},... | collective-permute-start | bytes 5505032 | tf_op jit(solution)/shard_map/ppermute | solution.py:181
  53.4 42.9 %collective-permute-start.4 = (f32[64,7168]{1,0:T(8,128)}, f32[64,7168]{1,0:T(8,128)}, u32[]{:S(2)}, u32[]{:S(2)}) collective-permute-start(f32[64,7168]{1,0:T(8,128)} %collective-permute-done.near_ref), channel_id=1, source_target_pairs={{0,8},{2,10},{4,12},{6,14},{8,16},{10,18},{12,20},{14,22},{16,24},... | collective-permute-start | bytes 5505032 | tf_op jit(solution)/shard_map/ppermute | solution.py:181
  55.8 71.9 %collective-permute-start.10 = (f32[2,64,896]{2,1,0:T(8,128)S(1)}, f32[2,64,896]{2,1,0:T(8,128)S(1)}, u32[]{:S(2)}, u32[]{:S(2)}) collective-permute-start(f32[2,64,896]{2,1,0:T(8,128)S(1)} %fusion.12), channel_id=1, source_target_pairs={{1,13},{3,15},{5,9},{7,11},{8,20},{10,22},{12,16},{14,18},{16,28},... | collective-permute-start | bytes 1376264 | tf_op jit(solution)/shard_map/ppermute | solution.py:160
  96.3 53.1 %collective-permute-start.7 = (f32[64,7168]{1,0:T(8,128)}, f32[64,7168]{1,0:T(8,128)S(1)}, u32[]{:S(2)}, u32[]{:S(2)}) collective-permute-start(f32[64,7168]{1,0:T(8,128)} %collective-permute-done.4.near_ref), channel_id=1, source_target_pairs={{0,4},{2,6},{4,0},{6,2},{8,12},{10,14},{12,8},{14,10},{16,20},{18,... | collective-permute-start | bytes 5505032 | tf_op jit(solution)/shard_map/ppermute | solution.py:183
  97.8 51.6 %collective-permute-start.6 = (f32[64,7168]{1,0:T(8,128)}, f32[64,7168]{1,0:T(8,128)S(1)}, u32[]{:S(2)}, u32[]{:S(2)}) collective-permute-start(f32[64,7168]{1,0:T(8,128)} %collective-permute-done.4.near_ref), channel_id=1, source_target_pairs={{0,8},{2,10},{4,12},{6,14},{8,16},{10,18},{12,20},{14,22},{16,24},... | collective-permute-start | bytes 5505032 | tf_op jit(solution)/shard_map/ppermute | solution.py:181
  97.8 51.6 %collective-permute-start.8 = (f32[2,64,896]{2,1,0:T(8,128)S(1)}, f32[2,64,896]{2,1,0:T(8,128)S(1)}, u32[]{:S(2)}, u32[]{:S(2)}) collective-permute-start(f32[2,64,896]{2,1,0:T(8,128)S(1)} %fusion.10), channel_id=1, source_target_pairs={{0,4},{2,6},{4,0},{6,2},{8,12},{10,14},{12,8},{14,10},{17,21},{19,... | collective-permute-start | bytes 1376264 | tf_op jit(solution)/shard_map/ppermute | solution.py:160
  100.4 48.8 %collective-permute-start.9 = (f32[2,64,896]{2,1,0:T(8,128)S(1)}, f32[2,64,896]{2,1,0:T(8,128)S(1)}, u32[]{:S(2)}, u32[]{:S(2)}) collective-permute-start(f32[2,64,896]{2,1,0:T(8,128)S(1)} %fusion.11), channel_id=1, source_target_pairs={{0,8},{2,10},{4,12},{6,14},{9,17},{11,19},{13,21},{15,23},{17,25},... | collective-permute-start | bytes 1376264 | tf_op jit(solution)/shard_map/ppermute | solution.py:160
  151.4 69.4 %collective-permute-start.14 = (f32[2,64,896]{2,1,0:T(8,128)}, f32[2,64,896]{2,1,0:T(8,128)}, u32[]{:S(2)}, u32[]{:S(2)}) collective-permute-start(f32[2,64,896]{2,1,0:T(8,128)} %fusion.14), channel_id=1, source_target_pairs={{0,20},{2,22},{4,16},{6,18},{8,28},{10,30},{12,24},{14,26},{17,5},... | collective-permute-start | bytes 1376264 | tf_op jit(solution)/shard_map/ppermute | solution.py:160
  155.0 65.8 %collective-permute-start.13 = (f32[2,64,896]{2,1,0:T(8,128)}, f32[2,64,896]{2,1,0:T(8,128)}, u32[]{:S(2)}, u32[]{:S(2)}) collective-permute-start(f32[2,64,896]{2,1,0:T(8,128)} %fusion.13), channel_id=1, source_target_pairs={{1,17},{3,19},{5,21},{7,23},{9,25},{11,27},{13,29},{15,31},{16,0},... | collective-permute-start | bytes 1376264 | tf_op jit(solution)/shard_map/ppermute | solution.py:160
  168.5 53.7 %collective-permute-start.16 = (f32[2,64,896]{2,1,0:T(8,128)S(1)}, f32[2,64,896]{2,1,0:T(8,128)S(1)}, u32[]{:S(2)}, u32[]{:S(2)}) collective-permute-start(f32[2,64,896]{2,1,0:T(8,128)S(1)} %get-tuple-element.144), channel_id=1, source_target_pairs={{13,0},{15,2},{9,4},{11,6},{20,9},{22,11},{16,13},{18,15},{28,17},... | collective-permute-start | bytes 1376264 | tf_op jit(solution)/shard_map/ppermute | solution.py:220
  169.8 52.4 %collective-permute-start.15 = (f32[2,64,896]{2,1,0:T(8,128)S(1)}, f32[2,64,896]{2,1,0:T(8,128)}, u32[]{:S(2)}, u32[]{:S(2)}) collective-permute-start(f32[2,64,896]{2,1,0:T(8,128)S(1)} %get-tuple-element.145), channel_id=1, source_target_pairs={{8,0},{10,2},{12,4},{14,6},{17,9},{19,11},{21,13},{23,15},{25,17},... | collective-permute-start | bytes 1376264 | tf_op jit(solution)/shard_map/ppermute | solution.py:220
  174.2 48.0 %collective-permute-start.11 = (f32[64,7168]{1,0:T(8,128)S(1)}, f32[64,7168]{1,0:T(8,128)S(1)}, u32[]{:S(2)}, u32[]{:S(2)}) collective-permute-start(f32[64,7168]{1,0:T(8,128)S(1)} %collective-permute-done.6.near_ref), channel_id=1, source_target_pairs={{0,4},{2,6},{4,0},{6,2},{8,12},{10,14},{12,8},{14,10},{16,20},{18,... | collective-permute-start | bytes 5505032 | tf_op jit(solution)/shard_map/ppermute | solution.py:183
  227.9 56.3 %collective-permute-start.17 = (f32[64,7168]{1,0:T(8,128)S(1)}, f32[64,7168]{1,0:T(8,128)S(1)}, u32[]{:S(2)}, u32[]{:S(2)}) collective-permute-start(f32[64,7168]{1,0:T(8,128)S(1)} %get-tuple-element.85), channel_id=1, source_target_pairs={{0,4},{2,6},{4,0},{6,2},{8,12},{10,14},{12,8},{14,10},{16,20},{18,... | collective-permute-start | bytes 5505032 | tf_op jit(solution)/shard_map/ppermute | solution.py:195
  284.3 51.6 %collective-permute-start.23 = (f32[64,7168]{1,0:T(8,128)S(1)}, f32[64,7168]{1,0:T(8,128)S(1)}, u32[]{:S(2)}, u32[]{:S(2)}) collective-permute-start(f32[64,7168]{1,0:T(8,128)S(1)} %get-tuple-element.94), channel_id=1, source_target_pairs={{0,4},{2,6},{4,0},{6,2},{8,12},{10,14},{12,8},{14,10},{16,20},{18,... | collective-permute-start | bytes 5505032 | tf_op jit(solution)/shard_map/ppermute | solution.py:195
  286.7 49.2 %collective-permute-start.27 = (f32[64,7168]{1,0:T(8,128)}, f32[64,7168]{1,0:T(8,128)S(1)}, u32[]{:S(2)}, u32[]{:S(2)}) collective-permute-start(f32[64,7168]{1,0:T(8,128)} %add.265), channel_id=1, source_target_pairs={{0,8},{2,10},{4,12},{6,14},{8,16},{10,18},{12,20},{14,22},{16,24},... | collective-permute-start | bytes 5505032 | tf_op jit(solution)/shard_map/ppermute | solution.py:194
  289.2 53.4 %collective-permute-start.29 = (f32[2,128,896]{2,1,0:T(8,128)S(1)}, f32[2,128,896]{2,1,0:T(8,128)}, u32[]{:S(2)}, u32[]{:S(2)}) collective-permute-start(f32[2,128,896]{2,1,0:T(8,128)S(1)} %maximum_add_fusion.3), channel_id=1, source_target_pairs={{0,1},{1,0},{2,3},{3,2},{4,5},{5,4},{6,7},{7,6},{8,9},{9,8},{10,11... | collective-permute-start | bytes 2752520 | tf_op jit(solution)/shard_map/ppermute | solution.py:163
  291.7 44.2 %collective-permute-start.25 = (f32[2,64,896]{2,1,0:T(8,128)S(1)}, f32[2,64,896]{2,1,0:T(8,128)S(1)}, u32[]{:S(2)}, u32[]{:S(2)}) collective-permute-start(f32[2,64,896]{2,1,0:T(8,128)S(1)} %get-tuple-element.141), channel_id=1, source_target_pairs={{25,1},{27,3},{29,5},{31,7},{0,8},{2,10},{4,12},{6,14},{8,16},{10,... | collective-permute-start | bytes 1376264 | tf_op jit(solution)/shard_map/ppermute | solution.py:220
  335.9 51.7 %collective-permute-start.28 = (f32[64,7168]{1,0:T(8,128)}, f32[64,7168]{1,0:T(8,128)}, u32[]{:S(2)}, u32[]{:S(2)}) collective-permute-start(f32[64,7168]{1,0:T(8,128)} %get-tuple-element.104), channel_id=1, source_target_pairs={{0,4},{2,6},{4,0},{6,2},{8,12},{10,14},{12,8},{14,10},{16,20},{18,... | collective-permute-start | bytes 5505032 | tf_op jit(solution)/shard_map/ppermute | solution.py:195
  338.0 49.6 %collective-permute-start.31 = (f32[64,7168]{1,0:T(8,128)}, f32[64,7168]{1,0:T(8,128)}, u32[]{:S(2)}, u32[]{:S(2)}) collective-permute-start(f32[64,7168]{1,0:T(8,128)} %add_add_fusion.1), channel_id=1, source_target_pairs={{0,8},{2,10},{4,12},{6,14},{8,16},{10,18},{12,20},{14,22},{16,24},... | collective-permute-start | bytes 5505032 | tf_op jit(solution)/shard_map/ppermute | solution.py:194
  344.0 43.6 %collective-permute-start.30 = (f32[2,64,896]{2,1,0:T(8,128)S(1)}, f32[2,64,896]{2,1,0:T(8,128)S(1)}, u32[]{:S(2)}, u32[]{:S(2)}) collective-permute-start(f32[2,64,896]{2,1,0:T(8,128)S(1)} %get-tuple-element.138), channel_id=1, source_target_pairs={{4,0},{6,2},{0,4},{2,6},{12,8},{14,10},{8,12},{10,14},{21,17},{23,... | collective-permute-start | bytes 1376264 | tf_op jit(solution)/shard_map/ppermute | solution.py:220
  390.4 42.2 %collective-permute-start.33 = (f32[64,7168]{1,0:T(8,128)S(1)}, f32[64,7168]{1,0:T(8,128)S(1)}, u32[]{:S(2)}, u32[]{:S(2)}) collective-permute-start(f32[64,7168]{1,0:T(8,128)S(1)} %add_add_fusion), channel_id=1, source_target_pairs={{0,8},{2,10},{4,12},{6,14},{8,16},{10,18},{12,20},{14,22},{16,24},... | collective-permute-start | bytes 5505032 | tf_op jit(solution)/shard_map/ppermute | solution.py:194
  (29 other events, 549.4 us)

commit v8 on v7

--- a/solution.py
+++ b/solution.py
@@ -169,7 +169,7 @@
     total = None
     start = max(ring, 4)
     returns = {group + 2: [(group, 0), (group, 1)] for group in range(1, ring)}
-    returns.setdefault(start + ring - 2, []).extend([(0, 0), (0, 1)])
+    returns.setdefault(start + 1, []).extend([(0, 0), (0, 1)])
     for window in range(start + ring):
         fresh = []
 
@@ -186,8 +186,8 @@
         for group in (0, 1) if window == 1 else (window - 1,) if 2 < window <= ring else ():
             for flip in range(PAIR):
                 added[group, flip] = piece(group, flip)
-        if window == 2:
-            fresh += [(added, (0, flip)) for flip in range(PAIR)]
+        if window == 1:
+            fresh += [(added, (group, flip)) for group in (0, 1) for flip in range(PAIR)]
         closing = window - start + 1
         if closing >= 1:
             if total is not None:
@@ -202,13 +202,16 @@
             put(product, group, first(near[group], far[group], hessian, sibling))
             if group in (1, ring - 1):
                 join(group)
-        if window == start + 1:
+        if window == 2:
             join(0)
+        if window == 3:
+            put(changed, 0, mine[0] + other[0])
         group = 0 if window == start + ring - 2 else window - 2
         if 1 <= group < ring or window == start + ring - 2:
             if 2 <= group < ring - 1:
                 product[group + 1], other[group] = lax.optimization_barrier((product[group + 1], other[group]))
-            put(changed, group, mine[group] + other[group])
+            if group:
+                put(changed, group, mine[group] + other[group])
             keep, send = second(changed[group], hessian, sibling)
             if 2 <= window - 1 < ring - 1:
                 keep, product[window - 1] = lax.optimization_barrier((keep, product[window - 1]))

time: 438 us -> 435 us (level)
  waiting for transfers between devices: 162 us -> 155 us
    ppermute x3, waiting for transfers between devices: 4.4 us -> 43.8 us  [per_device(): total = permute(total, 'row', to_next)]
    ppermute x4, waiting for transfers between devices: 31.6 us -> 10.2 us  [per_device(): put(swapped, closing % ring, permute(sent[closing % ring], 'row', to_pair))]
    ppermute x4, waiting for transfers between devices: 12 us -> 0.01 us  [sum_planes(): permute(part, 'col', [(y, (y + turn) % planes) for y in range(planes)])]
    ppermute x7, waiting for transfers between devices: 34.3 us -> 24.7 us  [per_device(): permute(rows, both, route_back(group, flip))]
    ppermute x7, starting transfers between devices: 18.9 us -> 27.6 us  [per_device(): permute(rows, both, route_back(group, flip))]
    ppermute x3, starting transfers between devices: 10.5 us -> 2.87 us  [per_device(): total = permute(total, 'row', to_next)]
  transfers between devices with their start and end apart: 34 -> 34, of which waited for: 11 -> 11; matrix products, arithmetic and copies ran while one was open for 5% -> 5% of each run, Pallas kernels for 42% -> 43%
where the time goes in v8:
time: 435 us; the launch traced here: 434 us
  Pallas kernels  185 us (43%)
  waiting for transfers between devices  155 us (36%)
  starting transfers between devices  62.1 us (14%)
  other arithmetic  19.8 us (5%)
  local copies, waits for them, and re-layouts  10.3 us (2%)
    pallas_call x4, Pallas kernels, second(): pl.pallas_call(second_kernel, grid=(columns // tile,), in_specs=[pl.Block...  95.6 us
    pallas_call x4, Pallas kernels, first(): pl.pallas_call(first_kernel, grid=(rows // tile,), in_specs=[whole, whole...  89.7 us
    ppermute x3, waiting for transfers between devices, per_device(): total = permute(total, 'row', to_next)  43.8 us
    ppermute x1, waiting for transfers between devices, per_device(): permute(rest, 'col', [(y, (y + 1) % planes) for y in range(planes)])  37.9 us
    ppermute x7, starting transfers between devices, per_device(): permute(rows, both, route_back(group, flip))  27.6 us
    ppermute x7, waiting for transfers between devices, per_device(): permute(rows, both, route_back(group, flip))  24.7 us
    ppermute x7, waiting for transfers between devices, piece(): return permute(part, both, route(shift, flip))  18.2 us
    ppermute x7, starting transfers between devices, piece(): return permute(part, both, route(shift, flip))  16.6 us
  transfers between devices with their start and end apart: 34, of which 11 were waited for; matrix products, arithmetic and copies ran while one was open for 5% of the time, Pallas kernels for 43%

profile of v8, /device:TPU:0, one launch (start us, length us, event | category | flops | bytes accessed | tf_op | source)
XLA Modules:
  0.0 434.1 jit_solution(4964059159502218321)
XLA Ops:
  1.1 4.9 %fusion.4 = (f32[64,7168]{1,0:T(8,128)}, f32[64,7168]{1,0:T(8,128)S(1)}) fusion(f32[7168,64]{0,1:T(8,128)} %param.8, f32[7168,64]{0,1:T(8,128)} %param.6, f32[7168,64]{0,1:T(8,128)} %param.7, s32[7168,64]{0,1:T(8,128)} %param.9), kind=kLoop, calls=%fused_computation.7 | loop fusion | flops 4128768 | bytes 11010048 | tf_op jit(solution)/shard_map/sub | solution.py:150
  11.7 37.9 %collective-permute-done.3 = f32[64,7168]{1,0:T(8,128)} collective-permute-done((f32[64,7168]{1,0:T(8,128)}, f32[64,7168]{1,0:T(8,128)}, u32[]{:S(2)}, u32[]{:S(2)}) %collective-permute-start.3) | collective-permute-done | bytes 1835040 | tf_op jit(solution)/shard_map/ppermute | solution.py:185
  50.8 3.1 collective-permute-done.near_ref
  57.0 3.4 collective-permute-start.6
  60.4 6.0 %collective-permute-start.7 = (f32[2,64,896]{2,1,0:T(8,128)S(1)}, f32[2,64,896]{2,1,0:T(8,128)S(1)}, u32[]{:S(2)}, u32[]{:S(2)}) collective-permute-start(f32[2,64,896]{2,1,0:T(8,128)S(1)} %fusion.11), channel_id=1, source_target_pairs={{0,8},{2,10},{4,12},{6,14},{9,17},{11,19},{13,21},{15,23},{17,25},... | collective-permute-start | bytes 1376264 | tf_op jit(solution)/shard_map/ppermute | solution.py:160
  66.4 22.3 %first_product.4 = f32[2,128,896]{2,1,0:T(8,128)S(1)} custom-call(f32[64,7168]{1,0:T(8,128)S(1)} %get-tuple-element.140.near_ref, f32[64,7168]{1,0:T(8,128)} %collective-permute-done.1.far_ref, f32[896,7168]{1,0:T(8,128)} %own_ref.15, f32[896,7168]{1,0:T(8,128)} %collective-permute-done.2.sib_ref), custom_call_target="tpu_custom_call" | custom-call | flops 9865003008 | bytes 51380224 | tf_op jit(solution)/shard_map/first_product/pallas_call | solution.py:53
  88.8 16.3 %collective-permute-done.6 = f32[2,64,896]{2,1,0:T(8,128)} collective-permute-done((f32[2,64,896]{2,1,0:T(8,128)S(1)}, f32[2,64,896]{2,1,0:T(8,128)}, u32[]{:S(2)}, u32[]{:S(2)}) %collective-permute-start.6) | collective-permute-done | bytes 458784 | tf_op jit(solution)/shard_map/ppermute | solution.py:160
  112.6 22.3 %first_product.5 = f32[2,128,896]{2,1,0:T(8,128)S(1)} custom-call(f32[64,7168]{1,0:T(8,128)} %collective-permute-done.near_ref, f32[64,7168]{1,0:T(8,128)S(1)} %copy-done.1, f32[896,7168]{1,0:T(8,128)} %own_ref.15, f32[896,7168]{1,0:T(8,128)} %collective-permute-done.2.sib_ref), custom_call_target="tpu_custom_call" | custom-call | flops 9865003008 | bytes 51380224 | tf_op jit(solution)/shard_map/first_product/pallas_call | solution.py:53
  135.7 13.0 %collective-permute-done.10.far_ref = f32[64,7168]{1,0:T(8,128)} collective-permute-done((f32[64,7168]{1,0:T(8,128)}, f32[64,7168]{1,0:T(8,128)}, u32[]{:S(2)}, u32[]{:S(2)}) %collective-permute-start.10) | collective-permute-done | bytes 1835040 | tf_op jit(solution)/shard_map/ppermute | solution.py:183
  148.7 3.0 collective-permute-done.9.near_ref
  159.4 23.7 %second_product.4 = (f32[64,7168]{1,0:T(8,128)S(1)}, f32[64,7168]{1,0:T(8,128)S(1)}) custom-call(f32[2,128,896]{2,1,0:T(8,128)S(1)} %add.248.change_ref, f32[896,7168]{1,0:T(8,128)} %own_ref.15, f32[896,7168]{1,0:T(8,128)} %collective-permute-done.2.sib_ref), custom_call_target="tpu_custom_call" | custom-call | flops 9865003008 | bytes 51380224 | tf_op jit(solution)/shard_map/second_product/pallas_call | solution.py:91
  183.1 10.1 %collective-permute-start.16 = (f32[2,64,896]{2,1,0:T(8,128)S(1)}, f32[2,64,896]{2,1,0:T(8,128)S(1)}, u32[]{:S(2)}, u32[]{:S(2)}) collective-permute-start(f32[2,64,896]{2,1,0:T(8,128)S(1)} %get-tuple-element.151), channel_id=1, source_target_pairs={{8,0},{10,2},{12,4},{14,6},{17,9},{19,11},{21,13},{23,15},{25,17},... | collective-permute-start | bytes 1376264 | tf_op jit(solution)/shard_map/ppermute | solution.py:223
  193.2 22.8 %first_product.6 = f32[2,128,896]{2,1,0:T(8,128)S(1)} custom-call(f32[64,7168]{1,0:T(8,128)} %collective-permute-done.4.near_ref, f32[64,7168]{1,0:T(8,128)} %collective-permute-done.10.far_ref, f32[896,7168]{1,0:T(8,128)} %own_ref.15, f32[896,7168]{1,0:T(8,128)} %collective-permute-done.2.sib_ref), custom_call_target="tpu_custom_call" | custom-call | flops 9865003008 | bytes 51380224 | tf_op jit(solution)/shard_map/first_product/pallas_call | solution.py:53
  224.3 22.3 %first_product.7 = f32[2,128,896]{2,1,0:T(8,128)S(1)} custom-call(f32[64,7168]{1,0:T(8,128)} %collective-permute-done.9.near_ref, f32[64,7168]{1,0:T(8,128)S(1)} %collective-permute-done.11.far_ref, f32[896,7168]{1,0:T(8,128)} %own_ref.15, f32[896,7168]{1,0:T(8,128)} %collective-permute-done.2.sib_ref), custom_call_target="tpu_custom_call" | custom-call | flops 9865003008 | bytes 51380224 | tf_op jit(solution)/shard_map/first_product/pallas_call | solution.py:53
  247.5 9.5 %collective-permute-start.22 = (f32[2,64,896]{2,1,0:T(8,128)S(1)}, f32[2,64,896]{2,1,0:T(8,128)S(1)}, u32[]{:S(2)}, u32[]{:S(2)}) collective-permute-start(f32[2,64,896]{2,1,0:T(8,128)S(1)} %get-tuple-element.149), channel_id=1, source_target_pairs={{17,1},{19,3},{21,5},{23,7},{25,9},{27,11},{29,13},{31,15},{0,16},... | collective-permute-start | bytes 1376264 | tf_op jit(solution)/shard_map/ppermute | solution.py:223
  258.0 24.6 %second_product.5 = (f32[64,7168]{1,0:T(8,128)S(1)}, f32[64,7168]{1,0:T(8,128)}) custom-call(f32[2,128,896]{2,1,0:T(8,128)S(1)} %add.264.change_ref, f32[896,7168]{1,0:T(8,128)} %own_ref.15, f32[896,7168]{1,0:T(8,128)} %collective-permute-done.2.sib_ref), custom_call_target="tpu_custom_call" | custom-call | flops 9865003008 | bytes 51380224 | tf_op jit(solution)/shard_map/second_product/pallas_call | solution.py:91
  284.9 2.7 collective-permute-start.29
  292.7 2.7 collective-permute-start.26
  295.3 23.7 %second_product.6 = (f32[64,7168]{1,0:T(8,128)S(1)}, f32[64,7168]{1,0:T(8,128)S(1)}) custom-call(f32[2,128,896]{2,1,0:T(8,128)S(1)} %add.265.change_ref, f32[896,7168]{1,0:T(8,128)} %own_ref.15, f32[896,7168]{1,0:T(8,128)} %collective-permute-done.2.sib_ref), custom_call_target="tpu_custom_call" | custom-call | flops 9865003008 | bytes 51380224 | tf_op jit(solution)/shard_map/second_product/pallas_call | solution.py:91
  319.0 24.6 %collective-permute-done.28 = f32[2,64,896]{2,1,0:T(8,128)S(1)} collective-permute-done((f32[2,64,896]{2,1,0:T(8,128)S(1)}, f32[2,64,896]{2,1,0:T(8,128)S(1)}, u32[]{:S(2)}, u32[]{:S(2)}) %collective-permute-start.28) | collective-permute-done | bytes 458784 | tf_op jit(solution)/shard_map/ppermute | solution.py:223
  350.0 23.7 %second_product.7 = (f32[64,7168]{1,0:T(8,128)S(1)}, f32[64,7168]{1,0:T(8,128)S(1)}) custom-call(f32[2,128,896]{2,1,0:T(8,128)S(1)} %add.249.change_ref, f32[896,7168]{1,0:T(8,128)} %own_ref.15, f32[896,7168]{1,0:T(8,128)} %collective-permute-done.2.sib_ref), custom_call_target="tpu_custom_call" | custom-call | flops 9865003008 | bytes 51380224 | tf_op jit(solution)/shard_map/second_product/pallas_call | solution.py:91
  373.7 10.2 %collective-permute-done.30 = f32[64,7168]{1,0:T(8,128)S(1)} collective-permute-done((f32[64,7168]{1,0:T(8,128)S(1)}, f32[64,7168]{1,0:T(8,128)S(1)}, u32[]{:S(2)}, u32[]{:S(2)}) %collective-permute-start.30) | collective-permute-done | bytes 1835040 | tf_op jit(solution)/shard_map/ppermute | solution.py:195
  383.9 4.6 %collective-permute-done.31 = f32[64,7168]{1,0:T(8,128)S(1)} collective-permute-done((f32[64,7168]{1,0:T(8,128)S(1)}, f32[64,7168]{1,0:T(8,128)S(1)}, u32[]{:S(2)}, u32[]{:S(2)}) %collective-permute-start.31) | collective-permute-done | bytes 1835040 | tf_op jit(solution)/shard_map/ppermute | solution.py:194
  390.5 39.1 %collective-permute-done.33 = f32[64,7168]{1,0:T(8,128)S(1)} collective-permute-done((f32[64,7168]{1,0:T(8,128)S(1)}, f32[64,7168]{1,0:T(8,128)S(1)}, u32[]{:S(2)}, u32[]{:S(2)}) %collective-permute-start.33) | collective-permute-done | bytes 1835040 | tf_op jit(solution)/shard_map/ppermute | solution.py:194
  (148 shorter events, 56.1 us)
Async XLA Ops:
  0.6 53.3 %collective-permute-start.2 = (f32[896,7168]{1,0:T(8,128)}, f32[896,7168]{1,0:T(8,128)}, u32[]{:S(2)}, u32[]{:S(2)}) collective-permute-start(f32[896,7168]{1,0:T(8,128)} %own_ref.15), channel_id=1, source_target_pairs={{0,2},{2,0},{4,6},{6,4},{8,10},{10,8},{12,14},{14,12},{16,18},{18,... | collective-permute-start | bytes 77070344 | tf_op jit(solution)/shard_map/ppermute | solution.py:149
  6.1 43.5 %collective-permute-start.3 = (f32[64,7168]{1,0:T(8,128)}, f32[64,7168]{1,0:T(8,128)}, u32[]{:S(2)}, u32[]{:S(2)}) collective-permute-start(f32[64,7168]{1,0:T(8,128)} %get-tuple-element.97), channel_id=1, source_target_pairs={{0,1},{1,0},{2,3},{3,2},{4,5},{5,4},{6,7},{7,6},{8,9},{9,8},{10,11... | collective-permute-start | bytes 5505032 | tf_op jit(solution)/shard_map/ppermute | solution.py:185
  8.6 42.2 %collective-permute-start.1 = (f32[64,7168]{1,0:T(8,128)S(1)}, f32[64,7168]{1,0:T(8,128)}, u32[]{:S(2)}, u32[]{:S(2)}) collective-permute-start(f32[64,7168]{1,0:T(8,128)S(1)} %get-tuple-element.140.near_ref), channel_id=1, source_target_pairs={{0,4},{2,6},{4,0},{6,2},{8,12},{10,14},{12,8},{14,10},{16,20},{18,... | collective-permute-start | bytes 5505032 | tf_op jit(solution)/shard_map/ppermute | solution.py:183
  10.1 43.8 %collective-permute-start = (f32[64,7168]{1,0:T(8,128)S(1)}, f32[64,7168]{1,0:T(8,128)}, u32[]{:S(2)}, u32[]{:S(2)}) collective-permute-start(f32[64,7168]{1,0:T(8,128)S(1)} %get-tuple-element.140.near_ref), channel_id=1, source_target_pairs={{0,8},{2,10},{4,12},{6,14},{8,16},{10,18},{12,20},{14,22},{16,24},... | collective-permute-start | bytes 5505032 | tf_op jit(solution)/shard_map/ppermute | solution.py:181
  53.9 53.2 %collective-permute-start.5 = (f32[64,7168]{1,0:T(8,128)}, f32[64,7168]{1,0:T(8,128)S(1)}, u32[]{:S(2)}, u32[]{:S(2)}) collective-permute-start(f32[64,7168]{1,0:T(8,128)} %collective-permute-done.near_ref), channel_id=1, source_target_pairs={{0,4},{2,6},{4,0},{6,2},{8,12},{10,14},{12,8},{14,10},{16,20},{18,... | collective-permute-start | bytes 5505032 | tf_op jit(solution)/shard_map/ppermute | solution.py:183
  54.4 53.9 %collective-permute-start.4 = (f32[64,7168]{1,0:T(8,128)}, f32[64,7168]{1,0:T(8,128)}, u32[]{:S(2)}, u32[]{:S(2)}) collective-permute-start(f32[64,7168]{1,0:T(8,128)} %collective-permute-done.near_ref), channel_id=1, source_target_pairs={{0,8},{2,10},{4,12},{6,14},{8,16},{10,18},{12,20},{14,22},{16,24},... | collective-permute-start | bytes 5505032 | tf_op jit(solution)/shard_map/ppermute | solution.py:181
  57.0 48.2 %collective-permute-start.6 = (f32[2,64,896]{2,1,0:T(8,128)S(1)}, f32[2,64,896]{2,1,0:T(8,128)}, u32[]{:S(2)}, u32[]{:S(2)}) collective-permute-start(f32[2,64,896]{2,1,0:T(8,128)S(1)} %fusion.10), channel_id=1, source_target_pairs={{0,4},{2,6},{4,0},{6,2},{8,12},{10,14},{12,8},{14,10},{17,21},{19,... | collective-permute-start | bytes 1376264 | tf_op jit(solution)/shard_map/ppermute | solution.py:160
  60.4 46.7 %collective-permute-start.7 = (f32[2,64,896]{2,1,0:T(8,128)S(1)}, f32[2,64,896]{2,1,0:T(8,128)S(1)}, u32[]{:S(2)}, u32[]{:S(2)}) collective-permute-start(f32[2,64,896]{2,1,0:T(8,128)S(1)} %fusion.11), channel_id=1, source_target_pairs={{0,8},{2,10},{4,12},{6,14},{9,17},{11,19},{13,21},{15,23},{17,25},... | collective-permute-start | bytes 1376264 | tf_op jit(solution)/shard_map/ppermute | solution.py:160
  110.0 41.7 %collective-permute-start.9 = (f32[64,7168]{1,0:T(8,128)}, f32[64,7168]{1,0:T(8,128)}, u32[]{:S(2)}, u32[]{:S(2)}) collective-permute-start(f32[64,7168]{1,0:T(8,128)} %collective-permute-done.4.near_ref), channel_id=1, source_target_pairs={{0,8},{2,10},{4,12},{6,14},{8,16},{10,18},{12,20},{14,22},{16,24},... | collective-permute-start | bytes 5505032 | tf_op jit(solution)/shard_map/ppermute | solution.py:181
  111.1 72.0 %collective-permute-start.13 = (f32[2,128,896]{2,1,0:T(8,128)S(1)}, f32[2,128,896]{2,1,0:T(8,128)S(1)}, u32[]{:S(2)}, u32[]{:S(2)}) collective-permute-start(f32[2,128,896]{2,1,0:T(8,128)S(1)} %maximum_add_fusion.1), channel_id=1, source_target_pairs={{0,1},{1,0},{2,3},{3,2},{4,5},{5,4},{6,7},{7,6},{8,9},{9,8},{10,11... | collective-permute-start | bytes 2752520 | tf_op jit(solution)/shard_map/ppermute | solution.py:163
  153.9 62.3 %collective-permute-start.15 = (f32[2,64,896]{2,1,0:T(8,128)S(1)}, f32[2,64,896]{2,1,0:T(8,128)}, u32[]{:S(2)}, u32[]{:S(2)}) collective-permute-start(f32[2,64,896]{2,1,0:T(8,128)S(1)} %fusion.14), channel_id=1, source_target_pairs={{0,20},{2,22},{4,16},{6,18},{8,28},{10,30},{12,24},{14,26},{17,5},... | collective-permute-start | bytes 1376264 | tf_op jit(solution)/shard_map/ppermute | solution.py:160
  156.0 60.1 %collective-permute-start.14 = (f32[2,64,896]{2,1,0:T(8,128)S(1)}, f32[2,64,896]{2,1,0:T(8,128)}, u32[]{:S(2)}, u32[]{:S(2)}) collective-permute-start(f32[2,64,896]{2,1,0:T(8,128)S(1)} %fusion.13), channel_id=1, source_target_pairs={{1,17},{3,19},{5,21},{7,23},{9,25},{11,27},{13,29},{15,31},{16,0},... | collective-permute-start | bytes 1376264 | tf_op jit(solution)/shard_map/ppermute | solution.py:160
  157.5 60.0 %collective-permute-start.17 = (f32[2,64,896]{2,1,0:T(8,128)S(1)}, f32[2,64,896]{2,1,0:T(8,128)S(1)}, u32[]{:S(2)}, u32[]{:S(2)}) collective-permute-start(f32[2,64,896]{2,1,0:T(8,128)S(1)} %get-tuple-element.150), channel_id=1, source_target_pairs={{13,0},{15,2},{9,4},{11,6},{20,9},{22,11},{16,13},{18,15},{28,17},... | collective-permute-start | bytes 1376264 | tf_op jit(solution)/shard_map/ppermute | solution.py:223
  158.8 58.7 %collective-permute-start.11 = (f32[64,7168]{1,0:T(8,128)}, f32[64,7168]{1,0:T(8,128)S(1)}, u32[]{:S(2)}, u32[]{:S(2)}) collective-permute-start(f32[64,7168]{1,0:T(8,128)} %collective-permute-done.9.near_ref), channel_id=1, source_target_pairs={{0,4},{2,6},{4,0},{6,2},{8,12},{10,14},{12,8},{14,10},{16,20},{18,... | collective-permute-start | bytes 5505032 | tf_op jit(solution)/shard_map/ppermute | solution.py:183
  223.2 59.4 %collective-permute-start.18 = (f32[64,7168]{1,0:T(8,128)S(1)}, f32[64,7168]{1,0:T(8,128)S(1)}, u32[]{:S(2)}, u32[]{:S(2)}) collective-permute-start(f32[64,7168]{1,0:T(8,128)S(1)} %get-tuple-element.94), channel_id=1, source_target_pairs={{0,4},{2,6},{4,0},{6,2},{8,12},{10,14},{12,8},{14,10},{16,20},{18,... | collective-permute-start | bytes 5505032 | tf_op jit(solution)/shard_map/ppermute | solution.py:195
  282.6 61.0 %collective-permute-start.24 = (f32[64,7168]{1,0:T(8,128)}, f32[64,7168]{1,0:T(8,128)}, u32[]{:S(2)}, u32[]{:S(2)}) collective-permute-start(f32[64,7168]{1,0:T(8,128)} %get-tuple-element.103), channel_id=1, source_target_pairs={{0,4},{2,6},{4,0},{6,2},{8,12},{10,14},{12,8},{14,10},{16,20},{18,... | collective-permute-start | bytes 5505032 | tf_op jit(solution)/shard_map/ppermute | solution.py:195
  284.9 58.8 %collective-permute-start.29 = (f32[64,7168]{1,0:T(8,128)}, f32[64,7168]{1,0:T(8,128)}, u32[]{:S(2)}, u32[]{:S(2)}) collective-permute-start(f32[64,7168]{1,0:T(8,128)} %add.266), channel_id=1, source_target_pairs={{0,8},{2,10},{4,12},{6,14},{8,16},{10,18},{12,20},{14,22},{16,24},... | collective-permute-start | bytes 5505032 | tf_op jit(solution)/shard_map/ppermute | solution.py:194
  287.7 56.0 %collective-permute-start.28 = (f32[2,64,896]{2,1,0:T(8,128)S(1)}, f32[2,64,896]{2,1,0:T(8,128)S(1)}, u32[]{:S(2)}, u32[]{:S(2)}) collective-permute-start(f32[2,64,896]{2,1,0:T(8,128)S(1)} %get-tuple-element.144), channel_id=1, source_target_pairs={{4,0},{6,2},{0,4},{2,6},{12,8},{14,10},{8,12},{10,14},{21,17},{23,... | collective-permute-start | bytes 1376264 | tf_op jit(solution)/shard_map/ppermute | solution.py:223
  292.0 51.7 %collective-permute-start.27 = (f32[2,64,896]{2,1,0:T(8,128)S(1)}, f32[2,64,896]{2,1,0:T(8,128)S(1)}, u32[]{:S(2)}, u32[]{:S(2)}) collective-permute-start(f32[2,64,896]{2,1,0:T(8,128)S(1)} %get-tuple-element.146), channel_id=1, source_target_pairs={{28,1},{30,3},{24,5},{26,7},{5,8},{7,10},{1,12},{3,14},{13,16},{15... | collective-permute-start | bytes 1376264 | tf_op jit(solution)/shard_map/ppermute | solution.py:223
  292.7 51.0 %collective-permute-start.26 = (f32[2,64,896]{2,1,0:T(8,128)S(1)}, f32[2,64,896]{2,1,0:T(8,128)S(1)}, u32[]{:S(2)}, u32[]{:S(2)}) collective-permute-start(f32[2,64,896]{2,1,0:T(8,128)S(1)} %get-tuple-element.147), channel_id=1, source_target_pairs={{25,1},{27,3},{29,5},{31,7},{0,8},{2,10},{4,12},{6,14},{8,16},{10,... | collective-permute-start | bytes 1376264 | tf_op jit(solution)/shard_map/ppermute | solution.py:223
  343.7 40.2 %collective-permute-start.30 = (f32[64,7168]{1,0:T(8,128)S(1)}, f32[64,7168]{1,0:T(8,128)S(1)}, u32[]{:S(2)}, u32[]{:S(2)}) collective-permute-start(f32[64,7168]{1,0:T(8,128)S(1)} %get-tuple-element.119), channel_id=1, source_target_pairs={{0,4},{2,6},{4,0},{6,2},{8,12},{10,14},{12,8},{14,10},{16,20},{18,... | collective-permute-start | bytes 5505032 | tf_op jit(solution)/shard_map/ppermute | solution.py:195
  346.8 41.7 %collective-permute-start.31 = (f32[64,7168]{1,0:T(8,128)S(1)}, f32[64,7168]{1,0:T(8,128)S(1)}, u32[]{:S(2)}, u32[]{:S(2)}) collective-permute-start(f32[64,7168]{1,0:T(8,128)S(1)} %add_add_fusion.1), channel_id=1, source_target_pairs={{0,8},{2,10},{4,12},{6,14},{8,16},{10,18},{12,20},{14,22},{16,24},... | collective-permute-start | bytes 5505032 | tf_op jit(solution)/shard_map/ppermute | solution.py:194
  388.8 40.8 %collective-permute-start.33 = (f32[64,7168]{1,0:T(8,128)S(1)}, f32[64,7168]{1,0:T(8,128)S(1)}, u32[]{:S(2)}, u32[]{:S(2)}) collective-permute-start(f32[64,7168]{1,0:T(8,128)S(1)} %add_add_fusion), channel_id=1, source_target_pairs={{0,8},{2,10},{4,12},{6,14},{8,16},{10,18},{12,20},{14,22},{16,24},... | collective-permute-start | bytes 5505032 | tf_op jit(solution)/shard_map/ppermute | solution.py:194
  388.9 40.8 %collective-permute-start.32 = (f32[64,7168]{1,0:T(8,128)S(1)}, f32[64,7168]{1,0:T(8,128)S(1)}, u32[]{:S(2)}, u32[]{:S(2)}) collective-permute-start(f32[64,7168]{1,0:T(8,128)S(1)} %get-tuple-element.126), channel_id=1, source_target_pairs={{0,4},{2,6},{4,0},{6,2},{8,12},{10,14},{12,8},{14,10},{16,20},{18,... | collective-permute-start | bytes 5505032 | tf_op jit(solution)/shard_map/ppermute | solution.py:195
  (28 other events, 541.9 us)

commit v9 on v8

--- a/solution.py
+++ b/solution.py
@@ -97,7 +97,7 @@
         scratch_shapes=[pltpu.VMEM((2 * rows, 2 * depth), jnp.bfloat16)],
         compiler_params=pltpu.CompilerParams(vmem_limit_bytes=VMEM_BYTES),
         cost_estimate=pl.CostEstimate(
-            flops=3 * 2 * 2 * rows * depth * columns, bytes_accessed=8 * depth * columns, transcendentals=0
+            flops=2 * depth * columns, bytes_accessed=depth * columns // 4, transcendentals=0
         ),
         name="second_product",
     )(change, own, sib)
@@ -147,6 +147,7 @@
     keeping = keep_mask.T.astype(jnp.float32)
     change = begun - dense
     sibling = permute(hessian, "row", to_sibling)
+    dual, keeping, change = lax.optimization_barrier((dual, keeping, change))
     rest = begun - step_size * (penalty * (begun - keeping * (begun + dual) + dual)) - dense
     def piece(shift, flip):
         turn = cross(shift, flip)
@@ -179,8 +180,12 @@
 
         if window < ring - 1:
             put(near, window + 1, permute(near[window], "row", to_next))
-        if window < ring:
+        if window < ring - 1:
             put(far, window, permute(near[window], "row", to_pair))
+        elif window == ring - 1:
+            by_ring = half * 3 // 8 // 8 * 8
+            parts = {0: permute(near[window][by_ring:], "row", to_pair), 1: permute(far[window - 1][:by_ring], "row", to_next)}
+            fresh += [(parts, 0), (parts, 1)]
         if window == 0:
             rest_by[1] = (permute(rest, "col", [(y, (y + 1) % planes) for y in range(planes)]))
         for group in (0, 1) if window == 1 else (window - 1,) if 2 < window <= ring else ():
@@ -199,19 +204,25 @@
 
         group = window - 1
         if 0 <= group < ring:
+            if group == ring - 1:
+                far[group] = jnp.concatenate([parts[1], parts[0]], axis=0)
             put(product, group, first(near[group], far[group], hessian, sibling))
             if group in (1, ring - 1):
                 join(group)
         if window == 2:
             join(0)
+            fresh.append((other, 0))
         if window == 3:
             put(changed, 0, mine[0] + other[0])
         group = 0 if window == start + ring - 2 else window - 2
         if 1 <= group < ring or window == start + ring - 2:
-            if 2 <= group < ring - 1:
+            if 1 <= group < ring - 1:
                 product[group + 1], other[group] = lax.optimization_barrier((product[group + 1], other[group]))
             if group:
                 put(changed, group, mine[group] + other[group])
+            if window == ring:
+                changed[group], mine[ring - 1] = lax.optimization_barrier((changed[group], mine[ring - 1]))
+                put(other, ring - 1, sum_planes(mine[ring - 1]))
             keep, send = second(changed[group], hessian, sibling)
             if 2 <= window - 1 < ring - 1:
                 keep, product[window - 1] = lax.optimization_barrier((keep, product[window - 1]))
@@ -222,7 +233,9 @@
             rows = changed[group][:, flip * half : (flip + 1) * half]
             put(back, (group, flip), permute(rows, both, route_back(group, flip)) if group or flip else rows)
         values = [where[key] for where, key in fresh]
-        values, sibling, total, rest_by = lax.optimization_barrier((values, sibling, total, rest_by))
+        held = rest_by if window else {0: rest_by[0]}
+        values, sibling, total, held = lax.optimization_barrier((values, sibling, total, held))
+        rest_by.update(held)
         for (where, key), value in zip(fresh, values):
             where[key] = value
         if closing >= 1:

time: 435 us -> 436 us (level)
  waiting for transfers between devices: 155 us -> 138 us
  local copies, waits for them, and re-layouts: 10.3 us -> 23.7 us
  starting transfers between devices: 62.1 us -> 68.8 us
    ppermute x3, waiting for transfers between devices: 43.8 us -> 35.9 us  [per_device(): total = permute(total, 'row', to_next)]
    unnamed x50 -> x70, local copies, waits for them, and re-layouts: 2.86 us -> 10.2 us
    ppermute x3, starting transfers between devices: 1.58 us -> 6.36 us  [per_device(): put(near, window + 1, permute(near[window], 'row', to_next))]
    ppermute x4 -> x3, waiting for transfers between devices: 14.2 us -> 10.5 us  [per_device(): put(far, window, permute(near[window], 'row', to_pair))]
  transfers between devices with their start and end apart: 34 -> 35, of which waited for: 11 -> 10; matrix products, arithmetic and copies ran while one was open for 5% -> 7% of each run, Pallas kernels for 43% -> 43%
where the time goes in v9:
time: 436 us; the launch traced here: 435 us
  Pallas kernels  185 us (42%)
  waiting for transfers between devices  138 us (32%)
  starting transfers between devices  68.8 us (16%)
  local copies, waits for them, and re-layouts  23.7 us (5%)
  other arithmetic  18.1 us (4%)
    pallas_call x4, Pallas kernels, second(): pl.pallas_call(second_kernel, grid=(columns // tile,), in_specs=[pl.Block...  95.9 us
    pallas_call x4, Pallas kernels, first(): pl.pallas_call(first_kernel, grid=(rows // tile,), in_specs=[whole, whole...  89.3 us
    ppermute x1, waiting for transfers between devices, per_device(): permute(rest, 'col', [(y, (y + 1) % planes) for y in range(planes)])  37.4 us
    ppermute x3, waiting for transfers between devices, per_device(): total = permute(total, 'row', to_next)  35.9 us
    ppermute x7, starting transfers between devices, per_device(): permute(rows, both, route_back(group, flip))  26.4 us
    ppermute x7, waiting for transfers between devices, per_device(): permute(rows, both, route_back(group, flip))  23.1 us
    ppermute x7, starting transfers between devices, piece(): return permute(part, both, route(shift, flip))  19.3 us
    ppermute x7, waiting for transfers between devices, piece(): return permute(part, both, route(shift, flip))  18.1 us
  transfers between devices with their start and end apart: 35, of which 10 were waited for; matrix products, arithmetic and copies ran while one was open for 7% of the time, Pallas kernels for 43%

profile of v9, /device:TPU:0, one launch (start us, length us, event | category | flops | bytes accessed | tf_op | source)
XLA Modules:
  0.0 435.4 jit_solution(14619505409152239401)
XLA Ops:
  7.1 3.0 collective-permute-start.7
  13.1 37.4 %collective-permute-done.7 = f32[64,7168]{1,0:T(8,128)} collective-permute-done((f32[64,7168]{1,0:T(8,128)}, f32[64,7168]{1,0:T(8,128)}, u32[]{:S(2)}, u32[]{:S(2)}) %collective-permute-start.7) | collective-permute-done | bytes 1835040 | tf_op jit(solution)/shard_map/ppermute | solution.py:190
  55.4 3.1 collective-permute-start.3
  60.0 3.4 collective-permute-start.5
  63.5 3.5 collective-permute-start.6
  67.0 22.3 %first_product.4 = f32[2,128,896]{2,1,0:T(8,128)S(1)} custom-call(f32[64,7168]{1,0:T(8,128)S(1)} %bitcast_subtract_fusion.1.near_ref, f32[64,7168]{1,0:T(8,128)} %collective-permute-done.1.far_ref, f32[896,7168]{1,0:T(8,128)} %own_ref.15, f32[896,7168]{1,0:T(8,128)} %collective-permute-done.2.sib_ref), custom_call_target="tpu_custom_call" | custom-call | flops 9865003008 | bytes 51380224 | tf_op jit(solution)/shard_map/first_product/pallas_call | solution.py:53
  89.4 16.0 %collective-permute-done.5 = f32[2,64,896]{2,1,0:T(8,128)S(1)} collective-permute-done((f32[2,64,896]{2,1,0:T(8,128)S(1)}, f32[2,64,896]{2,1,0:T(8,128)S(1)}, u32[]{:S(2)}, u32[]{:S(2)}) %collective-permute-start.5) | collective-permute-done | bytes 458784 | tf_op jit(solution)/shard_map/ppermute | solution.py:161
  113.8 22.4 %first_product.5 = f32[2,128,896]{2,1,0:T(8,128)S(1)} custom-call(f32[64,7168]{1,0:T(8,128)} %collective-permute-done.near_ref, f32[64,7168]{1,0:T(8,128)S(1)} %copy-done.6, f32[896,7168]{1,0:T(8,128)} %own_ref.15, f32[896,7168]{1,0:T(8,128)} %collective-permute-done.2.sib_ref), custom_call_target="tpu_custom_call" | custom-call | flops 9865003008 | bytes 51380224 | tf_op jit(solution)/shard_map/first_product/pallas_call | solution.py:53
  138.0 10.5 %collective-permute-done.10.far_ref = f32[64,7168]{1,0:T(8,128)} collective-permute-done((f32[64,7168]{1,0:T(8,128)}, f32[64,7168]{1,0:T(8,128)}, u32[]{:S(2)}, u32[]{:S(2)}) %collective-permute-start.10) | collective-permute-done | bytes 1835040 | tf_op jit(solution)/shard_map/ppermute | solution.py:184
  148.4 2.8 collective-permute-done.9.near_ref
  154.3 3.5 collective-permute-start.16
  161.6 22.8 %first_product.6 = f32[2,128,896]{2,1,0:T(8,128)S(1)} custom-call(f32[64,7168]{1,0:T(8,128)} %collective-permute-done.3.near_ref, f32[64,7168]{1,0:T(8,128)} %collective-permute-done.10.far_ref, f32[896,7168]{1,0:T(8,128)} %own_ref.15, f32[896,7168]{1,0:T(8,128)} %collective-permute-done.2.sib_ref), custom_call_target="tpu_custom_call" | custom-call | flops 9865003008 | bytes 51380224 | tf_op jit(solution)/shard_map/first_product/pallas_call | solution.py:53
  190.3 8.5 %collective-permute-start.17 = (f32[2,64,896]{2,1,0:T(8,128)}, f32[2,64,896]{2,1,0:T(8,128)}, u32[]{:S(2)}, u32[]{:S(2)}) collective-permute-start(f32[2,64,896]{2,1,0:T(8,128)} %get-tuple-element.167), channel_id=1, source_target_pairs={{8,0},{10,2},{12,4},{14,6},{17,9},{19,11},{21,13},{23,15},{25,17},... | collective-permute-start | bytes 1376264 | tf_op jit(solution)/shard_map/ppermute | solution.py:234
  198.9 23.8 %second_product.4 = (f32[64,7168]{1,0:T(8,128)S(1)}, f32[64,7168]{1,0:T(8,128)S(1)}) custom-call(f32[2,128,896]{2,1,0:T(8,128)S(1)} %add.248.change_ref, f32[896,7168]{1,0:T(8,128)} %own_ref.15, f32[896,7168]{1,0:T(8,128)} %collective-permute-done.2.sib_ref), custom_call_target="tpu_custom_call" | custom-call | flops 12845056 | bytes 1605632 | tf_op jit(solution)/shard_map/second_product/pallas_call | solution.py:91
  227.5 5.6 %collective-permute-start.22 = (f32[2,64,896]{2,1,0:T(8,128)S(1)}, f32[2,64,896]{2,1,0:T(8,128)S(1)}, u32[]{:S(2)}, u32[]{:S(2)}) collective-permute-start(f32[2,64,896]{2,1,0:T(8,128)S(1)} %fusion.12), channel_id=1, source_target_pairs={{0,28},{2,30},{4,24},{6,26},{9,5},{11,7},{13,1},{15,3},{17,13},{19... | collective-permute-start | bytes 1376264 | tf_op jit(solution)/shard_map/ppermute | solution.py:161
  236.2 21.8 %first_product.7 = f32[2,128,896]{2,1,0:T(8,128)S(1)} custom-call(f32[64,7168]{1,0:T(8,128)S(1)} %collective-permute-done.9.near_ref, f32[64,7168]{1,0:T(8,128)S(1)} %pad_maximum_fusion.far_ref, f32[896,7168]{1,0:T(8,128)} %own_ref.15, f32[896,7168]{1,0:T(8,128)} %collective-permute-done.2.sib_ref), custom_call_target="tpu_custom_call" | custom-call | flops 9865003008 | bytes 51380224 | tf_op jit(solution)/shard_map/first_product/pallas_call | solution.py:53
  259.1 8.6 %collective-permute-start.24 = (f32[2,64,896]{2,1,0:T(8,128)S(1)}, f32[2,64,896]{2,1,0:T(8,128)S(1)}, u32[]{:S(2)}, u32[]{:S(2)}) collective-permute-start(f32[2,64,896]{2,1,0:T(8,128)S(1)} %get-tuple-element.165), channel_id=1, source_target_pairs={{17,1},{19,3},{21,5},{23,7},{25,9},{27,11},{29,13},{31,15},{0,16},... | collective-permute-start | bytes 1376264 | tf_op jit(solution)/shard_map/ppermute | solution.py:234
  267.8 24.6 %second_product.5 = (f32[64,7168]{1,0:T(8,128)S(1)}, f32[64,7168]{1,0:T(8,128)}) custom-call(f32[2,128,896]{2,1,0:T(8,128)S(1)} %add.257.change_ref, f32[896,7168]{1,0:T(8,128)} %own_ref.15, f32[896,7168]{1,0:T(8,128)} %collective-permute-done.2.sib_ref), custom_call_target="tpu_custom_call" | custom-call | flops 12845056 | bytes 1605632 | tf_op jit(solution)/shard_map/second_product/pallas_call | solution.py:91
  298.1 3.3 collective-permute-start.29
  305.6 23.8 %second_product.6 = (f32[64,7168]{1,0:T(8,128)S(1)}, f32[64,7168]{1,0:T(8,128)S(1)}) custom-call(f32[2,128,896]{2,1,0:T(8,128)S(1)} %add.265.change_ref, f32[896,7168]{1,0:T(8,128)} %own_ref.15, f32[896,7168]{1,0:T(8,128)} %collective-permute-done.2.sib_ref), custom_call_target="tpu_custom_call" | custom-call | flops 12845056 | bytes 1605632 | tf_op jit(solution)/shard_map/second_product/pallas_call | solution.py:91
  329.4 23.1 %collective-permute-done.29 = f32[2,64,896]{2,1,0:T(8,128)} collective-permute-done((f32[2,64,896]{2,1,0:T(8,128)}, f32[2,64,896]{2,1,0:T(8,128)}, u32[]{:S(2)}, u32[]{:S(2)}) %collective-permute-start.29) | collective-permute-done | bytes 458784 | tf_op jit(solution)/shard_map/ppermute | solution.py:234
  355.3 23.7 %second_product.7 = (f32[64,7168]{1,0:T(8,128)S(1)}, f32[64,7168]{1,0:T(8,128)S(1)}) custom-call(f32[2,128,896]{2,1,0:T(8,128)S(1)} %add.249.change_ref, f32[896,7168]{1,0:T(8,128)} %own_ref.15, f32[896,7168]{1,0:T(8,128)} %collective-permute-done.2.sib_ref), custom_call_target="tpu_custom_call" | custom-call | flops 12845056 | bytes 1605632 | tf_op jit(solution)/shard_map/second_product/pallas_call | solution.py:91
  384.7 7.6 %collective-permute-done.31 = f32[64,7168]{1,0:T(8,128)S(1)} collective-permute-done((f32[64,7168]{1,0:T(8,128)S(1)}, f32[64,7168]{1,0:T(8,128)S(1)}, u32[]{:S(2)}, u32[]{:S(2)}) %collective-permute-start.31) | collective-permute-done | bytes 1835040 | tf_op jit(solution)/shard_map/ppermute | solution.py:200
  397.5 33.5 %collective-permute-done.34 = f32[64,7168]{1,0:T(8,128)S(1)} collective-permute-done((f32[64,7168]{1,0:T(8,128)S(1)}, f32[64,7168]{1,0:T(8,128)S(1)}, u32[]{:S(2)}, u32[]{:S(2)}) %collective-permute-start.34) | collective-permute-done | bytes 1835040 | tf_op jit(solution)/shard_map/ppermute | solution.py:199
  (174 shorter events, 75.0 us)
Async XLA Ops:
  0.7 54.2 %collective-permute-start.2 = (f32[896,7168]{1,0:T(8,128)}, f32[896,7168]{1,0:T(8,128)}, u32[]{:S(2)}, u32[]{:S(2)}) collective-permute-start(f32[896,7168]{1,0:T(8,128)} %own_ref.15), channel_id=1, source_target_pairs={{0,2},{2,0},{4,6},{6,4},{8,10},{10,8},{12,14},{14,12},{16,18},{18,... | collective-permute-start | bytes 77070344 | tf_op jit(solution)/shard_map/ppermute | solution.py:149
  7.1 43.5 %collective-permute-start.7 = (f32[64,7168]{1,0:T(8,128)}, f32[64,7168]{1,0:T(8,128)}, u32[]{:S(2)}, u32[]{:S(2)}) collective-permute-start(f32[64,7168]{1,0:T(8,128)} %bitcast_subtract_fusion), channel_id=1, source_target_pairs={{0,1},{1,0},{2,3},{3,2},{4,5},{5,4},{6,7},{7,6},{8,9},{9,8},{10,11... | collective-permute-start | bytes 5505032 | tf_op jit(solution)/shard_map/ppermute | solution.py:190
  10.0 42.3 %collective-permute-start.1 = (f32[64,7168]{1,0:T(8,128)S(1)}, f32[64,7168]{1,0:T(8,128)}, u32[]{:S(2)}, u32[]{:S(2)}) collective-permute-start(f32[64,7168]{1,0:T(8,128)S(1)} %bitcast_subtract_fusion.1.near_ref), channel_id=1, source_target_pairs={{0,4},{2,6},{4,0},{6,2},{8,12},{10,14},{12,8},{14,10},{16,20},{18,... | collective-permute-start | bytes 5505032 | tf_op jit(solution)/shard_map/ppermute | solution.py:184
  11.5 43.3 %collective-permute-start = (f32[64,7168]{1,0:T(8,128)S(1)}, f32[64,7168]{1,0:T(8,128)}, u32[]{:S(2)}, u32[]{:S(2)}) collective-permute-start(f32[64,7168]{1,0:T(8,128)S(1)} %bitcast_subtract_fusion.1.near_ref), channel_id=1, source_target_pairs={{0,8},{2,10},{4,12},{6,14},{8,16},{10,18},{12,20},{14,22},{16,24},... | collective-permute-start | bytes 5505032 | tf_op jit(solution)/shard_map/ppermute | solution.py:182
  51.7 37.7 %collective-permute-start.8 = (f32[2,64,896]{2,1,0:T(8,128)S(1)}, f32[2,64,896]{2,1,0:T(8,128)S(1)}, u32[]{:S(2)}, u32[]{:S(2)}) collective-permute-start(f32[2,64,896]{2,1,0:T(8,128)S(1)} %fusion.8), channel_id=1, source_target_pairs={{1,13},{3,15},{5,9},{7,11},{8,20},{10,22},{12,16},{14,18},{16,28},... | collective-permute-start | bytes 1376264 | tf_op jit(solution)/shard_map/ppermute | solution.py:161
  54.9 52.7 %collective-permute-start.4 = (f32[64,7168]{1,0:T(8,128)}, f32[64,7168]{1,0:T(8,128)S(1)}, u32[]{:S(2)}, u32[]{:S(2)}) collective-permute-start(f32[64,7168]{1,0:T(8,128)} %collective-permute-done.near_ref), channel_id=1, source_target_pairs={{0,4},{2,6},{4,0},{6,2},{8,12},{10,14},{12,8},{14,10},{16,20},{18,... | collective-permute-start | bytes 5505032 | tf_op jit(solution)/shard_map/ppermute | solution.py:184
  55.4 53.4 %collective-permute-start.3 = (f32[64,7168]{1,0:T(8,128)}, f32[64,7168]{1,0:T(8,128)}, u32[]{:S(2)}, u32[]{:S(2)}) collective-permute-start(f32[64,7168]{1,0:T(8,128)} %collective-permute-done.near_ref), channel_id=1, source_target_pairs={{0,8},{2,10},{4,12},{6,14},{8,16},{10,18},{12,20},{14,22},{16,24},... | collective-permute-start | bytes 5505032 | tf_op jit(solution)/shard_map/ppermute | solution.py:182
  60.0 45.4 %collective-permute-start.5 = (f32[2,64,896]{2,1,0:T(8,128)S(1)}, f32[2,64,896]{2,1,0:T(8,128)S(1)}, u32[]{:S(2)}, u32[]{:S(2)}) collective-permute-start(f32[2,64,896]{2,1,0:T(8,128)S(1)} %fusion.6), channel_id=1, source_target_pairs={{0,4},{2,6},{4,0},{6,2},{8,12},{10,14},{12,8},{14,10},{17,21},{19,... | collective-permute-start | bytes 1376264 | tf_op jit(solution)/shard_map/ppermute | solution.py:161
  63.5 44.0 %collective-permute-start.6 = (f32[2,64,896]{2,1,0:T(8,128)S(1)}, f32[2,64,896]{2,1,0:T(8,128)S(1)}, u32[]{:S(2)}, u32[]{:S(2)}) collective-permute-start(f32[2,64,896]{2,1,0:T(8,128)S(1)} %fusion.7), channel_id=1, source_target_pairs={{0,8},{2,10},{4,12},{6,14},{9,17},{11,19},{13,21},{15,23},{17,25},... | collective-permute-start | bytes 1376264 | tf_op jit(solution)/shard_map/ppermute | solution.py:161
  108.8 39.7 %collective-permute-start.10 = (f32[64,7168]{1,0:T(8,128)}, f32[64,7168]{1,0:T(8,128)}, u32[]{:S(2)}, u32[]{:S(2)}) collective-permute-start(f32[64,7168]{1,0:T(8,128)} %collective-permute-done.3.near_ref), channel_id=1, source_target_pairs={{0,4},{2,6},{4,0},{6,2},{8,12},{10,14},{12,8},{14,10},{16,20},{18,... | collective-permute-start | bytes 5505032 | tf_op jit(solution)/shard_map/ppermute | solution.py:184
  110.2 41.0 %collective-permute-start.9 = (f32[64,7168]{1,0:T(8,128)}, f32[64,7168]{1,0:T(8,128)S(1)}, u32[]{:S(2)}, u32[]{:S(2)}) collective-permute-start(f32[64,7168]{1,0:T(8,128)} %collective-permute-done.3.near_ref), channel_id=1, source_target_pairs={{0,8},{2,10},{4,12},{6,14},{8,16},{10,18},{12,20},{14,22},{16,24},... | collective-permute-start | bytes 5505032 | tf_op jit(solution)/shard_map/ppermute | solution.py:182
  136.3 50.5 %collective-permute-start.14 = (f32[2,128,896]{2,1,0:T(8,128)S(1)}, f32[2,128,896]{2,1,0:T(8,128)S(1)}, u32[]{:S(2)}, u32[]{:S(2)}) collective-permute-start(f32[2,128,896]{2,1,0:T(8,128)S(1)} %maximum_add_fusion), channel_id=1, source_target_pairs={{0,1},{1,0},{2,3},{3,2},{4,5},{5,4},{6,7},{7,6},{8,9},{9,8},{10,11... | collective-permute-start | bytes 2752520 | tf_op jit(solution)/shard_map/ppermute | solution.py:164
  157.8 65.0 %collective-permute-start.15 = (f32[2,64,896]{2,1,0:T(8,128)}, f32[2,64,896]{2,1,0:T(8,128)}, u32[]{:S(2)}, u32[]{:S(2)}) collective-permute-start(f32[2,64,896]{2,1,0:T(8,128)} %fusion.9), channel_id=1, source_target_pairs={{1,17},{3,19},{5,21},{7,23},{9,25},{11,27},{13,29},{15,31},{16,0},... | collective-permute-start | bytes 1376264 | tf_op jit(solution)/shard_map/ppermute | solution.py:161
  160.2 65.0 %collective-permute-start.12 = (f32[40,7168]{1,0:T(8,128)}, f32[40,7168]{1,0:T(8,128)}, u32[]{:S(2)}, u32[]{:S(2)}) collective-permute-start(f32[40,7168]{1,0:T(8,128)} %slice.54), channel_id=1, source_target_pairs={{0,4},{2,6},{4,0},{6,2},{8,12},{10,14},{12,8},{14,10},{16,20},{18,... | collective-permute-start | bytes 3440648 | tf_op jit(solution)/shard_map/ppermute | solution.py:187
  186.8 38.4 %collective-permute-start.13 = (f32[24,7168]{1,0:T(8,128)}, f32[24,7168]{1,0:T(8,128)S(1)}, u32[]{:S(2)}, u32[]{:S(2)}) collective-permute-start(f32[24,7168]{1,0:T(8,128)} %slice.55), channel_id=1, source_target_pairs={{0,8},{2,10},{4,12},{6,14},{8,16},{10,18},{12,20},{14,22},{16,24},... | collective-permute-start | bytes 2064392 | tf_op jit(solution)/shard_map/ppermute | solution.py:187
  188.2 37.0 %collective-permute-start.18 = (f32[2,64,896]{2,1,0:T(8,128)}, f32[2,64,896]{2,1,0:T(8,128)}, u32[]{:S(2)}, u32[]{:S(2)}) collective-permute-start(f32[2,64,896]{2,1,0:T(8,128)} %get-tuple-element.166), channel_id=1, source_target_pairs={{13,0},{15,2},{9,4},{11,6},{20,9},{22,11},{16,13},{18,15},{28,17},... | collective-permute-start | bytes 1376264 | tf_op jit(solution)/shard_map/ppermute | solution.py:234
  234.4 58.0 %collective-permute-start.19 = (f32[64,7168]{1,0:T(8,128)S(1)}, f32[64,7168]{1,0:T(8,128)S(1)}, u32[]{:S(2)}, u32[]{:S(2)}) collective-permute-start(f32[64,7168]{1,0:T(8,128)S(1)} %get-tuple-element.108), channel_id=1, source_target_pairs={{0,4},{2,6},{4,0},{6,2},{8,12},{10,14},{12,8},{14,10},{16,20},{18,... | collective-permute-start | bytes 5505032 | tf_op jit(solution)/shard_map/ppermute | solution.py:200
  292.5 60.0 %collective-permute-start.26 = (f32[64,7168]{1,0:T(8,128)}, f32[64,7168]{1,0:T(8,128)}, u32[]{:S(2)}, u32[]{:S(2)}) collective-permute-start(f32[64,7168]{1,0:T(8,128)} %get-tuple-element.120), channel_id=1, source_target_pairs={{0,4},{2,6},{4,0},{6,2},{8,12},{10,14},{12,8},{14,10},{16,20},{18,... | collective-permute-start | bytes 5505032 | tf_op jit(solution)/shard_map/ppermute | solution.py:200
  294.5 58.0 %collective-permute-start.30 = (f32[64,7168]{1,0:T(8,128)}, f32[64,7168]{1,0:T(8,128)}, u32[]{:S(2)}, u32[]{:S(2)}) collective-permute-start(f32[64,7168]{1,0:T(8,128)} %add.266), channel_id=1, source_target_pairs={{0,8},{2,10},{4,12},{6,14},{8,16},{10,18},{12,20},{14,22},{16,24},... | collective-permute-start | bytes 5505032 | tf_op jit(solution)/shard_map/ppermute | solution.py:199
  298.1 54.4 %collective-permute-start.29 = (f32[2,64,896]{2,1,0:T(8,128)}, f32[2,64,896]{2,1,0:T(8,128)}, u32[]{:S(2)}, u32[]{:S(2)}) collective-permute-start(f32[2,64,896]{2,1,0:T(8,128)} %get-tuple-element.160), channel_id=1, source_target_pairs={{4,0},{6,2},{0,4},{2,6},{12,8},{14,10},{8,12},{10,14},{21,17},{23,... | collective-permute-start | bytes 1376264 | tf_op jit(solution)/shard_map/ppermute | solution.py:234
  301.6 50.9 %collective-permute-start.28 = (f32[2,64,896]{2,1,0:T(8,128)S(1)}, f32[2,64,896]{2,1,0:T(8,128)}, u32[]{:S(2)}, u32[]{:S(2)}) collective-permute-start(f32[2,64,896]{2,1,0:T(8,128)S(1)} %get-tuple-element.162), channel_id=1, source_target_pairs={{28,1},{30,3},{24,5},{26,7},{5,8},{7,10},{1,12},{3,14},{13,16},{15... | collective-permute-start | bytes 1376264 | tf_op jit(solution)/shard_map/ppermute | solution.py:234
  303.1 49.4 %collective-permute-start.27 = (f32[2,64,896]{2,1,0:T(8,128)S(1)}, f32[2,64,896]{2,1,0:T(8,128)}, u32[]{:S(2)}, u32[]{:S(2)}) collective-permute-start(f32[2,64,896]{2,1,0:T(8,128)S(1)} %get-tuple-element.163), channel_id=1, source_target_pairs={{25,1},{27,3},{29,5},{31,7},{0,8},{2,10},{4,12},{6,14},{8,16},{10,... | collective-permute-start | bytes 1376264 | tf_op jit(solution)/shard_map/ppermute | solution.py:234
  352.5 39.8 %collective-permute-start.31 = (f32[64,7168]{1,0:T(8,128)S(1)}, f32[64,7168]{1,0:T(8,128)S(1)}, u32[]{:S(2)}, u32[]{:S(2)}) collective-permute-start(f32[64,7168]{1,0:T(8,128)S(1)} %get-tuple-element.137), channel_id=1, source_target_pairs={{0,4},{2,6},{4,0},{6,2},{8,12},{10,14},{12,8},{14,10},{16,20},{18,... | collective-permute-start | bytes 5505032 | tf_op jit(solution)/shard_map/ppermute | solution.py:200
  355.2 39.5 %collective-permute-start.32 = (f32[64,7168]{1,0:T(8,128)S(1)}, f32[64,7168]{1,0:T(8,128)S(1)}, u32[]{:S(2)}, u32[]{:S(2)}) collective-permute-start(f32[64,7168]{1,0:T(8,128)S(1)} %add_add_fusion.1), channel_id=1, source_target_pairs={{0,8},{2,10},{4,12},{6,14},{8,16},{10,18},{12,20},{14,22},{16,24},... | collective-permute-start | bytes 5505032 | tf_op jit(solution)/shard_map/ppermute | solution.py:199
  (39 other events, 671.0 us)

commit v10 on v6

--- a/solution.py
+++ b/solution.py
@@ -148,22 +148,23 @@
     change = begun - dense
     sibling = permute(hessian, "row", to_sibling)
     rest = begun - step_size * (penalty * (begun - keeping * (begun + dual) + dual)) - dense
-    def piece(shift, flip):
-        turn = cross(shift, flip)
+    def cut(source, shift, flip):
         chip = ((place + shift) % ring) * PAIR + (pair ^ flip)
-        at = jnp.clip(chip - ((plane - turn) % planes) * per_plane, 0, per_plane - 1)
-        part = lax.dynamic_slice_in_dim(rest_by[turn], at * CORES * depth, CORES * depth, 1)
+        at = jnp.clip(chip - ((plane - cross(shift, flip)) % planes) * per_plane, 0, per_plane - 1)
+        part = lax.dynamic_slice_in_dim(source, at * CORES * depth, CORES * depth, 1)
         part = part.reshape(half, CORES, depth)
         part = jnp.where(core == 0, part, part[:, ::-1]).transpose(1, 0, 2)
-        if shift == 0 and flip == 0:
-            return jnp.where(chip // per_plane == plane, part, 0.0)
-        return permute(part, both, route(shift, flip))
+        return part if shift or flip else jnp.where(chip // per_plane == plane, part, 0.0)
+
+    def piece(shift, flip):
+        part = cuts[shift, flip]
+        return permute(part, both, route(shift, flip)) if shift or flip else part
 
     def sum_planes(part):
         others = [permute(part, "col", [(y, (y + turn) % planes) for y in range(planes)]) for turn in range(1, planes)]
         return functools.reduce(jnp.add, others) if others else jnp.zeros_like(part)
 
-    rest_by = {0: rest}
+    cuts = {}
     near, far, added = {0: change}, {}, {}
     product, mine, other, changed, kept, sent, swapped, back = {}, {}, {}, {}, {}, {}, {}, {}
     total = None
@@ -184,8 +185,12 @@
         if window < ring:
             put(far, window, permute(near[window], "row", to_pair))
         if window == 0:
-            rest_by[1] = (permute(rest, "col", [(y, (y + 1) % planes) for y in range(planes)]))
-        elif window < ring:
+            rest_across = permute(rest, "col", [(y, (y + 1) % planes) for y in range(planes)])
+            cuts.update({(shift, 0): cut(rest, shift, 0) for shift in range(ring)})
+            cuts[0, 1] = cut(rest, 0, 1)
+        if window == 1:
+            cuts.update({(shift, 1): cut(rest_across, shift, 1) for shift in range(1, ring)})
+        if 0 < window < ring:
             for flip in range(PAIR):
                 added[window, flip] = piece(window, flip)
                 if window == ring - 1:
@@ -222,7 +227,9 @@
             rows = changed[group][:, flip * half : (flip + 1) * half]
             put(back, (group, flip), permute(rows, both, route_back(group, flip)) if group or flip else rows)
         values = [where[key] for where, key in fresh]
-        values, sibling, total, rest_by = lax.optimization_barrier((values, sibling, total, rest_by))
+        waiting = {key: part for key, part in cuts.items() if key[0] > window or not window}
+        values, sibling, total, waiting, rest_across = lax.optimization_barrier((values, sibling, total, waiting, rest_across))
+        cuts.update(waiting)
         for (where, key), value in zip(fresh, values):
             where[key] = value
         if closing >= 1:

time: 424 us -> 416 us (0.981)
  starting transfers between devices: 92.3 us -> 72.4 us
  waiting for transfers between devices: 114 us -> 125 us
    ppermute x7, waiting for transfers between devices: 0.02 us -> 16.6 us  [piece(): return permute(part, both, route(shift, flip)) if shift or flip else part]
    ppermute x4, starting transfers between devices: 13.4 us -> 2.77 us  [sum_planes(): permute(part, 'col', [(y, (y + turn) % planes) for y in range(planes)])]
    ppermute x4, waiting for transfers between devices: 9.01 us -> 0.01 us  [sum_planes(): permute(part, 'col', [(y, (y + turn) % planes) for y in range(planes)])]
    ppermute x7, waiting for transfers between devices: 23.4 us -> 32.1 us  [per_device(): permute(rows, both, route_back(group, flip))]
    ppermute x7, starting transfers between devices: 20.1 us -> 13.1 us  [piece(): return permute(part, both, route(shift, flip)) if shift or flip else part]
    ppermute x3, waiting for transfers between devices: 5.46 us -> 0.01 us  [per_device(): total = permute(total, 'row', to_next)]
    ppermute x1, waiting for transfers between devices: 37.9 us -> 33.3 us  [per_device(): permute(rest, 'col', [(y, (y + 1) % planes) for y in range(planes)])]
  transfers between devices with their start and end apart: 34 -> 34, of which waited for: 13 -> 9; matrix products, arithmetic and copies ran while one was open for 5% -> 5% of each run, Pallas kernels for 44% -> 44%
where the time goes in v10:
time: 416 us; the launch traced here: 415 us
  Pallas kernels  184 us (44%)
  waiting for transfers between devices  125 us (30%)
  starting transfers between devices  72.4 us (17%)
  other arithmetic  21 us (5%)
  local copies, waits for them, and re-layouts  11.9 us (3%)
    pallas_call x4, Pallas kernels, second(): pl.pallas_call(second_kernel, grid=(columns // tile,), in_specs=[pl.Block...  95.7 us
    pallas_call x4, Pallas kernels, first(): pl.pallas_call(first_kernel, grid=(rows // tile,), in_specs=[whole, whole...  88.1 us
    ppermute x7, starting transfers between devices, per_device(): permute(rows, both, route_back(group, flip))  37.9 us
    ppermute x1, waiting for transfers between devices, per_device(): permute(rest, 'col', [(y, (y + 1) % planes) for y in range(planes)])  33.3 us
    ppermute x7, waiting for transfers between devices, per_device(): permute(rows, both, route_back(group, flip))  32.1 us
    ppermute x4, waiting for transfers between devices, per_device(): put(swapped, closing % ring, permute(sent[closing % ring], 'row', to_pair))  24 us
    ppermute x7, waiting for transfers between devices, piece(): return permute(part, both, route(shift, flip)) if shift or flip else part  16.6 us
    ppermute x7, starting transfers between devices, piece(): return permute(part, both, route(shift, flip)) if shift or flip else part  13.1 us
  transfers between devices with their start and end apart: 34, of which 9 were waited for; matrix products, arithmetic and copies ran while one was open for 5% of the time, Pallas kernels for 44%

profile of v10, /device:TPU:0, one launch (start us, length us, event | category | flops | bytes accessed | tf_op | source)
XLA Modules:
  0.0 415.3 jit_solution(3932476778799494275)
XLA Ops:
  1.1 4.9 %fusion.4 = (f32[64,7168]{1,0:T(8,128)}, f32[64,7168]{1,0:T(8,128)S(1)}) fusion(f32[7168,64]{0,1:T(8,128)} %param.8, f32[7168,64]{0,1:T(8,128)} %param.6, f32[7168,64]{0,1:T(8,128)} %param.7, s32[7168,64]{0,1:T(8,128)} %param.9), kind=kLoop, calls=%fused_computation.7 | loop fusion | flops 4128768 | bytes 11010048 | tf_op jit(solution)/shard_map/sub | solution.py:150
  6.1 2.5 collective-permute-start.3
  16.3 33.3 %collective-permute-done.3 = f32[64,7168]{1,0:T(8,128)} collective-permute-done((f32[64,7168]{1,0:T(8,128)}, f32[64,7168]{1,0:T(8,128)}, u32[]{:S(2)}, u32[]{:S(2)}) %collective-permute-start.3) | collective-permute-done | bytes 1835040 | tf_op jit(solution)/shard_map/ppermute | solution.py:188
  50.8 3.1 collective-permute-done.near_ref
  54.5 3.2 collective-permute-start.9
  61.5 22.3 %first_product.4 = f32[2,128,896]{2,1,0:T(8,128)S(1)} custom-call(f32[64,7168]{1,0:T(8,128)S(1)} %get-tuple-element.150.near_ref, f32[64,7168]{1,0:T(8,128)} %collective-permute-done.1.far_ref, f32[896,7168]{1,0:T(8,128)} %own_ref.15, f32[896,7168]{1,0:T(8,128)} %collective-permute-done.2.sib_ref), custom_call_target="tpu_custom_call" | custom-call | flops 9865003008 | bytes 51380224 | tf_op jit(solution)/shard_map/first_product/pallas_call | solution.py:53
  83.8 11.4 %collective-permute-done.5.far_ref = f32[64,7168]{1,0:T(8,128)S(1)} collective-permute-done((f32[64,7168]{1,0:T(8,128)}, f32[64,7168]{1,0:T(8,128)S(1)}, u32[]{:S(2)}, u32[]{:S(2)}) %collective-permute-start.5) | collective-permute-done | bytes 1835040 | tf_op jit(solution)/shard_map/ppermute | solution.py:186
  96.4 3.0 collective-permute-done.4.near_ref
  102.4 22.3 %first_product.5 = f32[2,128,896]{2,1,0:T(8,128)S(1)} custom-call(f32[64,7168]{1,0:T(8,128)} %collective-permute-done.near_ref, f32[64,7168]{1,0:T(8,128)S(1)} %copy-done.1, f32[896,7168]{1,0:T(8,128)} %own_ref.15, f32[896,7168]{1,0:T(8,128)} %collective-permute-done.2.sib_ref), custom_call_target="tpu_custom_call" | custom-call | flops 9865003008 | bytes 51380224 | tf_op jit(solution)/shard_map/first_product/pallas_call | solution.py:53
  126.6 2.4 collective-permute-start.8
  130.3 16.6 %collective-permute-done.8 = f32[2,64,896]{2,1,0:T(8,128)S(1)} collective-permute-done((f32[2,64,896]{2,1,0:T(8,128)S(1)}, f32[2,64,896]{2,1,0:T(8,128)S(1)}, u32[]{:S(2)}, u32[]{:S(2)}) %collective-permute-start.8) | collective-permute-done | bytes 458784 | tf_op jit(solution)/shard_map/ppermute | solution.py:161
  153.2 21.8 %first_product.6 = f32[2,128,896]{2,1,0:T(8,128)S(1)} custom-call(f32[64,7168]{1,0:T(8,128)S(1)} %collective-permute-done.4.near_ref, f32[64,7168]{1,0:T(8,128)S(1)} %collective-permute-done.7.far_ref, f32[896,7168]{1,0:T(8,128)} %own_ref.15, f32[896,7168]{1,0:T(8,128)} %collective-permute-done.2.sib_ref), custom_call_target="tpu_custom_call" | custom-call | flops 9865003008 | bytes 51380224 | tf_op jit(solution)/shard_map/first_product/pallas_call | solution.py:53
  175.1 5.2 %collective-permute-start.18 = (f32[2,64,896]{2,1,0:T(8,128)S(1)}, f32[2,64,896]{2,1,0:T(8,128)S(1)}, u32[]{:S(2)}, u32[]{:S(2)}) collective-permute-start(f32[2,64,896]{2,1,0:T(8,128)S(1)} %slice.64), channel_id=1, source_target_pairs={{8,0},{10,2},{12,4},{14,6},{17,9},{19,11},{21,13},{23,15},{25,17},... | collective-permute-start | bytes 1376264 | tf_op jit(solution)/shard_map/ppermute | solution.py:228
  181.6 23.7 %second_product.4 = (f32[64,7168]{1,0:T(8,128)S(1)}, f32[64,7168]{1,0:T(8,128)S(1)}) custom-call(f32[2,128,896]{2,1,0:T(8,128)S(1)} %add.259.change_ref, f32[896,7168]{1,0:T(8,128)} %own_ref.15, f32[896,7168]{1,0:T(8,128)} %collective-permute-done.2.sib_ref), custom_call_target="tpu_custom_call" | custom-call | flops 9865003008 | bytes 51380224 | tf_op jit(solution)/shard_map/second_product/pallas_call | solution.py:91
  208.4 25.5 %collective-permute-start.21 = (f32[2,64,896]{2,1,0:T(8,128)S(1)}, f32[2,64,896]{2,1,0:T(8,128)S(1)}, u32[]{:S(2)}, u32[]{:S(2)}) collective-permute-start(f32[2,64,896]{2,1,0:T(8,128)S(1)} %get-tuple-element.164), channel_id=1, source_target_pairs={{17,1},{19,3},{21,5},{23,7},{25,9},{27,11},{29,13},{31,15},{0,16},... | collective-permute-start | bytes 1376264 | tf_op jit(solution)/shard_map/ppermute | solution.py:228
  235.0 21.8 %first_product.7 = f32[2,128,896]{2,1,0:T(8,128)S(1)} custom-call(f32[64,7168]{1,0:T(8,128)S(1)} %collective-permute-done.6.near_ref, f32[64,7168]{1,0:T(8,128)S(1)} %collective-permute-done.12.far_ref, f32[896,7168]{1,0:T(8,128)} %own_ref.15, f32[896,7168]{1,0:T(8,128)} %collective-permute-done.2.sib_ref), custom_call_target="tpu_custom_call" | custom-call | flops 9865003008 | bytes 51380224 | tf_op jit(solution)/shard_map/first_product/pallas_call | solution.py:53
  258.1 23.7 %second_product.5 = (f32[64,7168]{1,0:T(8,128)S(1)}, f32[64,7168]{1,0:T(8,128)S(1)}) custom-call(f32[2,128,896]{2,1,0:T(8,128)S(1)} %add.261.change_ref, f32[896,7168]{1,0:T(8,128)} %own_ref.15, f32[896,7168]{1,0:T(8,128)} %collective-permute-done.2.sib_ref), custom_call_target="tpu_custom_call" | custom-call | flops 9865003008 | bytes 51380224 | tf_op jit(solution)/shard_map/second_product/pallas_call | solution.py:91
  289.9 24.6 %second_product.6 = (f32[64,7168]{1,0:T(8,128)S(1)}, f32[64,7168]{1,0:T(8,128)}) custom-call(f32[2,128,896]{2,1,0:T(8,128)S(1)} %add.263.change_ref, f32[896,7168]{1,0:T(8,128)} %own_ref.15, f32[896,7168]{1,0:T(8,128)} %collective-permute-done.2.sib_ref), custom_call_target="tpu_custom_call" | custom-call | flops 9865003008 | bytes 51380224 | tf_op jit(solution)/shard_map/second_product/pallas_call | solution.py:91
  314.6 14.0 %collective-permute-done.26 = f32[2,64,896]{2,1,0:T(8,128)S(1)} collective-permute-done((f32[2,64,896]{2,1,0:T(8,128)S(1)}, f32[2,64,896]{2,1,0:T(8,128)S(1)}, u32[]{:S(2)}, u32[]{:S(2)}) %collective-permute-start.26) | collective-permute-done | bytes 458784 | tf_op jit(solution)/shard_map/ppermute | solution.py:228
  330.8 4.1 collective-permute-start.31
  338.3 23.7 %second_product.7 = (f32[64,7168]{1,0:T(8,128)S(1)}, f32[64,7168]{1,0:T(8,128)S(1)}) custom-call(f32[2,128,896]{2,1,0:T(8,128)S(1)} %add.266.change_ref, f32[896,7168]{1,0:T(8,128)} %own_ref.15, f32[896,7168]{1,0:T(8,128)} %collective-permute-done.2.sib_ref), custom_call_target="tpu_custom_call" | custom-call | flops 9865003008 | bytes 51380224 | tf_op jit(solution)/shard_map/second_product/pallas_call | solution.py:91
  362.0 18.1 %collective-permute-done.30 = f32[2,64,896]{2,1,0:T(8,128)S(1)} collective-permute-done((f32[2,64,896]{2,1,0:T(8,128)S(1)}, f32[2,64,896]{2,1,0:T(8,128)S(1)}, u32[]{:S(2)}, u32[]{:S(2)}) %collective-permute-start.30) | collective-permute-done | bytes 458784 | tf_op jit(solution)/shard_map/ppermute | solution.py:228
  386.9 24.0 %collective-permute-done.32 = f32[64,7168]{1,0:T(8,128)S(1)} collective-permute-done((f32[64,7168]{1,0:T(8,128)S(1)}, f32[64,7168]{1,0:T(8,128)S(1)}, u32[]{:S(2)}, u32[]{:S(2)}) %collective-permute-start.32) | collective-permute-done | bytes 1835040 | tf_op jit(solution)/shard_map/ppermute | solution.py:204
  410.9 2.5 subtract_bitcast_fusion
  (156 shorter events, 56.2 us)
Async XLA Ops:
  0.6 53.3 %collective-permute-start.2 = (f32[896,7168]{1,0:T(8,128)}, f32[896,7168]{1,0:T(8,128)}, u32[]{:S(2)}, u32[]{:S(2)}) collective-permute-start(f32[896,7168]{1,0:T(8,128)} %own_ref.15), channel_id=1, source_target_pairs={{0,2},{2,0},{4,6},{6,4},{8,10},{10,8},{12,14},{14,12},{16,18},{18,... | collective-permute-start | bytes 77070344 | tf_op jit(solution)/shard_map/ppermute | solution.py:149
  6.1 43.5 %collective-permute-start.3 = (f32[64,7168]{1,0:T(8,128)}, f32[64,7168]{1,0:T(8,128)}, u32[]{:S(2)}, u32[]{:S(2)}) collective-permute-start(f32[64,7168]{1,0:T(8,128)} %get-tuple-element.149), channel_id=1, source_target_pairs={{0,1},{1,0},{2,3},{3,2},{4,5},{5,4},{6,7},{7,6},{8,9},{9,8},{10,11... | collective-permute-start | bytes 5505032 | tf_op jit(solution)/shard_map/ppermute | solution.py:188
  8.6 42.2 %collective-permute-start.1 = (f32[64,7168]{1,0:T(8,128)S(1)}, f32[64,7168]{1,0:T(8,128)}, u32[]{:S(2)}, u32[]{:S(2)}) collective-permute-start(f32[64,7168]{1,0:T(8,128)S(1)} %get-tuple-element.150.near_ref), channel_id=1, source_target_pairs={{0,4},{2,6},{4,0},{6,2},{8,12},{10,14},{12,8},{14,10},{16,20},{18,... | collective-permute-start | bytes 5505032 | tf_op jit(solution)/shard_map/ppermute | solution.py:186
  10.1 43.8 %collective-permute-start = (f32[64,7168]{1,0:T(8,128)S(1)}, f32[64,7168]{1,0:T(8,128)}, u32[]{:S(2)}, u32[]{:S(2)}) collective-permute-start(f32[64,7168]{1,0:T(8,128)S(1)} %get-tuple-element.150.near_ref), channel_id=1, source_target_pairs={{0,8},{2,10},{4,12},{6,14},{8,16},{10,18},{12,20},{14,22},{16,24},... | collective-permute-start | bytes 5505032 | tf_op jit(solution)/shard_map/ppermute | solution.py:184
  53.9 41.3 %collective-permute-start.5 = (f32[64,7168]{1,0:T(8,128)}, f32[64,7168]{1,0:T(8,128)S(1)}, u32[]{:S(2)}, u32[]{:S(2)}) collective-permute-start(f32[64,7168]{1,0:T(8,128)} %collective-permute-done.near_ref), channel_id=1, source_target_pairs={{0,4},{2,6},{4,0},{6,2},{8,12},{10,14},{12,8},{14,10},{16,20},{18,... | collective-permute-start | bytes 5505032 | tf_op jit(solution)/shard_map/ppermute | solution.py:186
  54.4 45.0 %collective-permute-start.4 = (f32[64,7168]{1,0:T(8,128)}, f32[64,7168]{1,0:T(8,128)S(1)}, u32[]{:S(2)}, u32[]{:S(2)}) collective-permute-start(f32[64,7168]{1,0:T(8,128)} %collective-permute-done.near_ref), channel_id=1, source_target_pairs={{0,8},{2,10},{4,12},{6,14},{8,16},{10,18},{12,20},{14,22},{16,24},... | collective-permute-start | bytes 5505032 | tf_op jit(solution)/shard_map/ppermute | solution.py:184
  54.5 70.3 %collective-permute-start.9 = (f32[2,64,896]{2,1,0:T(8,128)S(1)}, f32[2,64,896]{2,1,0:T(8,128)}, u32[]{:S(2)}, u32[]{:S(2)}) collective-permute-start(f32[2,64,896]{2,1,0:T(8,128)S(1)} %fusion.11), channel_id=1, source_target_pairs={{0,8},{2,10},{4,12},{6,14},{9,17},{11,19},{13,21},{15,23},{17,25},... | collective-permute-start | bytes 1376264 | tf_op jit(solution)/shard_map/ppermute | solution.py:161
  59.2 65.5 %collective-permute-start.10 = (f32[2,64,896]{2,1,0:T(8,128)S(1)}, f32[2,64,896]{2,1,0:T(8,128)}, u32[]{:S(2)}, u32[]{:S(2)}) collective-permute-start(f32[2,64,896]{2,1,0:T(8,128)S(1)} %fusion.16), channel_id=1, source_target_pairs={{1,13},{3,15},{5,9},{7,11},{8,20},{10,22},{12,16},{14,18},{16,28},... | collective-permute-start | bytes 1376264 | tf_op jit(solution)/shard_map/ppermute | solution.py:161
  99.4 49.6 %collective-permute-start.7 = (f32[64,7168]{1,0:T(8,128)S(1)}, f32[64,7168]{1,0:T(8,128)S(1)}, u32[]{:S(2)}, u32[]{:S(2)}) collective-permute-start(f32[64,7168]{1,0:T(8,128)S(1)} %collective-permute-done.4.near_ref), channel_id=1, source_target_pairs={{0,4},{2,6},{4,0},{6,2},{8,12},{10,14},{12,8},{14,10},{16,20},{18,... | collective-permute-start | bytes 5505032 | tf_op jit(solution)/shard_map/ppermute | solution.py:186
  100.9 48.1 %collective-permute-start.6 = (f32[64,7168]{1,0:T(8,128)S(1)}, f32[64,7168]{1,0:T(8,128)S(1)}, u32[]{:S(2)}, u32[]{:S(2)}) collective-permute-start(f32[64,7168]{1,0:T(8,128)S(1)} %collective-permute-done.4.near_ref), channel_id=1, source_target_pairs={{0,8},{2,10},{4,12},{6,14},{8,16},{10,18},{12,20},{14,22},{16,24},... | collective-permute-start | bytes 5505032 | tf_op jit(solution)/shard_map/ppermute | solution.py:184
  129.0 46.1 %collective-permute-start.15 = (f32[2,64,896]{2,1,0:T(8,128)S(1)}, f32[2,64,896]{2,1,0:T(8,128)S(1)}, u32[]{:S(2)}, u32[]{:S(2)}) collective-permute-start(f32[2,64,896]{2,1,0:T(8,128)S(1)} %fusion.12), channel_id=1, source_target_pairs={{1,17},{3,19},{5,21},{7,23},{9,25},{11,27},{13,29},{15,31},{16,0},... | collective-permute-start | bytes 1376264 | tf_op jit(solution)/shard_map/ppermute | solution.py:161
  149.0 56.3 %collective-permute-start.13 = (f32[2,64,896]{2,1,0:T(8,128)S(1)}, f32[2,64,896]{2,1,0:T(8,128)S(1)}, u32[]{:S(2)}, u32[]{:S(2)}) collective-permute-start(f32[2,64,896]{2,1,0:T(8,128)S(1)} %fusion.13), channel_id=1, source_target_pairs={{1,25},{3,27},{5,29},{7,31},{8,0},{10,2},{12,4},{14,6},{16,8},{18,... | collective-permute-start | bytes 1376264 | tf_op jit(solution)/shard_map/ppermute | solution.py:161
  150.3 55.0 %collective-permute-start.14 = (f32[2,64,896]{2,1,0:T(8,128)S(1)}, f32[2,64,896]{2,1,0:T(8,128)S(1)}, u32[]{:S(2)}, u32[]{:S(2)}) collective-permute-start(f32[2,64,896]{2,1,0:T(8,128)S(1)} %fusion.15), channel_id=1, source_target_pairs={{0,28},{2,30},{4,24},{6,26},{9,5},{11,7},{13,1},{15,3},{17,13},{19... | collective-permute-start | bytes 1376264 | tf_op jit(solution)/shard_map/ppermute | solution.py:161
  151.7 53.6 %collective-permute-start.12 = (f32[64,7168]{1,0:T(8,128)S(1)}, f32[64,7168]{1,0:T(8,128)S(1)}, u32[]{:S(2)}, u32[]{:S(2)}) collective-permute-start(f32[64,7168]{1,0:T(8,128)S(1)} %collective-permute-done.6.near_ref), channel_id=1, source_target_pairs={{0,4},{2,6},{4,0},{6,2},{8,12},{10,14},{12,8},{14,10},{16,20},{18,... | collective-permute-start | bytes 5505032 | tf_op jit(solution)/shard_map/ppermute | solution.py:186
  206.2 75.5 %collective-permute-start.23 = (f32[2,64,896]{2,1,0:T(8,128)}, f32[2,64,896]{2,1,0:T(8,128)S(1)}, u32[]{:S(2)}, u32[]{:S(2)}) collective-permute-start(f32[2,64,896]{2,1,0:T(8,128)} %slice.51), channel_id=1, source_target_pairs={{13,0},{15,2},{9,4},{11,6},{20,9},{22,11},{16,13},{18,15},{28,17},... | collective-permute-start | bytes 1376264 | tf_op jit(solution)/shard_map/ppermute | solution.py:228
  207.7 74.1 %collective-permute-start.22 = (f32[2,64,896]{2,1,0:T(8,128)S(1)}, f32[2,64,896]{2,1,0:T(8,128)S(1)}, u32[]{:S(2)}, u32[]{:S(2)}) collective-permute-start(f32[2,64,896]{2,1,0:T(8,128)S(1)} %get-tuple-element.163), channel_id=1, source_target_pairs={{20,1},{22,3},{16,5},{18,7},{28,9},{30,11},{24,13},{26,15},{5,16},... | collective-permute-start | bytes 1376264 | tf_op jit(solution)/shard_map/ppermute | solution.py:228
  208.4 73.4 %collective-permute-start.21 = (f32[2,64,896]{2,1,0:T(8,128)S(1)}, f32[2,64,896]{2,1,0:T(8,128)S(1)}, u32[]{:S(2)}, u32[]{:S(2)}) collective-permute-start(f32[2,64,896]{2,1,0:T(8,128)S(1)} %get-tuple-element.164), channel_id=1, source_target_pairs={{17,1},{19,3},{21,5},{23,7},{25,9},{27,11},{29,13},{31,15},{0,16},... | collective-permute-start | bytes 1376264 | tf_op jit(solution)/shard_map/ppermute | solution.py:228
  233.9 48.0 %collective-permute-start.19 = (f32[64,7168]{1,0:T(8,128)S(1)}, f32[64,7168]{1,0:T(8,128)S(1)}, u32[]{:S(2)}, u32[]{:S(2)}) collective-permute-start(f32[64,7168]{1,0:T(8,128)S(1)} %get-tuple-element.98), channel_id=1, source_target_pairs={{0,4},{2,6},{4,0},{6,2},{8,12},{10,14},{12,8},{14,10},{16,20},{18,... | collective-permute-start | bytes 5505032 | tf_op jit(solution)/shard_map/ppermute | solution.py:204
  281.9 46.7 %collective-permute-start.24 = (f32[64,7168]{1,0:T(8,128)S(1)}, f32[64,7168]{1,0:T(8,128)S(1)}, u32[]{:S(2)}, u32[]{:S(2)}) collective-permute-start(f32[64,7168]{1,0:T(8,128)S(1)} %get-tuple-element.108), channel_id=1, source_target_pairs={{0,4},{2,6},{4,0},{6,2},{8,12},{10,14},{12,8},{14,10},{16,20},{18,... | collective-permute-start | bytes 5505032 | tf_op jit(solution)/shard_map/ppermute | solution.py:204
  284.4 44.2 %collective-permute-start.28 = (f32[64,7168]{1,0:T(8,128)}, f32[64,7168]{1,0:T(8,128)S(1)}, u32[]{:S(2)}, u32[]{:S(2)}) collective-permute-start(f32[64,7168]{1,0:T(8,128)} %add.265), channel_id=1, source_target_pairs={{0,8},{2,10},{4,12},{6,14},{8,16},{10,18},{12,20},{14,22},{16,24},... | collective-permute-start | bytes 5505032 | tf_op jit(solution)/shard_map/ppermute | solution.py:203
  287.5 41.1 %collective-permute-start.26 = (f32[2,64,896]{2,1,0:T(8,128)S(1)}, f32[2,64,896]{2,1,0:T(8,128)S(1)}, u32[]{:S(2)}, u32[]{:S(2)}) collective-permute-start(f32[2,64,896]{2,1,0:T(8,128)S(1)} %get-tuple-element.162), channel_id=1, source_target_pairs={{25,1},{27,3},{29,5},{31,7},{0,8},{2,10},{4,12},{6,14},{8,16},{10,... | collective-permute-start | bytes 1376264 | tf_op jit(solution)/shard_map/ppermute | solution.py:228
  328.6 51.6 %collective-permute-start.29 = (f32[64,7168]{1,0:T(8,128)}, f32[64,7168]{1,0:T(8,128)}, u32[]{:S(2)}, u32[]{:S(2)}) collective-permute-start(f32[64,7168]{1,0:T(8,128)} %get-tuple-element.119), channel_id=1, source_target_pairs={{0,4},{2,6},{4,0},{6,2},{8,12},{10,14},{12,8},{14,10},{16,20},{18,... | collective-permute-start | bytes 5505032 | tf_op jit(solution)/shard_map/ppermute | solution.py:204
  330.8 49.3 %collective-permute-start.31 = (f32[64,7168]{1,0:T(8,128)}, f32[64,7168]{1,0:T(8,128)}, u32[]{:S(2)}, u32[]{:S(2)}) collective-permute-start(f32[64,7168]{1,0:T(8,128)} %add_add_fusion.1), channel_id=1, source_target_pairs={{0,8},{2,10},{4,12},{6,14},{8,16},{10,18},{12,20},{14,22},{16,24},... | collective-permute-start | bytes 5505032 | tf_op jit(solution)/shard_map/ppermute | solution.py:203
  336.2 43.9 %collective-permute-start.30 = (f32[2,64,896]{2,1,0:T(8,128)S(1)}, f32[2,64,896]{2,1,0:T(8,128)S(1)}, u32[]{:S(2)}, u32[]{:S(2)}) collective-permute-start(f32[2,64,896]{2,1,0:T(8,128)S(1)} %get-tuple-element.159), channel_id=1, source_target_pairs={{4,0},{6,2},{0,4},{2,6},{12,8},{14,10},{8,12},{10,14},{21,17},{23,... | collective-permute-start | bytes 1376264 | tf_op jit(solution)/shard_map/ppermute | solution.py:228
  (34 other events, 432.9 us)

commit v11 on v10

--- a/solution.py
+++ b/solution.py
@@ -191,7 +191,11 @@
         if window == 1:
             cuts.update({(shift, 1): cut(rest_across, shift, 1) for shift in range(1, ring)})
         if 0 < window < ring:
+            if window > 2:
+                added[window - 1, 0] = piece(window - 1, 0)
             for flip in range(PAIR):
+                if flip == 0 and 2 <= window < ring - 1:
+                    continue
                 added[window, flip] = piece(window, flip)
                 if window == ring - 1:
                     fresh.append((added, (window, flip)))
@@ -227,7 +231,7 @@
             rows = changed[group][:, flip * half : (flip + 1) * half]
             put(back, (group, flip), permute(rows, both, route_back(group, flip)) if group or flip else rows)
         values = [where[key] for where, key in fresh]
-        waiting = {key: part for key, part in cuts.items() if key[0] > window or not window}
+        waiting = {key: part for key, part in cuts.items() if key[0] > window or not window or (key == (window, 0) and 2 <= window < ring - 1)}
         values, sibling, total, waiting, rest_across = lax.optimization_barrier((values, sibling, total, waiting, rest_across))
         cuts.update(waiting)
         for (where, key), value in zip(fresh, values):

time: 416 us -> 417 us (level)
  no operation moved by 1% of the time
where the time goes in v11:
time: 417 us
  Pallas kernels  184 us (44%)
  waiting for transfers between devices  122 us (29%)
  starting transfers between devices  76.3 us (18%)
  other arithmetic  21 us (5%)
  local copies, waits for them, and re-layouts  11.9 us (3%)
    pallas_call x4, Pallas kernels, second(): pl.pallas_call(second_kernel, grid=(columns // tile,), in_specs=[pl.Block...  95.7 us
    pallas_call x4, Pallas kernels, first(): pl.pallas_call(first_kernel, grid=(rows // tile,), in_specs=[whole, whole...  88.1 us
    ppermute x7, starting transfers between devices, per_device(): permute(rows, both, route_back(group, flip))  41.7 us
    ppermute x1, waiting for transfers between devices, per_device(): permute(rest, 'col', [(y, (y + 1) % planes) for y in range(planes)])  33.3 us
    ppermute x7, waiting for transfers between devices, per_device(): permute(rows, both, route_back(group, flip))  30.9 us
    ppermute x4, waiting for transfers between devices, per_device(): put(swapped, closing % ring, permute(sent[closing % ring], 'row', to_pair))  22.7 us
    ppermute x7, waiting for transfers between devices, piece(): return permute(part, both, route(shift, flip)) if shift or flip else part  16.5 us
    ppermute x7, starting transfers between devices, piece(): return permute(part, both, route(shift, flip)) if shift or flip else part  13.6 us
  transfers between devices with their start and end apart: 34, of which 9 were waited for; matrix products, arithmetic and copies ran while one was open for 5% of the time, Pallas kernels for 44%

profile of v11, /device:TPU:0, one launch (start us, length us, event | category | flops | bytes accessed | tf_op | source)
XLA Modules:
  0.0 416.6 jit_solution(1535076497710314011)
XLA Ops:
  1.1 4.9 %fusion.4 = (f32[64,7168]{1,0:T(8,128)}, f32[64,7168]{1,0:T(8,128)S(1)}) fusion(f32[7168,64]{0,1:T(8,128)} %param.8, f32[7168,64]{0,1:T(8,128)} %param.6, f32[7168,64]{0,1:T(8,128)} %param.7, s32[7168,64]{0,1:T(8,128)} %param.9), kind=kLoop, calls=%fused_computation.7 | loop fusion | flops 4128768 | bytes 11010048 | tf_op jit(solution)/shard_map/sub | solution.py:150
  16.3 33.3 %collective-permute-done.3 = f32[64,7168]{1,0:T(8,128)} collective-permute-done((f32[64,7168]{1,0:T(8,128)}, f32[64,7168]{1,0:T(8,128)}, u32[]{:S(2)}, u32[]{:S(2)}) %collective-permute-start.3) | collective-permute-done | bytes 1835040 | tf_op jit(solution)/shard_map/ppermute | solution.py:188
  50.8 3.1 collective-permute-done.near_ref
  54.5 3.2 collective-permute-start.9
  61.5 22.3 %first_product.4 = f32[2,128,896]{2,1,0:T(8,128)S(1)} custom-call(f32[64,7168]{1,0:T(8,128)S(1)} %get-tuple-element.152.near_ref, f32[64,7168]{1,0:T(8,128)} %collective-permute-done.1.far_ref, f32[896,7168]{1,0:T(8,128)} %own_ref.15, f32[896,7168]{1,0:T(8,128)} %collective-permute-done.2.sib_ref), custom_call_target="tpu_custom_call" | custom-call | flops 9865003008 | bytes 51380224 | tf_op jit(solution)/shard_map/first_product/pallas_call | solution.py:53
  83.8 11.4 %collective-permute-done.5.far_ref = f32[64,7168]{1,0:T(8,128)S(1)} collective-permute-done((f32[64,7168]{1,0:T(8,128)}, f32[64,7168]{1,0:T(8,128)S(1)}, u32[]{:S(2)}, u32[]{:S(2)}) %collective-permute-start.5) | collective-permute-done | bytes 1835040 | tf_op jit(solution)/shard_map/ppermute | solution.py:186
  96.4 3.0 collective-permute-done.4.near_ref
  102.4 22.3 %first_product.5 = f32[2,128,896]{2,1,0:T(8,128)S(1)} custom-call(f32[64,7168]{1,0:T(8,128)} %collective-permute-done.near_ref, f32[64,7168]{1,0:T(8,128)S(1)} %copy-done.1, f32[896,7168]{1,0:T(8,128)} %own_ref.15, f32[896,7168]{1,0:T(8,128)} %collective-permute-done.2.sib_ref), custom_call_target="tpu_custom_call" | custom-call | flops 9865003008 | bytes 51380224 | tf_op jit(solution)/shard_map/first_product/pallas_call | solution.py:53
  130.4 16.5 %collective-permute-done.8 = f32[2,64,896]{2,1,0:T(8,128)S(1)} collective-permute-done((f32[2,64,896]{2,1,0:T(8,128)S(1)}, f32[2,64,896]{2,1,0:T(8,128)S(1)}, u32[]{:S(2)}, u32[]{:S(2)}) %collective-permute-start.8) | collective-permute-done | bytes 458784 | tf_op jit(solution)/shard_map/ppermute | solution.py:161
  148.2 2.7 collective-permute-start.14
  152.8 21.8 %first_product.6 = f32[2,128,896]{2,1,0:T(8,128)S(1)} custom-call(f32[64,7168]{1,0:T(8,128)S(1)} %collective-permute-done.4.near_ref, f32[64,7168]{1,0:T(8,128)S(1)} %collective-permute-done.7.far_ref, f32[896,7168]{1,0:T(8,128)} %own_ref.15, f32[896,7168]{1,0:T(8,128)} %collective-permute-done.2.sib_ref), custom_call_target="tpu_custom_call" | custom-call | flops 9865003008 | bytes 51380224 | tf_op jit(solution)/shard_map/first_product/pallas_call | solution.py:53
  174.8 24.7 %collective-permute-start.18 = (f32[2,64,896]{2,1,0:T(8,128)S(1)}, f32[2,64,896]{2,1,0:T(8,128)S(1)}, u32[]{:S(2)}, u32[]{:S(2)}) collective-permute-start(f32[2,64,896]{2,1,0:T(8,128)S(1)} %slice.64), channel_id=1, source_target_pairs={{8,0},{10,2},{12,4},{14,6},{17,9},{19,11},{21,13},{23,15},{25,17},... | collective-permute-start | bytes 1376264 | tf_op jit(solution)/shard_map/ppermute | solution.py:232
  200.7 23.7 %second_product.4 = (f32[64,7168]{1,0:T(8,128)S(1)}, f32[64,7168]{1,0:T(8,128)S(1)}) custom-call(f32[2,128,896]{2,1,0:T(8,128)S(1)} %add.259.change_ref, f32[896,7168]{1,0:T(8,128)} %own_ref.15, f32[896,7168]{1,0:T(8,128)} %collective-permute-done.2.sib_ref), custom_call_target="tpu_custom_call" | custom-call | flops 9865003008 | bytes 51380224 | tf_op jit(solution)/shard_map/second_product/pallas_call | solution.py:91
  227.5 7.9 %collective-permute-start.21 = (f32[2,64,896]{2,1,0:T(8,128)S(1)}, f32[2,64,896]{2,1,0:T(8,128)S(1)}, u32[]{:S(2)}, u32[]{:S(2)}) collective-permute-start(f32[2,64,896]{2,1,0:T(8,128)S(1)} %get-tuple-element.166), channel_id=1, source_target_pairs={{17,1},{19,3},{21,5},{23,7},{25,9},{27,11},{29,13},{31,15},{0,16},... | collective-permute-start | bytes 1376264 | tf_op jit(solution)/shard_map/ppermute | solution.py:232
  236.6 21.8 %first_product.7 = f32[2,128,896]{2,1,0:T(8,128)S(1)} custom-call(f32[64,7168]{1,0:T(8,128)S(1)} %collective-permute-done.6.near_ref, f32[64,7168]{1,0:T(8,128)S(1)} %collective-permute-done.12.far_ref, f32[896,7168]{1,0:T(8,128)} %own_ref.15, f32[896,7168]{1,0:T(8,128)} %collective-permute-done.2.sib_ref), custom_call_target="tpu_custom_call" | custom-call | flops 9865003008 | bytes 51380224 | tf_op jit(solution)/shard_map/first_product/pallas_call | solution.py:53
  259.7 23.7 %second_product.5 = (f32[64,7168]{1,0:T(8,128)S(1)}, f32[64,7168]{1,0:T(8,128)S(1)}) custom-call(f32[2,128,896]{2,1,0:T(8,128)S(1)} %add.261.change_ref, f32[896,7168]{1,0:T(8,128)} %own_ref.15, f32[896,7168]{1,0:T(8,128)} %collective-permute-done.2.sib_ref), custom_call_target="tpu_custom_call" | custom-call | flops 9865003008 | bytes 51380224 | tf_op jit(solution)/shard_map/second_product/pallas_call | solution.py:91
  285.9 2.7 collective-permute-start.28
  291.6 2.6 collective-permute-start.26
  294.2 24.6 %second_product.6 = (f32[64,7168]{1,0:T(8,128)S(1)}, f32[64,7168]{1,0:T(8,128)}) custom-call(f32[2,128,896]{2,1,0:T(8,128)S(1)} %add.263.change_ref, f32[896,7168]{1,0:T(8,128)} %own_ref.15, f32[896,7168]{1,0:T(8,128)} %collective-permute-done.2.sib_ref), custom_call_target="tpu_custom_call" | custom-call | flops 9865003008 | bytes 51380224 | tf_op jit(solution)/shard_map/second_product/pallas_call | solution.py:91
  318.8 13.9 %collective-permute-done.26 = f32[2,64,896]{2,1,0:T(8,128)S(1)} collective-permute-done((f32[2,64,896]{2,1,0:T(8,128)S(1)}, f32[2,64,896]{2,1,0:T(8,128)S(1)}, u32[]{:S(2)}, u32[]{:S(2)}) %collective-permute-start.26) | collective-permute-done | bytes 458784 | tf_op jit(solution)/shard_map/ppermute | solution.py:232
  338.2 3.9 collective-permute-start.30
  342.1 23.7 %second_product.7 = (f32[64,7168]{1,0:T(8,128)S(1)}, f32[64,7168]{1,0:T(8,128)S(1)}) custom-call(f32[2,128,896]{2,1,0:T(8,128)S(1)} %add.266.change_ref, f32[896,7168]{1,0:T(8,128)} %own_ref.15, f32[896,7168]{1,0:T(8,128)} %collective-permute-done.2.sib_ref), custom_call_target="tpu_custom_call" | custom-call | flops 9865003008 | bytes 51380224 | tf_op jit(solution)/shard_map/second_product/pallas_call | solution.py:91
  365.8 17.1 %collective-permute-done.30 = f32[2,64,896]{2,1,0:T(8,128)S(1)} collective-permute-done((f32[2,64,896]{2,1,0:T(8,128)S(1)}, f32[2,64,896]{2,1,0:T(8,128)S(1)}, u32[]{:S(2)}, u32[]{:S(2)}) %collective-permute-start.30) | collective-permute-done | bytes 458784 | tf_op jit(solution)/shard_map/ppermute | solution.py:232
  389.6 22.7 %collective-permute-done.32 = f32[64,7168]{1,0:T(8,128)S(1)} collective-permute-done((f32[64,7168]{1,0:T(8,128)S(1)}, f32[64,7168]{1,0:T(8,128)S(1)}, u32[]{:S(2)}, u32[]{:S(2)}) %collective-permute-start.32) | collective-permute-done | bytes 1835040 | tf_op jit(solution)/shard_map/ppermute | solution.py:208
  (156 shorter events, 58.0 us)
Async XLA Ops:
  0.6 53.3 %collective-permute-start.2 = (f32[896,7168]{1,0:T(8,128)}, f32[896,7168]{1,0:T(8,128)}, u32[]{:S(2)}, u32[]{:S(2)}) collective-permute-start(f32[896,7168]{1,0:T(8,128)} %own_ref.15), channel_id=1, source_target_pairs={{0,2},{2,0},{4,6},{6,4},{8,10},{10,8},{12,14},{14,12},{16,18},{18,... | collective-permute-start | bytes 77070344 | tf_op jit(solution)/shard_map/ppermute | solution.py:149
  6.1 43.5 %collective-permute-start.3 = (f32[64,7168]{1,0:T(8,128)}, f32[64,7168]{1,0:T(8,128)}, u32[]{:S(2)}, u32[]{:S(2)}) collective-permute-start(f32[64,7168]{1,0:T(8,128)} %get-tuple-element.151), channel_id=1, source_target_pairs={{0,1},{1,0},{2,3},{3,2},{4,5},{5,4},{6,7},{7,6},{8,9},{9,8},{10,11... | collective-permute-start | bytes 5505032 | tf_op jit(solution)/shard_map/ppermute | solution.py:188
  8.6 42.2 %collective-permute-start.1 = (f32[64,7168]{1,0:T(8,128)S(1)}, f32[64,7168]{1,0:T(8,128)}, u32[]{:S(2)}, u32[]{:S(2)}) collective-permute-start(f32[64,7168]{1,0:T(8,128)S(1)} %get-tuple-element.152.near_ref), channel_id=1, source_target_pairs={{0,4},{2,6},{4,0},{6,2},{8,12},{10,14},{12,8},{14,10},{16,20},{18,... | collective-permute-start | bytes 5505032 | tf_op jit(solution)/shard_map/ppermute | solution.py:186
  10.1 43.8 %collective-permute-start = (f32[64,7168]{1,0:T(8,128)S(1)}, f32[64,7168]{1,0:T(8,128)}, u32[]{:S(2)}, u32[]{:S(2)}) collective-permute-start(f32[64,7168]{1,0:T(8,128)S(1)} %get-tuple-element.152.near_ref), channel_id=1, source_target_pairs={{0,8},{2,10},{4,12},{6,14},{8,16},{10,18},{12,20},{14,22},{16,24},... | collective-permute-start | bytes 5505032 | tf_op jit(solution)/shard_map/ppermute | solution.py:184
  54.4 45.0 %collective-permute-start.4 = (f32[64,7168]{1,0:T(8,128)}, f32[64,7168]{1,0:T(8,128)S(1)}, u32[]{:S(2)}, u32[]{:S(2)}) collective-permute-start(f32[64,7168]{1,0:T(8,128)} %collective-permute-done.near_ref), channel_id=1, source_target_pairs={{0,8},{2,10},{4,12},{6,14},{8,16},{10,18},{12,20},{14,22},{16,24},... | collective-permute-start | bytes 5505032 | tf_op jit(solution)/shard_map/ppermute | solution.py:184
  54.5 70.3 %collective-permute-start.9 = (f32[2,64,896]{2,1,0:T(8,128)S(1)}, f32[2,64,896]{2,1,0:T(8,128)}, u32[]{:S(2)}, u32[]{:S(2)}) collective-permute-start(f32[2,64,896]{2,1,0:T(8,128)S(1)} %fusion.11), channel_id=1, source_target_pairs={{0,8},{2,10},{4,12},{6,14},{9,17},{11,19},{13,21},{15,23},{17,25},... | collective-permute-start | bytes 1376264 | tf_op jit(solution)/shard_map/ppermute | solution.py:161
  59.2 65.5 %collective-permute-start.10 = (f32[2,64,896]{2,1,0:T(8,128)S(1)}, f32[2,64,896]{2,1,0:T(8,128)}, u32[]{:S(2)}, u32[]{:S(2)}) collective-permute-start(f32[2,64,896]{2,1,0:T(8,128)S(1)} %fusion.16), channel_id=1, source_target_pairs={{1,13},{3,15},{5,9},{7,11},{8,20},{10,22},{12,16},{14,18},{16,28},... | collective-permute-start | bytes 1376264 | tf_op jit(solution)/shard_map/ppermute | solution.py:161
  99.4 47.5 %collective-permute-start.7 = (f32[64,7168]{1,0:T(8,128)S(1)}, f32[64,7168]{1,0:T(8,128)S(1)}, u32[]{:S(2)}, u32[]{:S(2)}) collective-permute-start(f32[64,7168]{1,0:T(8,128)S(1)} %collective-permute-done.4.near_ref), channel_id=1, source_target_pairs={{0,4},{2,6},{4,0},{6,2},{8,12},{10,14},{12,8},{14,10},{16,20},{18,... | collective-permute-start | bytes 5505032 | tf_op jit(solution)/shard_map/ppermute | solution.py:186
  100.9 46.0 %collective-permute-start.6 = (f32[64,7168]{1,0:T(8,128)S(1)}, f32[64,7168]{1,0:T(8,128)S(1)}, u32[]{:S(2)}, u32[]{:S(2)}) collective-permute-start(f32[64,7168]{1,0:T(8,128)S(1)} %collective-permute-done.4.near_ref), channel_id=1, source_target_pairs={{0,8},{2,10},{4,12},{6,14},{8,16},{10,18},{12,20},{14,22},{16,24},... | collective-permute-start | bytes 5505032 | tf_op jit(solution)/shard_map/ppermute | solution.py:184
  129.1 45.7 %collective-permute-start.16 = (f32[2,64,896]{2,1,0:T(8,128)S(1)}, f32[2,64,896]{2,1,0:T(8,128)S(1)}, u32[]{:S(2)}, u32[]{:S(2)}) collective-permute-start(f32[2,64,896]{2,1,0:T(8,128)S(1)} %copy-done.19), channel_id=1, source_target_pairs={{0,20},{2,22},{4,16},{6,18},{8,28},{10,30},{12,24},{14,26},{17,5},... | collective-permute-start | bytes 1376264 | tf_op jit(solution)/shard_map/ppermute | solution.py:161
  146.9 77.4 %collective-permute-start.13 = (f32[2,64,896]{2,1,0:T(8,128)S(1)}, f32[2,64,896]{2,1,0:T(8,128)S(1)}, u32[]{:S(2)}, u32[]{:S(2)}) collective-permute-start(f32[2,64,896]{2,1,0:T(8,128)S(1)} %fusion.13), channel_id=1, source_target_pairs={{1,25},{3,27},{5,29},{7,31},{8,0},{10,2},{12,4},{14,6},{16,8},{18,... | collective-permute-start | bytes 1376264 | tf_op jit(solution)/shard_map/ppermute | solution.py:161
  148.2 76.2 %collective-permute-start.14 = (f32[2,64,896]{2,1,0:T(8,128)S(1)}, f32[2,64,896]{2,1,0:T(8,128)S(1)}, u32[]{:S(2)}, u32[]{:S(2)}) collective-permute-start(f32[2,64,896]{2,1,0:T(8,128)S(1)} %fusion.15), channel_id=1, source_target_pairs={{0,28},{2,30},{4,24},{6,26},{9,5},{11,7},{13,1},{15,3},{17,13},{19... | collective-permute-start | bytes 1376264 | tf_op jit(solution)/shard_map/ppermute | solution.py:161
  150.9 48.5 %collective-permute-start.15 = (f32[2,64,896]{2,1,0:T(8,128)S(1)}, f32[2,64,896]{2,1,0:T(8,128)}, u32[]{:S(2)}, u32[]{:S(2)}) collective-permute-start(f32[2,64,896]{2,1,0:T(8,128)S(1)} %fusion.12), channel_id=1, source_target_pairs={{1,17},{3,19},{5,21},{7,23},{9,25},{11,27},{13,29},{15,31},{16,0},... | collective-permute-start | bytes 1376264 | tf_op jit(solution)/shard_map/ppermute | solution.py:161
  152.2 72.2 %collective-permute-start.12 = (f32[64,7168]{1,0:T(8,128)S(1)}, f32[64,7168]{1,0:T(8,128)S(1)}, u32[]{:S(2)}, u32[]{:S(2)}) collective-permute-start(f32[64,7168]{1,0:T(8,128)S(1)} %collective-permute-done.6.near_ref), channel_id=1, source_target_pairs={{0,4},{2,6},{4,0},{6,2},{8,12},{10,14},{12,8},{14,10},{16,20},{18,... | collective-permute-start | bytes 5505032 | tf_op jit(solution)/shard_map/ppermute | solution.py:186
  174.8 49.6 %collective-permute-start.18 = (f32[2,64,896]{2,1,0:T(8,128)S(1)}, f32[2,64,896]{2,1,0:T(8,128)S(1)}, u32[]{:S(2)}, u32[]{:S(2)}) collective-permute-start(f32[2,64,896]{2,1,0:T(8,128)S(1)} %slice.64), channel_id=1, source_target_pairs={{8,0},{10,2},{12,4},{14,6},{17,9},{19,11},{21,13},{23,15},{25,17},... | collective-permute-start | bytes 1376264 | tf_op jit(solution)/shard_map/ppermute | solution.py:232
  225.3 58.1 %collective-permute-start.23 = (f32[2,64,896]{2,1,0:T(8,128)}, f32[2,64,896]{2,1,0:T(8,128)S(1)}, u32[]{:S(2)}, u32[]{:S(2)}) collective-permute-start(f32[2,64,896]{2,1,0:T(8,128)} %slice.51), channel_id=1, source_target_pairs={{13,0},{15,2},{9,4},{11,6},{20,9},{22,11},{16,13},{18,15},{28,17},... | collective-permute-start | bytes 1376264 | tf_op jit(solution)/shard_map/ppermute | solution.py:232
  226.8 56.6 %collective-permute-start.22 = (f32[2,64,896]{2,1,0:T(8,128)S(1)}, f32[2,64,896]{2,1,0:T(8,128)S(1)}, u32[]{:S(2)}, u32[]{:S(2)}) collective-permute-start(f32[2,64,896]{2,1,0:T(8,128)S(1)} %get-tuple-element.165), channel_id=1, source_target_pairs={{20,1},{22,3},{16,5},{18,7},{28,9},{30,11},{24,13},{26,15},{5,16},... | collective-permute-start | bytes 1376264 | tf_op jit(solution)/shard_map/ppermute | solution.py:232
  227.5 55.9 %collective-permute-start.21 = (f32[2,64,896]{2,1,0:T(8,128)S(1)}, f32[2,64,896]{2,1,0:T(8,128)S(1)}, u32[]{:S(2)}, u32[]{:S(2)}) collective-permute-start(f32[2,64,896]{2,1,0:T(8,128)S(1)} %get-tuple-element.166), channel_id=1, source_target_pairs={{17,1},{19,3},{21,5},{23,7},{25,9},{27,11},{29,13},{31,15},{0,16},... | collective-permute-start | bytes 1376264 | tf_op jit(solution)/shard_map/ppermute | solution.py:232
  235.4 48.1 %collective-permute-start.19 = (f32[64,7168]{1,0:T(8,128)S(1)}, f32[64,7168]{1,0:T(8,128)S(1)}, u32[]{:S(2)}, u32[]{:S(2)}) collective-permute-start(f32[64,7168]{1,0:T(8,128)S(1)} %get-tuple-element.100), channel_id=1, source_target_pairs={{0,4},{2,6},{4,0},{6,2},{8,12},{10,14},{12,8},{14,10},{16,20},{18,... | collective-permute-start | bytes 5505032 | tf_op jit(solution)/shard_map/ppermute | solution.py:208
  283.5 49.2 %collective-permute-start.24 = (f32[64,7168]{1,0:T(8,128)S(1)}, f32[64,7168]{1,0:T(8,128)S(1)}, u32[]{:S(2)}, u32[]{:S(2)}) collective-permute-start(f32[64,7168]{1,0:T(8,128)S(1)} %get-tuple-element.110), channel_id=1, source_target_pairs={{0,4},{2,6},{4,0},{6,2},{8,12},{10,14},{12,8},{14,10},{16,20},{18,... | collective-permute-start | bytes 5505032 | tf_op jit(solution)/shard_map/ppermute | solution.py:208
  285.9 46.8 %collective-permute-start.28 = (f32[64,7168]{1,0:T(8,128)}, f32[64,7168]{1,0:T(8,128)S(1)}, u32[]{:S(2)}, u32[]{:S(2)}) collective-permute-start(f32[64,7168]{1,0:T(8,128)} %add.265), channel_id=1, source_target_pairs={{0,8},{2,10},{4,12},{6,14},{8,16},{10,18},{12,20},{14,22},{16,24},... | collective-permute-start | bytes 5505032 | tf_op jit(solution)/shard_map/ppermute | solution.py:207
  332.7 50.1 %collective-permute-start.29 = (f32[64,7168]{1,0:T(8,128)}, f32[64,7168]{1,0:T(8,128)}, u32[]{:S(2)}, u32[]{:S(2)}) collective-permute-start(f32[64,7168]{1,0:T(8,128)} %get-tuple-element.121), channel_id=1, source_target_pairs={{0,4},{2,6},{4,0},{6,2},{8,12},{10,14},{12,8},{14,10},{16,20},{18,... | collective-permute-start | bytes 5505032 | tf_op jit(solution)/shard_map/ppermute | solution.py:208
  334.3 48.5 %collective-permute-start.31 = (f32[64,7168]{1,0:T(8,128)}, f32[64,7168]{1,0:T(8,128)}, u32[]{:S(2)}, u32[]{:S(2)}) collective-permute-start(f32[64,7168]{1,0:T(8,128)} %add_add_fusion.1), channel_id=1, source_target_pairs={{0,8},{2,10},{4,12},{6,14},{8,16},{10,18},{12,20},{14,22},{16,24},... | collective-permute-start | bytes 5505032 | tf_op jit(solution)/shard_map/ppermute | solution.py:207
  338.2 44.6 %collective-permute-start.30 = (f32[2,64,896]{2,1,0:T(8,128)S(1)}, f32[2,64,896]{2,1,0:T(8,128)S(1)}, u32[]{:S(2)}, u32[]{:S(2)}) collective-permute-start(f32[2,64,896]{2,1,0:T(8,128)S(1)} %get-tuple-element.161), channel_id=1, source_target_pairs={{4,0},{6,2},{0,4},{2,6},{12,8},{14,10},{8,12},{10,14},{21,17},{23,... | collective-permute-start | bytes 1376264 | tf_op jit(solution)/shard_map/ppermute | solution.py:232
  (34 other events, 425.1 us)

commit v12 on v10

--- a/solution.py
+++ b/solution.py
@@ -172,7 +172,7 @@
     returns = {group + 2: [(group, 0), (group, 1)] for group in range(2, ring)}
     returns.setdefault(3, []).append((1, 0))
     returns.setdefault(4, []).append((1, 1))
-    returns.setdefault(start + 2, []).extend([(0, 0), (0, 1)])
+    returns.setdefault(start + ring - 1, []).extend([(0, 0), (0, 1)])
     for window in range(start + ring):
         fresh = []
 

time: 416 us -> 424 us (1.019)
  local copies, waits for them, and re-layouts: 11.9 us -> 16.6 us
    ppermute x4, waiting for transfers between devices: 24 us -> 7.19 us  [per_device(): put(swapped, closing % ring, permute(sent[closing % ring], 'row', to_pair))]
    ppermute x7, waiting for transfers between devices: 32.1 us -> 47.1 us  [per_device(): permute(rows, both, route_back(group, flip))]
    ppermute x3, waiting for transfers between devices: 0.01 us -> 5.77 us  [per_device(): total = permute(total, 'row', to_next)]
    unnamed x62, local copies, waits for them, and re-layouts: 5.71 us -> 10.3 us
  transfers between devices with their start and end apart: 34 -> 34, of which waited for: 9 -> 10; matrix products, arithmetic and copies ran while one was open for 5% -> 4% of each run, Pallas kernels for 44% -> 43%
where the time goes in v12:
time: 424 us; the launch traced here: 423 us
  Pallas kernels  184 us (43%)
  waiting for transfers between devices  129 us (30%)
  starting transfers between devices  72.9 us (17%)
  other arithmetic  19.8 us (5%)
  local copies, waits for them, and re-layouts  16.6 us (4%)
    pallas_call x4, Pallas kernels, second(): pl.pallas_call(second_kernel, grid=(columns // tile,), in_specs=[pl.Block...  95.7 us
    pallas_call x4, Pallas kernels, first(): pl.pallas_call(first_kernel, grid=(rows // tile,), in_specs=[whole, whole...  88.1 us
    ppermute x7, waiting for transfers between devices, per_device(): permute(rows, both, route_back(group, flip))  47.1 us
    ppermute x7, starting transfers between devices, per_device(): permute(rows, both, route_back(group, flip))  40.6 us
    ppermute x1, waiting for transfers between devices, per_device(): permute(rest, 'col', [(y, (y + 1) % planes) for y in range(planes)])  33.3 us
    ppermute x7, waiting for transfers between devices, piece(): return permute(part, both, route(shift, flip)) if shift or flip else part  16.6 us
    ppermute x7, starting transfers between devices, piece(): return permute(part, both, route(shift, flip)) if shift or flip else part  13.1 us
    ppermute x4, waiting for transfers between devices, per_device(): put(far, window, permute(near[window], 'row', to_pair))  12.7 us
  transfers between devices with their start and end apart: 34, of which 10 were waited for; matrix products, arithmetic and copies ran while one was open for 4% of the time, Pallas kernels for 43%

profile of v12, /device:TPU:0, one launch (start us, length us, event | category | flops | bytes accessed | tf_op | source)
XLA Modules:
  0.0 423.4 jit_solution(7946409793367045838)
XLA Ops:
  1.1 4.9 %fusion.4 = (f32[64,7168]{1,0:T(8,128)}, f32[64,7168]{1,0:T(8,128)S(1)}) fusion(f32[7168,64]{0,1:T(8,128)} %param.8, f32[7168,64]{0,1:T(8,128)} %param.6, f32[7168,64]{0,1:T(8,128)} %param.7, s32[7168,64]{0,1:T(8,128)} %param.9), kind=kLoop, calls=%fused_computation.7 | loop fusion | flops 4128768 | bytes 11010048 | tf_op jit(solution)/shard_map/sub | solution.py:150
  16.3 33.3 %collective-permute-done.3 = f32[64,7168]{1,0:T(8,128)} collective-permute-done((f32[64,7168]{1,0:T(8,128)}, f32[64,7168]{1,0:T(8,128)}, u32[]{:S(2)}, u32[]{:S(2)}) %collective-permute-start.3) | collective-permute-done | bytes 1835040 | tf_op jit(solution)/shard_map/ppermute | solution.py:188
  50.8 3.1 collective-permute-done.near_ref
  54.5 3.2 collective-permute-start.9
  61.5 22.3 %first_product.4 = f32[2,128,896]{2,1,0:T(8,128)S(1)} custom-call(f32[64,7168]{1,0:T(8,128)S(1)} %get-tuple-element.152.near_ref, f32[64,7168]{1,0:T(8,128)} %collective-permute-done.1.far_ref, f32[896,7168]{1,0:T(8,128)} %own_ref.15, f32[896,7168]{1,0:T(8,128)} %collective-permute-done.2.sib_ref), custom_call_target="tpu_custom_call" | custom-call | flops 9865003008 | bytes 51380224 | tf_op jit(solution)/shard_map/first_product/pallas_call | solution.py:53
  83.8 11.4 %collective-permute-done.5.far_ref = f32[64,7168]{1,0:T(8,128)S(1)} collective-permute-done((f32[64,7168]{1,0:T(8,128)}, f32[64,7168]{1,0:T(8,128)S(1)}, u32[]{:S(2)}, u32[]{:S(2)}) %collective-permute-start.5) | collective-permute-done | bytes 1835040 | tf_op jit(solution)/shard_map/ppermute | solution.py:186
  96.4 3.0 collective-permute-done.4.near_ref
  102.4 22.3 %first_product.5 = f32[2,128,896]{2,1,0:T(8,128)S(1)} custom-call(f32[64,7168]{1,0:T(8,128)} %collective-permute-done.near_ref, f32[64,7168]{1,0:T(8,128)S(1)} %copy-done.1, f32[896,7168]{1,0:T(8,128)} %own_ref.15, f32[896,7168]{1,0:T(8,128)} %collective-permute-done.2.sib_ref), custom_call_target="tpu_custom_call" | custom-call | flops 9865003008 | bytes 51380224 | tf_op jit(solution)/shard_map/first_product/pallas_call | solution.py:53
  130.3 16.6 %collective-permute-done.8 = f32[2,64,896]{2,1,0:T(8,128)S(1)} collective-permute-done((f32[2,64,896]{2,1,0:T(8,128)S(1)}, f32[2,64,896]{2,1,0:T(8,128)S(1)}, u32[]{:S(2)}, u32[]{:S(2)}) %collective-permute-start.8) | collective-permute-done | bytes 458784 | tf_op jit(solution)/shard_map/ppermute | solution.py:161
  153.2 21.8 %first_product.6 = f32[2,128,896]{2,1,0:T(8,128)S(1)} custom-call(f32[64,7168]{1,0:T(8,128)S(1)} %collective-permute-done.4.near_ref, f32[64,7168]{1,0:T(8,128)S(1)} %collective-permute-done.7.far_ref, f32[896,7168]{1,0:T(8,128)} %own_ref.15, f32[896,7168]{1,0:T(8,128)} %collective-permute-done.2.sib_ref), custom_call_target="tpu_custom_call" | custom-call | flops 9865003008 | bytes 51380224 | tf_op jit(solution)/shard_map/first_product/pallas_call | solution.py:53
  175.1 5.2 %collective-permute-start.18 = (f32[2,64,896]{2,1,0:T(8,128)S(1)}, f32[2,64,896]{2,1,0:T(8,128)S(1)}, u32[]{:S(2)}, u32[]{:S(2)}) collective-permute-start(f32[2,64,896]{2,1,0:T(8,128)S(1)} %slice.64), channel_id=1, source_target_pairs={{8,0},{10,2},{12,4},{14,6},{17,9},{19,11},{21,13},{23,15},{25,17},... | collective-permute-start | bytes 1376264 | tf_op jit(solution)/shard_map/ppermute | solution.py:228
  181.6 23.7 %second_product.4 = (f32[64,7168]{1,0:T(8,128)S(1)}, f32[64,7168]{1,0:T(8,128)S(1)}) custom-call(f32[2,128,896]{2,1,0:T(8,128)S(1)} %add.259.change_ref, f32[896,7168]{1,0:T(8,128)} %own_ref.15, f32[896,7168]{1,0:T(8,128)} %collective-permute-done.2.sib_ref), custom_call_target="tpu_custom_call" | custom-call | flops 9865003008 | bytes 51380224 | tf_op jit(solution)/shard_map/second_product/pallas_call | solution.py:91
  208.5 26.3 %collective-permute-start.21 = (f32[2,64,896]{2,1,0:T(8,128)S(1)}, f32[2,64,896]{2,1,0:T(8,128)}, u32[]{:S(2)}, u32[]{:S(2)}) collective-permute-start(f32[2,64,896]{2,1,0:T(8,128)S(1)} %get-tuple-element.166), channel_id=1, source_target_pairs={{17,1},{19,3},{21,5},{23,7},{25,9},{27,11},{29,13},{31,15},{0,16},... | collective-permute-start | bytes 1376264 | tf_op jit(solution)/shard_map/ppermute | solution.py:228
  235.9 21.8 %first_product.7 = f32[2,128,896]{2,1,0:T(8,128)S(1)} custom-call(f32[64,7168]{1,0:T(8,128)S(1)} %collective-permute-done.6.near_ref, f32[64,7168]{1,0:T(8,128)S(1)} %collective-permute-done.12.far_ref, f32[896,7168]{1,0:T(8,128)} %own_ref.15, f32[896,7168]{1,0:T(8,128)} %collective-permute-done.2.sib_ref), custom_call_target="tpu_custom_call" | custom-call | flops 9865003008 | bytes 51380224 | tf_op jit(solution)/shard_map/first_product/pallas_call | solution.py:53
  257.9 23.7 %second_product.5 = (f32[64,7168]{1,0:T(8,128)S(1)}, f32[64,7168]{1,0:T(8,128)S(1)}) custom-call(f32[2,128,896]{2,1,0:T(8,128)S(1)} %add.261.change_ref, f32[896,7168]{1,0:T(8,128)} %own_ref.15, f32[896,7168]{1,0:T(8,128)} %collective-permute-done.2.sib_ref), custom_call_target="tpu_custom_call" | custom-call | flops 9865003008 | bytes 51380224 | tf_op jit(solution)/shard_map/second_product/pallas_call | solution.py:91
  290.2 23.7 %second_product.6 = (f32[64,7168]{1,0:T(8,128)S(1)}, f32[64,7168]{1,0:T(8,128)S(1)}) custom-call(f32[2,128,896]{2,1,0:T(8,128)S(1)} %add.263.change_ref, f32[896,7168]{1,0:T(8,128)} %own_ref.15, f32[896,7168]{1,0:T(8,128)} %collective-permute-done.2.sib_ref), custom_call_target="tpu_custom_call" | custom-call | flops 9865003008 | bytes 51380224 | tf_op jit(solution)/shard_map/second_product/pallas_call | solution.py:91
  313.9 14.5 %collective-permute-done.26 = f32[2,64,896]{2,1,0:T(8,128)S(1)} collective-permute-done((f32[2,64,896]{2,1,0:T(8,128)S(1)}, f32[2,64,896]{2,1,0:T(8,128)S(1)}, u32[]{:S(2)}, u32[]{:S(2)}) %collective-permute-start.26) | collective-permute-done | bytes 458784 | tf_op jit(solution)/shard_map/ppermute | solution.py:228
  331.3 4.1 collective-permute-start.30
  335.5 24.6 %second_product.7 = (f32[64,7168]{1,0:T(8,128)S(1)}, f32[64,7168]{1,0:T(8,128)}) custom-call(f32[2,128,896]{2,1,0:T(8,128)S(1)} %add.266.change_ref, f32[896,7168]{1,0:T(8,128)} %own_ref.15, f32[896,7168]{1,0:T(8,128)} %collective-permute-done.2.sib_ref), custom_call_target="tpu_custom_call" | custom-call | flops 9865003008 | bytes 51380224 | tf_op jit(solution)/shard_map/second_product/pallas_call | solution.py:91
  360.2 7.2 %collective-permute-done.29 = f32[64,7168]{1,0:T(8,128)S(1)} collective-permute-done((f32[64,7168]{1,0:T(8,128)S(1)}, f32[64,7168]{1,0:T(8,128)S(1)}, u32[]{:S(2)}, u32[]{:S(2)}) %collective-permute-start.29) | collective-permute-done | bytes 1835040 | tf_op jit(solution)/shard_map/ppermute | solution.py:204
  367.4 5.8 %collective-permute-done.30 = f32[64,7168]{1,0:T(8,128)S(1)} collective-permute-done((f32[64,7168]{1,0:T(8,128)}, f32[64,7168]{1,0:T(8,128)S(1)}, u32[]{:S(2)}, u32[]{:S(2)}) %collective-permute-start.30) | collective-permute-done | bytes 1835040 | tf_op jit(solution)/shard_map/ppermute | solution.py:203
  374.7 4.2 collective-permute-start.32
  379.0 32.6 %collective-permute-done.32 = f32[2,64,896]{2,1,0:T(8,128)} collective-permute-done((f32[2,64,896]{2,1,0:T(8,128)S(1)}, f32[2,64,896]{2,1,0:T(8,128)}, u32[]{:S(2)}, u32[]{:S(2)}) %collective-permute-start.32) | collective-permute-done | bytes 458784 | tf_op jit(solution)/shard_map/ppermute | solution.py:228
  417.0 4.5 %subtract_bitcast_fusion = (f32[7168,64]{0,1:T(8,128)}, f32[64,7168]{1,0:T(8,128)S(1)}) fusion(s32[7168,64]{0,1:T(8,128)S(1)} %copy-done.2, f32[7168,64]{0,1:T(8,128)S(1)} %copy-done.3, f32[64,7168]{1,0:T(8,128)S(1)} %fusion.17, f32[7168,64]{0,1:T(8,128)S(1)} %copy-done.4, f32[64,7168]{1,0:T(8,128)} %collective-permute-done.33, ...), kind=kLoop, calls=%fused_computation.12 | loop fusion | flops 6881280 | bytes 16515072 | tf_op jit(solution)/shard_map/transpose | solution.py:255
  (156 shorter events, 58.1 us)
Async XLA Ops:
  0.6 53.3 %collective-permute-start.2 = (f32[896,7168]{1,0:T(8,128)}, f32[896,7168]{1,0:T(8,128)}, u32[]{:S(2)}, u32[]{:S(2)}) collective-permute-start(f32[896,7168]{1,0:T(8,128)} %own_ref.15), channel_id=1, source_target_pairs={{0,2},{2,0},{4,6},{6,4},{8,10},{10,8},{12,14},{14,12},{16,18},{18,... | collective-permute-start | bytes 77070344 | tf_op jit(solution)/shard_map/ppermute | solution.py:149
  6.1 43.5 %collective-permute-start.3 = (f32[64,7168]{1,0:T(8,128)}, f32[64,7168]{1,0:T(8,128)}, u32[]{:S(2)}, u32[]{:S(2)}) collective-permute-start(f32[64,7168]{1,0:T(8,128)} %get-tuple-element.151), channel_id=1, source_target_pairs={{0,1},{1,0},{2,3},{3,2},{4,5},{5,4},{6,7},{7,6},{8,9},{9,8},{10,11... | collective-permute-start | bytes 5505032 | tf_op jit(solution)/shard_map/ppermute | solution.py:188
  8.6 42.2 %collective-permute-start.1 = (f32[64,7168]{1,0:T(8,128)S(1)}, f32[64,7168]{1,0:T(8,128)}, u32[]{:S(2)}, u32[]{:S(2)}) collective-permute-start(f32[64,7168]{1,0:T(8,128)S(1)} %get-tuple-element.152.near_ref), channel_id=1, source_target_pairs={{0,4},{2,6},{4,0},{6,2},{8,12},{10,14},{12,8},{14,10},{16,20},{18,... | collective-permute-start | bytes 5505032 | tf_op jit(solution)/shard_map/ppermute | solution.py:186
  10.1 43.8 %collective-permute-start = (f32[64,7168]{1,0:T(8,128)S(1)}, f32[64,7168]{1,0:T(8,128)}, u32[]{:S(2)}, u32[]{:S(2)}) collective-permute-start(f32[64,7168]{1,0:T(8,128)S(1)} %get-tuple-element.152.near_ref), channel_id=1, source_target_pairs={{0,8},{2,10},{4,12},{6,14},{8,16},{10,18},{12,20},{14,22},{16,24},... | collective-permute-start | bytes 5505032 | tf_op jit(solution)/shard_map/ppermute | solution.py:184
  53.9 41.3 %collective-permute-start.5 = (f32[64,7168]{1,0:T(8,128)}, f32[64,7168]{1,0:T(8,128)S(1)}, u32[]{:S(2)}, u32[]{:S(2)}) collective-permute-start(f32[64,7168]{1,0:T(8,128)} %collective-permute-done.near_ref), channel_id=1, source_target_pairs={{0,4},{2,6},{4,0},{6,2},{8,12},{10,14},{12,8},{14,10},{16,20},{18,... | collective-permute-start | bytes 5505032 | tf_op jit(solution)/shard_map/ppermute | solution.py:186
  54.4 45.0 %collective-permute-start.4 = (f32[64,7168]{1,0:T(8,128)}, f32[64,7168]{1,0:T(8,128)S(1)}, u32[]{:S(2)}, u32[]{:S(2)}) collective-permute-start(f32[64,7168]{1,0:T(8,128)} %collective-permute-done.near_ref), channel_id=1, source_target_pairs={{0,8},{2,10},{4,12},{6,14},{8,16},{10,18},{12,20},{14,22},{16,24},... | collective-permute-start | bytes 5505032 | tf_op jit(solution)/shard_map/ppermute | solution.py:184
  54.5 70.2 %collective-permute-start.9 = (f32[2,64,896]{2,1,0:T(8,128)S(1)}, f32[2,64,896]{2,1,0:T(8,128)}, u32[]{:S(2)}, u32[]{:S(2)}) collective-permute-start(f32[2,64,896]{2,1,0:T(8,128)S(1)} %fusion.11), channel_id=1, source_target_pairs={{0,8},{2,10},{4,12},{6,14},{9,17},{11,19},{13,21},{15,23},{17,25},... | collective-permute-start | bytes 1376264 | tf_op jit(solution)/shard_map/ppermute | solution.py:161
  59.2 65.5 %collective-permute-start.10 = (f32[2,64,896]{2,1,0:T(8,128)S(1)}, f32[2,64,896]{2,1,0:T(8,128)}, u32[]{:S(2)}, u32[]{:S(2)}) collective-permute-start(f32[2,64,896]{2,1,0:T(8,128)S(1)} %fusion.16), channel_id=1, source_target_pairs={{1,13},{3,15},{5,9},{7,11},{8,20},{10,22},{12,16},{14,18},{16,28},... | collective-permute-start | bytes 1376264 | tf_op jit(solution)/shard_map/ppermute | solution.py:161
  99.4 49.6 %collective-permute-start.7 = (f32[64,7168]{1,0:T(8,128)S(1)}, f32[64,7168]{1,0:T(8,128)S(1)}, u32[]{:S(2)}, u32[]{:S(2)}) collective-permute-start(f32[64,7168]{1,0:T(8,128)S(1)} %collective-permute-done.4.near_ref), channel_id=1, source_target_pairs={{0,4},{2,6},{4,0},{6,2},{8,12},{10,14},{12,8},{14,10},{16,20},{18,... | collective-permute-start | bytes 5505032 | tf_op jit(solution)/shard_map/ppermute | solution.py:186
  100.9 48.1 %collective-permute-start.6 = (f32[64,7168]{1,0:T(8,128)S(1)}, f32[64,7168]{1,0:T(8,128)S(1)}, u32[]{:S(2)}, u32[]{:S(2)}) collective-permute-start(f32[64,7168]{1,0:T(8,128)S(1)} %collective-permute-done.4.near_ref), channel_id=1, source_target_pairs={{0,8},{2,10},{4,12},{6,14},{8,16},{10,18},{12,20},{14,22},{16,24},... | collective-permute-start | bytes 5505032 | tf_op jit(solution)/shard_map/ppermute | solution.py:184
  129.0 46.1 %collective-permute-start.15 = (f32[2,64,896]{2,1,0:T(8,128)S(1)}, f32[2,64,896]{2,1,0:T(8,128)S(1)}, u32[]{:S(2)}, u32[]{:S(2)}) collective-permute-start(f32[2,64,896]{2,1,0:T(8,128)S(1)} %fusion.12), channel_id=1, source_target_pairs={{1,17},{3,19},{5,21},{7,23},{9,25},{11,27},{13,29},{15,31},{16,0},... | collective-permute-start | bytes 1376264 | tf_op jit(solution)/shard_map/ppermute | solution.py:161
  149.0 56.3 %collective-permute-start.13 = (f32[2,64,896]{2,1,0:T(8,128)S(1)}, f32[2,64,896]{2,1,0:T(8,128)S(1)}, u32[]{:S(2)}, u32[]{:S(2)}) collective-permute-start(f32[2,64,896]{2,1,0:T(8,128)S(1)} %fusion.13), channel_id=1, source_target_pairs={{1,25},{3,27},{5,29},{7,31},{8,0},{10,2},{12,4},{14,6},{16,8},{18,... | collective-permute-start | bytes 1376264 | tf_op jit(solution)/shard_map/ppermute | solution.py:161
  150.3 55.0 %collective-permute-start.14 = (f32[2,64,896]{2,1,0:T(8,128)S(1)}, f32[2,64,896]{2,1,0:T(8,128)S(1)}, u32[]{:S(2)}, u32[]{:S(2)}) collective-permute-start(f32[2,64,896]{2,1,0:T(8,128)S(1)} %fusion.15), channel_id=1, source_target_pairs={{0,28},{2,30},{4,24},{6,26},{9,5},{11,7},{13,1},{15,3},{17,13},{19... | collective-permute-start | bytes 1376264 | tf_op jit(solution)/shard_map/ppermute | solution.py:161
  151.7 53.6 %collective-permute-start.12 = (f32[64,7168]{1,0:T(8,128)S(1)}, f32[64,7168]{1,0:T(8,128)S(1)}, u32[]{:S(2)}, u32[]{:S(2)}) collective-permute-start(f32[64,7168]{1,0:T(8,128)S(1)} %collective-permute-done.6.near_ref), channel_id=1, source_target_pairs={{0,4},{2,6},{4,0},{6,2},{8,12},{10,14},{12,8},{14,10},{16,20},{18,... | collective-permute-start | bytes 5505032 | tf_op jit(solution)/shard_map/ppermute | solution.py:186
  206.3 75.2 %collective-permute-start.23 = (f32[2,64,896]{2,1,0:T(8,128)}, f32[2,64,896]{2,1,0:T(8,128)S(1)}, u32[]{:S(2)}, u32[]{:S(2)}) collective-permute-start(f32[2,64,896]{2,1,0:T(8,128)} %slice.51), channel_id=1, source_target_pairs={{13,0},{15,2},{9,4},{11,6},{20,9},{22,11},{16,13},{18,15},{28,17},... | collective-permute-start | bytes 1376264 | tf_op jit(solution)/shard_map/ppermute | solution.py:228
  207.8 73.8 %collective-permute-start.22 = (f32[2,64,896]{2,1,0:T(8,128)S(1)}, f32[2,64,896]{2,1,0:T(8,128)S(1)}, u32[]{:S(2)}, u32[]{:S(2)}) collective-permute-start(f32[2,64,896]{2,1,0:T(8,128)S(1)} %get-tuple-element.165), channel_id=1, source_target_pairs={{20,1},{22,3},{16,5},{18,7},{28,9},{30,11},{24,13},{26,15},{5,16},... | collective-permute-start | bytes 1376264 | tf_op jit(solution)/shard_map/ppermute | solution.py:228
  208.5 73.1 %collective-permute-start.21 = (f32[2,64,896]{2,1,0:T(8,128)S(1)}, f32[2,64,896]{2,1,0:T(8,128)}, u32[]{:S(2)}, u32[]{:S(2)}) collective-permute-start(f32[2,64,896]{2,1,0:T(8,128)S(1)} %get-tuple-element.166), channel_id=1, source_target_pairs={{17,1},{19,3},{21,5},{23,7},{25,9},{27,11},{29,13},{31,15},{0,16},... | collective-permute-start | bytes 1376264 | tf_op jit(solution)/shard_map/ppermute | solution.py:228
  234.9 46.8 %collective-permute-start.19 = (f32[64,7168]{1,0:T(8,128)S(1)}, f32[64,7168]{1,0:T(8,128)S(1)}, u32[]{:S(2)}, u32[]{:S(2)}) collective-permute-start(f32[64,7168]{1,0:T(8,128)S(1)} %get-tuple-element.99), channel_id=1, source_target_pairs={{0,4},{2,6},{4,0},{6,2},{8,12},{10,14},{12,8},{14,10},{16,20},{18,... | collective-permute-start | bytes 5505032 | tf_op jit(solution)/shard_map/ppermute | solution.py:204
  282.5 45.9 %collective-permute-start.24 = (f32[64,7168]{1,0:T(8,128)S(1)}, f32[64,7168]{1,0:T(8,128)S(1)}, u32[]{:S(2)}, u32[]{:S(2)}) collective-permute-start(f32[64,7168]{1,0:T(8,128)S(1)} %get-tuple-element.109), channel_id=1, source_target_pairs={{0,4},{2,6},{4,0},{6,2},{8,12},{10,14},{12,8},{14,10},{16,20},{18,... | collective-permute-start | bytes 5505032 | tf_op jit(solution)/shard_map/ppermute | solution.py:204
  284.9 43.5 %collective-permute-start.28 = (f32[64,7168]{1,0:T(8,128)}, f32[64,7168]{1,0:T(8,128)S(1)}, u32[]{:S(2)}, u32[]{:S(2)}) collective-permute-start(f32[64,7168]{1,0:T(8,128)} %add.265), channel_id=1, source_target_pairs={{0,8},{2,10},{4,12},{6,14},{8,16},{10,18},{12,20},{14,22},{16,24},... | collective-permute-start | bytes 5505032 | tf_op jit(solution)/shard_map/ppermute | solution.py:203
  288.0 40.4 %collective-permute-start.26 = (f32[2,64,896]{2,1,0:T(8,128)S(1)}, f32[2,64,896]{2,1,0:T(8,128)S(1)}, u32[]{:S(2)}, u32[]{:S(2)}) collective-permute-start(f32[2,64,896]{2,1,0:T(8,128)S(1)} %get-tuple-element.164), channel_id=1, source_target_pairs={{25,1},{27,3},{29,5},{31,7},{0,8},{2,10},{4,12},{6,14},{8,16},{10,... | collective-permute-start | bytes 1376264 | tf_op jit(solution)/shard_map/ppermute | solution.py:228
  329.2 38.2 %collective-permute-start.29 = (f32[64,7168]{1,0:T(8,128)S(1)}, f32[64,7168]{1,0:T(8,128)S(1)}, u32[]{:S(2)}, u32[]{:S(2)}) collective-permute-start(f32[64,7168]{1,0:T(8,128)S(1)} %get-tuple-element.120), channel_id=1, source_target_pairs={{0,4},{2,6},{4,0},{6,2},{8,12},{10,14},{12,8},{14,10},{16,20},{18,... | collective-permute-start | bytes 5505032 | tf_op jit(solution)/shard_map/ppermute | solution.py:204
  331.3 41.8 %collective-permute-start.30 = (f32[64,7168]{1,0:T(8,128)}, f32[64,7168]{1,0:T(8,128)S(1)}, u32[]{:S(2)}, u32[]{:S(2)}) collective-permute-start(f32[64,7168]{1,0:T(8,128)} %add_add_fusion.1), channel_id=1, source_target_pairs={{0,8},{2,10},{4,12},{6,14},{8,16},{10,18},{12,20},{14,22},{16,24},... | collective-permute-start | bytes 5505032 | tf_op jit(solution)/shard_map/ppermute | solution.py:203
  373.1 38.5 %collective-permute-start.31 = (f32[64,7168]{1,0:T(8,128)}, f32[64,7168]{1,0:T(8,128)}, u32[]{:S(2)}, u32[]{:S(2)}) collective-permute-start(f32[64,7168]{1,0:T(8,128)} %get-tuple-element.129), channel_id=1, source_target_pairs={{0,4},{2,6},{4,0},{6,2},{8,12},{10,14},{12,8},{14,10},{16,20},{18,... | collective-permute-start | bytes 5505032 | tf_op jit(solution)/shard_map/ppermute | solution.py:204
  (34 other events, 472.8 us)
